TPU v7x, 32 devices: a whole 2x2x4 slice. The times are simulated.
32 devices in a mesh: section: 2 (over x), batch: 4 (over z), tensor: 4 (over y, core).
Axes of the slice: x: 2, y: 2, z: 4, core: 2. Of those that a mesh axis runs over, the one named last changes fastest.
Arguments:
- inputs: bfloat16 [2, 4096, 768], P(None, ('batch', 'tensor')), may hold values from -6 to 6
- cotangent: bfloat16 [2, 4096, 768], P(None, ('batch', 'tensor')), may hold values from -6 to 6
- segments: int32 [2, 4, 1024], P(None, 'batch'), may hold values from 0 to 3, never falling along the last dimension, each value on 1 to 512 neighbouring positions
- ln1_gain: float32 [2, 768], P('section'), may hold values from 0.5 to 1.5
- ln1_bias: float32 [2, 768], P('section'), may hold values from -1.5 to 1.5
- w_query: bfloat16 [2, 768, 768], P('section', None, 'tensor'), may hold values from -0.21875 to 0.21875
- w_key: bfloat16 [2, 768, 768], P('section', None, 'tensor'), may hold values from -0.21875 to 0.21875
- w_value: bfloat16 [2, 768, 768], P('section', None, 'tensor'), may hold values from -0.21875 to 0.21875
- w_out: bfloat16 [2, 768, 768], P('section', 'tensor'), may hold values from -0.875 to 0.875
- ln2_gain: float32 [2, 768], P('section'), may hold values from 0.5 to 1.5
- ln2_bias: float32 [2, 768], P('section'), may hold values from -1.5 to 1.5
- w_up: bfloat16 [2, 768, 3072], P('section', None, 'tensor'), may hold values from -0.21875 to 0.21875
- b_up: float32 [2, 3072], P('section', 'tensor'), may hold values from -1.5 to 1.5
- w_down: bfloat16 [2, 3072, 768], P('section', 'tensor'), may hold values from -0.109375 to 0.109375
- b_down: float32 [2, 768], P('section'), may hold values from -1.5 to 1.5
Outputs:
- section_out: bfloat16 [2, 2, 4096, 768], P('section', None, ('batch', 'tensor'))
- section_grad: bfloat16 [2, 2, 4096, 768], P('section', None, ('batch', 'tensor'))
- ln1_gain_grad: float32 [2, 768], P('section')
- ln1_bias_grad: float32 [2, 768], P('section')
- w_query_grad: float32 [2, 768, 768], P('section', None, 'tensor')
- w_key_grad: float32 [2, 768, 768], P('section', None, 'tensor')
- w_value_grad: float32 [2, 768, 768], P('section', None, 'tensor')
- w_out_grad: float32 [2, 768, 768], P('section', 'tensor')
- ln2_gain_grad: float32 [2, 768], P('section')
- ln2_bias_grad: float32 [2, 768], P('section')
- w_up_grad: float32 [2, 768, 3072], P('section', None, 'tensor')
- b_up_grad: float32 [2, 3072], P('section', 'tensor')
- w_down_grad: float32 [2, 3072, 768], P('section', 'tensor')
- b_down_grad: float32 [2, 768], P('section')
Inputs may be any that keep to these rules, and one draw needn't show every extreme that they name: `segments`: along each sequence the segment numbers never fall.
All inputs are finite; a program needn't handle non-finite values.
Results may differ from a plain program's by a relative error of at most 0.025.
Values may be sent and summed in bfloat16 or wider, within the bound.
No kernel may reach another device: no remote copies, remote signals or barrier semaphores. Data moves between devices by JAX's collectives and lax.ppermute only.
A program may use at most 192 MiB of HBM per device.

v0:
```python
import jax
import jax.numpy as jnp
from jax import lax
from jax.sharding import PartitionSpec as P

HEAD_DIM = 64


epsilon = 1e-05


def passed_along(value, axis, steps):
    count = lax.axis_size(axis)
    first, last = (max(0, -steps), min(count, count - steps))
    return lax.ppermute(value, axis, [(source, source + steps) for source in range(first, last)])


def norm_rows(values, gain, bias):
    center = values - jnp.mean(values, axis=-1, keepdims=True)
    inverse = lax.rsqrt(jnp.mean(center * center, axis=-1, keepdims=True) + epsilon)
    normed = center * inverse
    return (normed * gain + bias, normed, inverse)


def norm_back(grad_norm, normed, inverse, gain):
    scaled = grad_norm * gain
    mean_one = jnp.mean(scaled, axis=-1, keepdims=True)
    mean_two = jnp.mean(scaled * normed, axis=-1, keepdims=True)
    grad_values = inverse * (scaled - mean_one - normed * mean_two)
    return (grad_values, jnp.sum(grad_norm * normed, axis=0), jnp.sum(grad_norm, axis=0))


def project(rows_in, weight):
    return jnp.dot(rows_in, weight, preferred_element_type=jnp.float32)


def contract_rows(left, right):
    return lax.dot_general(
        left, right, (((0,), (0,)), ((), ())), preferred_element_type=jnp.float32
    )


def times_transposed(left, right):
    return lax.dot_general(
        left, right, (((1,), (1,)), ((), ())), preferred_element_type=jnp.float32
    )


def gelu_tanh(pre_values):
    return jax.nn.gelu(pre_values, approximate=True)


def attention_rows(layer_in, gain, bias):
    normed_out, _, _ = norm_rows(layer_in, gain, bias)
    return lax.all_gather(normed_out.astype(jnp.bfloat16), "tensor", axis=0, tiled=True)


def feed_rows(mid_state, gain, bias):
    normed_out, _, _ = norm_rows(mid_state, gain, bias)
    return lax.all_gather(normed_out.astype(jnp.bfloat16), "tensor", axis=0, tiled=True)


def feed_hidden(normed_mid, w_up, b_up):
    pre_act = project(normed_mid, w_up) + b_up
    return (pre_act, gelu_tanh(pre_act).astype(jnp.bfloat16))


def block_mask(segment, offset, block_rows, key_end):
    query_pos = offset + jnp.arange(block_rows)
    key_pos = jnp.arange(key_end)
    query_seg = segment[offset : offset + block_rows]
    return (key_pos[None, :] <= query_pos[:, None]) & (
        segment[None, :key_end] == query_seg[:, None]
    )


def attend(normed_in, w_query, w_key, w_value, segment):
    length = normed_in.shape[0]
    head_count = w_query.shape[1] // HEAD_DIM
    scaling = HEAD_DIM ** (-0.5)
    head_shape = (length, head_count, HEAD_DIM)
    queries = project(normed_in, w_query).astype(jnp.bfloat16).reshape(head_shape)
    key_rows = project(normed_in, w_key).astype(jnp.bfloat16).reshape(head_shape)
    values = project(normed_in, w_value).astype(jnp.bfloat16).reshape(head_shape)
    block_rows = min(512, length)
    pieces = []
    row_sums = []
    for offset in range(0, length, block_rows):
        key_end = offset + block_rows
        scores = (
            jnp.einsum(
                "qhd,khd->hqk",
                queries[offset:key_end],
                key_rows[:key_end],
                preferred_element_type=jnp.float32,
            )
            * scaling
        )
        scores = jnp.where(block_mask(segment, offset, block_rows, key_end)[None], scores, -1e30)
        highest = jnp.max(scores, axis=-1, keepdims=True)
        exp_scores = jnp.exp(scores - highest)
        totals = jnp.sum(exp_scores, axis=-1, keepdims=True)
        probabilities = (exp_scores / totals).astype(jnp.bfloat16)
        pieces.append(
            jnp.einsum(
                "hqk,khd->qhd", probabilities, values[:key_end], preferred_element_type=jnp.float32
            ).astype(jnp.bfloat16)
        )
        row_sums.append((highest + jnp.log(totals))[..., 0])
    mixed_heads = jnp.concatenate(pieces, axis=0).reshape(length, head_count * HEAD_DIM)
    log_sums = jnp.concatenate(row_sums, axis=1)
    return (queries, key_rows, values, mixed_heads, log_sums)


def attend_back(queries, key_rows, values, log_sums, grad_mixed, segment):
    length, head_count = (queries.shape[0], queries.shape[1])
    scaling = HEAD_DIM ** (-0.5)
    grad_heads = grad_mixed.reshape(length, head_count, HEAD_DIM)
    grad_keys = jnp.zeros((length, head_count, HEAD_DIM), jnp.float32)
    grad_values = jnp.zeros((length, head_count, HEAD_DIM), jnp.float32)
    query_parts = []
    block_rows = min(512, length)
    for offset in range(0, length, block_rows):
        key_end = offset + block_rows
        query_block = queries[offset:key_end]
        grad_block = grad_heads[offset:key_end]
        key_block = key_rows[:key_end]
        scores = (
            jnp.einsum("qhd,khd->hqk", query_block, key_block, preferred_element_type=jnp.float32)
            * scaling
        )
        scores = jnp.where(block_mask(segment, offset, block_rows, key_end)[None], scores, -1e30)
        probabilities = jnp.exp(scores - log_sums[:, offset:key_end, None])
        grad_values = grad_values.at[:key_end].add(
            jnp.einsum(
                "hqk,qhd->khd",
                probabilities.astype(jnp.bfloat16),
                grad_block,
                preferred_element_type=jnp.float32,
            )
        )
        grad_probs = jnp.einsum(
            "qhd,khd->hqk", grad_block, values[:key_end], preferred_element_type=jnp.float32
        )
        inner_sum = jnp.sum(probabilities * grad_probs, axis=-1, keepdims=True)
        grad_scores = (probabilities * (grad_probs - inner_sum)).astype(jnp.bfloat16)
        query_parts.append(
            jnp.einsum("hqk,khd->qhd", grad_scores, key_block, preferred_element_type=jnp.float32)
            * scaling
        )
        grad_keys = grad_keys.at[:key_end].add(
            jnp.einsum("hqk,qhd->khd", grad_scores, query_block, preferred_element_type=jnp.float32)
            * scaling
        )
    flat_shape = (length, head_count * HEAD_DIM)
    grad_queries = jnp.concatenate(query_parts, axis=0).reshape(flat_shape).astype(jnp.bfloat16)
    return (
        grad_queries,
        grad_keys.reshape(flat_shape).astype(jnp.bfloat16),
        grad_values.reshape(flat_shape).astype(jnp.bfloat16),
    )


def layer_forward(layer_in, segment, weights):
    (
        gain_one,
        bias_one,
        w_query,
        w_key,
        w_value,
        w_out,
        gain_two,
        bias_two,
        w_up,
        b_up,
        w_down,
        b_down,
    ) = weights
    normed_in = attention_rows(layer_in, gain_one, bias_one)
    queries, key_rows, values, mixed_heads, log_sums = attend(
        normed_in, w_query, w_key, w_value, segment
    )
    mid_state = layer_in + lax.psum_scatter(
        project(mixed_heads, w_out).astype(jnp.bfloat16), "tensor", scatter_dimension=0, tiled=True
    ).astype(jnp.float32)
    normed_mid = feed_rows(mid_state, gain_two, bias_two)
    pre_act, activated = feed_hidden(normed_mid, w_up, b_up)
    feed_out = lax.psum_scatter(
        project(activated, w_down).astype(jnp.bfloat16), "tensor", scatter_dimension=0, tiled=True
    ).astype(jnp.float32)
    result = mid_state + feed_out + b_down
    stored = (
        layer_in,
        mid_state,
        normed_in,
        queries,
        key_rows,
        values,
        mixed_heads,
        log_sums,
        normed_mid,
        pre_act,
        activated,
    )
    return (result, stored)


def layer_backward(grad_out, stored, segment, weights):
    (
        gain_one,
        bias_one,
        w_query,
        w_key,
        w_value,
        w_out,
        gain_two,
        bias_two,
        w_up,
        b_up,
        w_down,
        b_down,
    ) = weights
    (
        layer_in,
        mid_state,
        normed_in,
        queries,
        key_rows,
        values,
        mixed_heads,
        log_sums,
        normed_mid,
        pre_act,
        activated,
    ) = stored
    grad_rows = lax.all_gather(grad_out.astype(jnp.bfloat16), "tensor", axis=0, tiled=True)
    grad_w_down = contract_rows(activated, grad_rows)
    grad_act = times_transposed(grad_rows, w_down)
    _, gelu_back = jax.vjp(gelu_tanh, pre_act)
    grad_pre = gelu_back(grad_act)[0].astype(jnp.bfloat16)
    grad_w_up = contract_rows(normed_mid, grad_pre)
    grad_b_up = jnp.sum(grad_pre.astype(jnp.float32), axis=0)
    grad_normed_mid = lax.psum_scatter(
        times_transposed(grad_pre, w_up).astype(jnp.bfloat16),
        "tensor",
        scatter_dimension=0,
        tiled=True,
    ).astype(jnp.float32)
    _, normed_two, inverse_two = norm_rows(mid_state, gain_two, bias_two)
    grad_mid_norm, grad_gain_two, grad_bias_two = norm_back(
        grad_normed_mid, normed_two, inverse_two, gain_two
    )
    grad_mid = grad_out + grad_mid_norm
    grad_attn = lax.all_gather(grad_mid.astype(jnp.bfloat16), "tensor", axis=0, tiled=True)
    grad_w_out = contract_rows(mixed_heads, grad_attn)
    grad_mixed = times_transposed(grad_attn, w_out).astype(jnp.bfloat16)
    grad_queries, grad_keys, grad_values = attend_back(
        queries, key_rows, values, log_sums, grad_mixed, segment
    )
    grad_w_query = contract_rows(normed_in, grad_queries)
    grad_w_key = contract_rows(normed_in, grad_keys)
    grad_w_value = contract_rows(normed_in, grad_values)
    partial_in = (
        times_transposed(grad_queries, w_query)
        + times_transposed(grad_keys, w_key)
        + times_transposed(grad_values, w_value)
    )
    grad_normed_in = lax.psum_scatter(
        partial_in.astype(jnp.bfloat16), "tensor", scatter_dimension=0, tiled=True
    ).astype(jnp.float32)
    _, normed_one, inverse_one = norm_rows(layer_in, gain_one, bias_one)
    grad_in_norm, grad_gain_one, grad_bias_one = norm_back(
        grad_normed_in, normed_one, inverse_one, gain_one
    )
    grad_in = grad_mid + grad_in_norm
    grad_b_down = jnp.sum(grad_out, axis=0)
    return (
        grad_in,
        (
            grad_gain_one,
            grad_bias_one,
            grad_w_query,
            grad_w_key,
            grad_w_value,
            grad_w_out,
            grad_gain_two,
            grad_bias_two,
            grad_w_up,
            grad_b_up,
            grad_w_down,
            grad_b_down,
        ),
    )


def body(
    inputs,
    cotangent,
    segments,
    ln1_gain,
    ln1_bias,
    w_query,
    w_key,
    w_value,
    w_out,
    ln2_gain,
    ln2_bias,
    w_up,
    b_up,
    w_down,
    b_down,
):
    weights = tuple(
        (
            array[0]
            for array in (
                ln1_gain,
                ln1_bias,
                w_query,
                w_key,
                w_value,
                w_out,
                ln2_gain,
                ln2_bias,
                w_up,
                b_up,
                w_down,
                b_down,
            )
        )
    )
    micro_count = inputs.shape[0]
    section_index = lax.axis_index("section")
    received = jnp.zeros(inputs.shape[1:], jnp.bfloat16)
    forward_out = jnp.zeros_like(inputs)
    stored_list = []
    for period in range(micro_count + 1):
        micro_index = period - section_index
        clipped = jnp.clip(micro_index, 0, micro_count - 1)
        is_valid = (micro_index >= 0) & (micro_index < micro_count)
        own_rows = lax.dynamic_index_in_dim(inputs, clipped, 0, keepdims=False)
        segment = lax.dynamic_index_in_dim(segments, clipped, 0, keepdims=False)[0]
        layer_in = jnp.where(section_index == 0, own_rows, received).astype(jnp.float32)
        result, stored = layer_forward(layer_in, segment, weights)
        rounded = result.astype(jnp.bfloat16)
        forward_out = jnp.where(
            is_valid, lax.dynamic_update_index_in_dim(forward_out, rounded, clipped, 0), forward_out
        )
        stored_list.append(stored)
        if period < micro_count:
            received = passed_along(rounded, "section", 1)
    stored_all = jax.tree.map(lambda *items: jnp.stack(items), *stored_list)
    grad_totals = jax.tree.map(lambda array: jnp.zeros(array.shape, jnp.float32), weights)
    back_received = jnp.zeros(inputs.shape[1:], jnp.bfloat16)
    backward_out = jnp.zeros_like(inputs)
    for period in range(micro_count + 1):
        micro_index = period - 1 + section_index
        clipped = jnp.clip(micro_index, 0, micro_count - 1)
        is_valid = (micro_index >= 0) & (micro_index < micro_count)
        slot_index = jnp.clip(period - 1 + 2 * section_index, 0, micro_count)
        stored = jax.tree.map(
            lambda array: lax.dynamic_index_in_dim(array, slot_index, 0, keepdims=False), stored_all
        )
        segment = lax.dynamic_index_in_dim(segments, clipped, 0, keepdims=False)[0]
        own_grad = lax.dynamic_index_in_dim(cotangent, clipped, 0, keepdims=False)
        grad_out = jnp.where(section_index == 1, own_grad, back_received).astype(jnp.float32)
        grad_out = jnp.where(is_valid, grad_out, jnp.zeros_like(grad_out))
        grad_in, grads_now = layer_backward(grad_out, stored, segment, weights)
        rounded = grad_in.astype(jnp.bfloat16)
        backward_out = jnp.where(
            is_valid,
            lax.dynamic_update_index_in_dim(backward_out, rounded, clipped, 0),
            backward_out,
        )
        grad_totals = jax.tree.map(jnp.add, grad_totals, grads_now)
        if period < micro_count:
            back_received = passed_along(rounded, "section", -1)
    summed_large = (
        lax.psum(grad_totals[2].astype(jnp.bfloat16), "batch").astype(jnp.float32),
        lax.psum(grad_totals[3].astype(jnp.bfloat16), "batch").astype(jnp.float32),
        lax.psum(grad_totals[4].astype(jnp.bfloat16), "batch").astype(jnp.float32),
        lax.psum(grad_totals[5].astype(jnp.bfloat16), "batch").astype(jnp.float32),
        lax.psum(grad_totals[8].astype(jnp.bfloat16), "batch").astype(jnp.float32),
        lax.psum(grad_totals[9].astype(jnp.bfloat16), "batch").astype(jnp.float32),
        lax.psum(grad_totals[10].astype(jnp.bfloat16), "batch").astype(jnp.float32),
    )
    summed_small = lax.psum(
        (grad_totals[0], grad_totals[1], grad_totals[6], grad_totals[7], grad_totals[11]),
        ("batch", "tensor"),
    )
    return (
        forward_out[None],
        backward_out[None],
        summed_small[0][None],
        summed_small[1][None],
        summed_large[0][None],
        summed_large[1][None],
        summed_large[2][None],
        summed_large[3][None],
        summed_small[2][None],
        summed_small[3][None],
        summed_large[4][None],
        summed_large[5][None],
        summed_large[6][None],
        summed_small[4][None],
    )


def solution(mesh):
    placed = (
        P(None, ("batch", "tensor"), None),
        P(None, ("batch", "tensor"), None),
        P(None, "batch", None),
        P("section", None),
        P("section", None),
        P("section", None, "tensor"),
        P("section", None, "tensor"),
        P("section", None, "tensor"),
        P("section", "tensor", None),
        P("section", None),
        P("section", None),
        P("section", None, "tensor"),
        P("section", "tensor"),
        P("section", "tensor", None),
        P("section", None),
    )
    return jax.shard_map(
        body,
        mesh=mesh,
        in_specs=placed,
        out_specs=(
            P("section", None, ("batch", "tensor"), None),
            P("section", None, ("batch", "tensor"), None),
            P("section", None),
            P("section", None),
            P("section", None, "tensor"),
            P("section", None, "tensor"),
            P("section", None, "tensor"),
            P("section", "tensor", None),
            P("section", None),
            P("section", None),
            P("section", None, "tensor"),
            P("section", "tensor"),
            P("section", "tensor", None),
            P("section", None),
        ),
        check_vma=False,
    )
```

profile of v0, /device:TPU:0, one launch (start us, length us, event | category | flops | bytes accessed | tf_op | source)
XLA Modules:
  0.0 1001.2 jit_solution(13226007894838023166)
XLA Ops:
  19.2 16.5 %all-gather.13.cloned.1.call-done = bf16[1024,768]{1,0:T(8,128)(2,1)} async-done(((bf16[256,768]{1,0:T(8,128)(2,1)}), bf16[1024,768]{1,0:T(8,128)(2,1)}) %all-gather.13.cloned.1.call-update) | async-done | bytes 1572880 | tf_op jit(solution)/shard_map/all_gather | solution.py:55
  51.6 28.2 %reduce-scatter.13.cloned.1.call-done = bf16[256,768]{1,0:T(8,128)(2,1)} async-done(((bf16[1024,768]{1,0:T(8,128)(2,1)}), bf16[256,768]{1,0:T(8,128)(2,1)}) %reduce-scatter.13.cloned.1.call-update) | async-done | bytes 393232 | tf_op jit(solution)/shard_map/reduce_scatter | solution.py:183
  85.3 19.6 %all-gather.15.cloned.1.call-done = bf16[1024,768]{1,0:T(8,128)(2,1)} async-done(((bf16[256,768]{1,0:T(8,128)(2,1)}), bf16[1024,768]{1,0:T(8,128)(2,1)}) %all-gather.15.cloned.1.call-update) | async-done | bytes 1572880 | tf_op jit(solution)/shard_map/all_gather | solution.py:60
  112.7 28.2 %reduce-scatter.15.cloned.1.call-done = bf16[256,768]{1,0:T(8,128)(2,1)} async-done(((bf16[1024,768]{1,0:T(8,128)(2,1)}), bf16[256,768]{1,0:T(8,128)(2,1)}) %reduce-scatter.15.cloned.1.call-update) | async-done | bytes 393232 | tf_op jit(solution)/shard_map/reduce_scatter | solution.py:188
  158.3 19.9 %all-gather.17.cloned.1.call-done = bf16[1024,768]{1,0:T(8,128)(2,1)} async-done(((bf16[256,768]{1,0:T(8,128)(2,1)}), bf16[1024,768]{1,0:T(8,128)(2,1)}) %all-gather.17.cloned.1.call-update) | async-done | bytes 1572880 | tf_op jit(solution)/shard_map/all_gather | solution.py:55
  194.3 28.0 %reduce-scatter.17.cloned.1.call-done = bf16[256,768]{1,0:T(8,128)(2,1)} async-done(((bf16[1024,768]{1,0:T(8,128)(2,1)}), bf16[256,768]{1,0:T(8,128)(2,1)}) %reduce-scatter.17.cloned.1.call-update) | async-done | bytes 393232 | tf_op jit(solution)/shard_map/reduce_scatter | solution.py:183
  227.6 19.8 %all-gather.19.cloned.1.call-done = bf16[1024,768]{1,0:T(8,128)(2,1)} async-done(((bf16[256,768]{1,0:T(8,128)(2,1)}), bf16[1024,768]{1,0:T(8,128)(2,1)}) %all-gather.19.cloned.1.call-update) | async-done | bytes 1572880 | tf_op jit(solution)/shard_map/all_gather | solution.py:60
  256.3 28.3 %reduce-scatter.19.cloned.1.call-done = bf16[256,768]{1,0:T(8,128)(2,1)} async-done(((bf16[1024,768]{1,0:T(8,128)(2,1)}), bf16[256,768]{1,0:T(8,128)(2,1)}) %reduce-scatter.19.cloned.1.call-update) | async-done | bytes 393232 | tf_op jit(solution)/shard_map/reduce_scatter | solution.py:188
  301.2 19.9 %all-gather.21.cloned.1.call-done = bf16[1024,768]{1,0:T(8,128)(2,1)} async-done(((bf16[256,768]{1,0:T(8,128)(2,1)}), bf16[1024,768]{1,0:T(8,128)(2,1)}) %all-gather.21.cloned.1.call-update) | async-done | bytes 1572880 | tf_op jit(solution)/shard_map/all_gather | solution.py:55
  337.0 28.3 %reduce-scatter.21.cloned.1.call-done = bf16[256,768]{1,0:T(8,128)(2,1)} async-done(((bf16[1024,768]{1,0:T(8,128)(2,1)}), bf16[256,768]{1,0:T(8,128)(2,1)}) %reduce-scatter.21.cloned.1.call-update) | async-done | bytes 393232 | tf_op jit(solution)/shard_map/reduce_scatter | solution.py:183
  372.5 17.8 %all-gather.23.cloned.1.call-done = bf16[1024,768]{1,0:T(8,128)(2,1)} async-done(((bf16[256,768]{1,0:T(8,128)(2,1)}), bf16[1024,768]{1,0:T(8,128)(2,1)}) %all-gather.23.cloned.1.call-update) | async-done | bytes 1572880 | tf_op jit(solution)/shard_map/all_gather | solution.py:60
  426.4 23.8 %reduce-scatter.25.cloned.1.call-done = bf16[256,768]{1,0:T(8,128)(2,1)} async-done(((bf16[1024,768]{1,0:T(8,128)(2,1)}), bf16[256,768]{1,0:T(8,128)(2,1)}) %reduce-scatter.25.cloned.1.call-update) | async-done | bytes 393232 | tf_op jit(solution)/shard_map/reduce_scatter | solution.py:243
  497.6 25.0 %reduce-scatter.27.cloned.1.call-done = bf16[256,768]{1,0:T(8,128)(2,1)} async-done(((bf16[1024,768]{1,0:T(8,128)(2,1)}), bf16[256,768]{1,0:T(8,128)(2,1)}) %reduce-scatter.27.cloned.1.call-update) | async-done | bytes 393232 | tf_op jit(solution)/shard_map/reduce_scatter | solution.py:268
  529.3 11.8 %collective-permute-done.2 = bf16[256,768]{1,0:T(8,128)(2,1)} collective-permute-done((bf16[256,768]{1,0:T(8,128)(2,1)}, bf16[256,768]{1,0:T(8,128)(2,1)}, u32[]{:S(2)}, u32[]{:S(2)}) %collective-permute-start.2) | collective-permute-done | bytes 393248 | tf_op jit(solution)/shard_map/ppermute | solution.py:15
  544.5 18.9 %all-gather.29.cloned.1.call-done = bf16[1024,768]{1,0:T(8,128)(2,1)} async-done(((bf16[256,768]{1,0:T(8,128)(2,1)}), bf16[1024,768]{1,0:T(8,128)(2,1)}) %all-gather.29.cloned.1.call-update) | async-done | bytes 1572880 | tf_op jit(solution)/shard_map/all_gather | solution.py:236
  575.9 25.8 %reduce-scatter.29.cloned.1.call-done = bf16[256,768]{1,0:T(8,128)(2,1)} async-done(((bf16[1024,768]{1,0:T(8,128)(2,1)}), bf16[256,768]{1,0:T(8,128)(2,1)}) %reduce-scatter.29.cloned.1.call-update) | async-done | bytes 393232 | tf_op jit(solution)/shard_map/reduce_scatter | solution.py:243
  614.5 12.4 %all-gather.31.cloned.1.call-done = bf16[1024,768]{1,0:T(8,128)(2,1)} async-done(((bf16[256,768]{1,0:T(8,128)(2,1)}), bf16[1024,768]{1,0:T(8,128)(2,1)}) %all-gather.31.cloned.1.call-update) | async-done | bytes 1572880 | tf_op jit(solution)/shard_map/all_gather | solution.py:254
  650.4 26.3 %reduce-scatter.31.cloned.1.call-done = bf16[256,768]{1,0:T(8,128)(2,1)} async-done(((bf16[1024,768]{1,0:T(8,128)(2,1)}), bf16[256,768]{1,0:T(8,128)(2,1)}) %reduce-scatter.31.cloned.1.call-update) | async-done | bytes 393232 | tf_op jit(solution)/shard_map/reduce_scatter | solution.py:268
  682.7 11.8 %collective-permute-done.3 = bf16[256,768]{1,0:T(8,128)(2,1)} collective-permute-done((bf16[256,768]{1,0:T(8,128)(2,1)}, bf16[256,768]{1,0:T(8,128)(2,1)}, u32[]{:S(2)}, u32[]{:S(2)}) %collective-permute-start.3) | collective-permute-done | bytes 393248 | tf_op jit(solution)/shard_map/ppermute | solution.py:15
  698.0 18.9 %all-gather.33.cloned.1.call-done = bf16[1024,768]{1,0:T(8,128)(2,1)} async-done(((bf16[256,768]{1,0:T(8,128)(2,1)}), bf16[1024,768]{1,0:T(8,128)(2,1)}) %all-gather.33.cloned.1.call-update) | async-done | bytes 1572880 | tf_op jit(solution)/shard_map/all_gather | solution.py:236
  728.1 27.0 %reduce-scatter.33.cloned.1.call-done = bf16[256,768]{1,0:T(8,128)(2,1)} async-done(((bf16[1024,768]{1,0:T(8,128)(2,1)}), bf16[256,768]{1,0:T(8,128)(2,1)}) %reduce-scatter.33.cloned.1.call-update) | async-done | bytes 393232 | tf_op jit(solution)/shard_map/reduce_scatter | solution.py:243
  846.4 11.9 %psum.93 = bf16[1,768]{1,0:T(2,128)(2,1)S(1)} all-reduce(bf16[1,768]{1,0:T(2,128)(2,1)S(1)} %broadcast_in_dim.316), channel_id=1, replica_groups=mesh['section'=2,'batch'=4,'tensor'=4] {'batch'}, use_global_device_ids=true, to_apply=%region_90.91 | all-reduce | flops 768 | bytes 3072 | tf_op jit(solution)/shard_map/psum | solution.py:384
  864.3 61.3 %all-reduce.6 = (f32[1,768]{1,0:T(1,128)}, f32[1,768]{1,0:T(1,128)}, f32[1,768]{1,0:T(1,128)}, f32[1,768]{1,0:T(1,128)}, f32[1,768]{1,0:T(1,128)}) all-reduce(f32[1,768]{1,0:T(1,128)S(1)} %broadcast_in_dim.302, f32[1,768]{1,0:T(1,128)} %broadcast_in_dim.303, ...), channel_id=1, replica_groups=mesh['section'=2,'batch'=4,'tensor'=4] {'batch','tensor'}, use_global_device_ids=true, to_apply=%region_69.70 | all-reduce | flops 3840 | bytes 30720 | tf_op jit(solution)/shard_map/psum | solution.py:387
  929.4 54.4 %all-reduce.10.cloned.1.call-done = (bf16[1,768,192]{1,2,0:T(8,128)(2,1)}, bf16[1,768,192]{1,2,0:T(8,128)(2,1)}, bf16[1,768,192]{1,2,0:T(8,128)(2,1)}, bf16[1,19...) async-done(((bf16[1,768,192]{1,2,0:T(8,128)(2,1)}, bf16[1,768,192]{1,2,0:T(8,128)(2,1)}, bf16[1,768,192]{1,2,0:T(8,128)(2,1)}, ...) | async-done | bytes 3538960 | tf_op jit(solution)/shard_map/psum | solution.py:379
  (682 shorter events, 400.9 us)
Async XLA Ops:
  13.2 66.6 %reduce-scatter.13.cloned.1.call-start = ((), (), s32[]{:S(2)}) async-start(), calls=%async_computation.13 | async-start | bytes 1966080 | tf_op jit(solution)/shard_map/reduce_scatter | solution.py:183
  51.4 53.4 %all-gather.15.cloned.1.call-start = ((), (), s32[]{:S(2)}) async-start(), calls=%async_computation.14 | async-start | bytes 1966080 | tf_op jit(solution)/shard_map/all_gather | solution.py:60
  85.1 55.9 %reduce-scatter.15.cloned.1.call-start = ((), (), s32[]{:S(2)}) async-start(), calls=%async_computation.15 | async-start | bytes 1966080 | tf_op jit(solution)/shard_map/reduce_scatter | solution.py:188
  112.6 65.5 %all-gather.17.cloned.1.call-start = ((), (), s32[]{:S(2)}) async-start(), calls=%async_computation.16 | async-start | bytes 1966080 | tf_op jit(solution)/shard_map/all_gather | solution.py:55
  157.3 65.1 %reduce-scatter.17.cloned.1.call-start = ((), (), s32[]{:S(2)}) async-start(), calls=%async_computation.17 | async-start | bytes 1966080 | tf_op jit(solution)/shard_map/reduce_scatter | solution.py:183
  194.1 53.4 %all-gather.19.cloned.1.call-start = ((), (), s32[]{:S(2)}) async-start(), calls=%async_computation.18 | async-start | bytes 1966080 | tf_op jit(solution)/shard_map/all_gather | solution.py:60
  227.6 57.0 %reduce-scatter.19.cloned.1.call-start = ((), (), s32[]{:S(2)}) async-start(), calls=%async_computation.19 | async-start | bytes 1966080 | tf_op jit(solution)/shard_map/reduce_scatter | solution.py:188
  256.2 64.8 %all-gather.21.cloned.1.call-start = ((), (), s32[]{:S(2)}) async-start(), calls=%async_computation.20 | async-start | bytes 1966080 | tf_op jit(solution)/shard_map/all_gather | solution.py:55
  300.2 65.0 %reduce-scatter.21.cloned.1.call-start = ((), (), s32[]{:S(2)}) async-start(), calls=%async_computation.21 | async-start | bytes 1966080 | tf_op jit(solution)/shard_map/reduce_scatter | solution.py:183
  336.9 53.3 %all-gather.23.cloned.1.call-start = ((), (), s32[]{:S(2)}) async-start(), calls=%async_computation.22 | async-start | bytes 1966080 | tf_op jit(solution)/shard_map/all_gather | solution.py:60
  370.4 41.6 %all-gather.25.cloned.1.call-start = ((), (), s32[]{:S(2)}) async-start(), calls=%async_computation.24 | async-start | bytes 1966080 | tf_op jit(solution)/shard_map/all_gather | solution.py:236
  372.0 78.2 %reduce-scatter.25.cloned.1.call-start = ((), (), s32[]{:S(2)}) async-start(), calls=%async_computation.25 | async-start | bytes 1966080 | tf_op jit(solution)/shard_map/reduce_scatter | solution.py:243
  421.8 52.8 %all-gather.27.cloned.1.call-start = ((), (), s32[]{:S(2)}) async-start(), calls=%async_computation.26 | async-start | bytes 1966080 | tf_op jit(solution)/shard_map/all_gather | solution.py:254
  454.8 67.8 %reduce-scatter.27.cloned.1.call-start = ((), (), s32[]{:S(2)}) async-start(), calls=%async_computation.27 | async-start | bytes 1966080 | tf_op jit(solution)/shard_map/reduce_scatter | solution.py:268
  494.3 69.1 %all-gather.29.cloned.1.call-start = ((), (), s32[]{:S(2)}) async-start(), calls=%async_computation.28 | async-start | bytes 1966080 | tf_op jit(solution)/shard_map/all_gather | solution.py:236
  544.5 57.2 %reduce-scatter.29.cloned.1.call-start = ((), (), s32[]{:S(2)}) async-start(), calls=%async_computation.29 | async-start | bytes 1966080 | tf_op jit(solution)/shard_map/reduce_scatter | solution.py:243
  573.4 53.5 %all-gather.31.cloned.1.call-start = ((), (), s32[]{:S(2)}) async-start(), calls=%async_computation.30 | async-start | bytes 1966080 | tf_op jit(solution)/shard_map/all_gather | solution.py:254
  607.1 69.7 %reduce-scatter.31.cloned.1.call-start = ((), (), s32[]{:S(2)}) async-start(), calls=%async_computation.31 | async-start | bytes 1966080 | tf_op jit(solution)/shard_map/reduce_scatter | solution.py:268
  648.4 68.5 %all-gather.33.cloned.1.call-start = ((), (), s32[]{:S(2)}) async-start(), calls=%async_computation.32 | async-start | bytes 1966080 | tf_op jit(solution)/shard_map/all_gather | solution.py:236
  697.9 57.2 %reduce-scatter.33.cloned.1.call-start = ((), (), s32[]{:S(2)}) async-start(), calls=%async_computation.33 | async-start | bytes 1966080 | tf_op jit(solution)/shard_map/reduce_scatter | solution.py:243
  726.8 67.1 %all-gather.35.cloned.1.call-start = ((), (), s32[]{:S(2)}) async-start(), calls=%async_computation.34 | async-start | bytes 1966080 | tf_op jit(solution)/shard_map/all_gather | solution.py:254
  760.1 80.6 %reduce-scatter.23.cloned.1.call-start = ((), (), s32[]{:S(2)}) async-start(), calls=%async_computation.23 | async-start | bytes 1966080 | tf_op jit(solution)/shard_map/reduce_scatter | solution.py:188
  776.1 84.3 %reduce-scatter.35.cloned.1.call-start = ((), (), s32[]{:S(2)}) async-start(), calls=%async_computation.35 | async-start | bytes 1966080 | tf_op jit(solution)/shard_map/reduce_scatter | solution.py:268
  815.5 168.4 %all-reduce.10.cloned.1.call-start = ((), (), s32[]{:S(2)}) async-start(), calls=%async_computation.36 | async-start | bytes 7077888 | tf_op jit(solution)/shard_map/psum | solution.py:379
  (182 other events, 1935.0 us)
Sparse Core Ops, SparseCore 0:
  13.3 22.3 all-gather.12
  51.6 28.1 reduce-scatter.12
  85.2 19.6 all-gather.14
  112.8 28.1 reduce-scatter.14
  157.4 20.6 all-gather.16
  194.2 28.1 reduce-scatter.16
  227.7 19.6 all-gather.18
  256.4 28.1 reduce-scatter.18
  300.3 20.6 all-gather.20
  337.0 28.1 reduce-scatter.20
  370.6 19.6 all-gather.22
  392.3 19.6 all-gather.24
  422.0 28.1 reduce-scatter.24
  455.0 19.6 all-gather.26
  494.4 28.1 reduce-scatter.26
  573.5 28.1 reduce-scatter.28
  607.2 19.6 all-gather.30
  648.5 28.1 reduce-scatter.30
  698.1 18.7 all-gather.32
  727.0 28.1 reduce-scatter.32
  760.3 19.6 all-gather.34
  782.5 28.1 reduce-scatter.22
  815.6 28.1 reduce-scatter.34
  847.8 135.9 all-reduce.9
  (1 shorter events, 18.7 us)
where the time goes:
time: 1010 us; the launch traced here: 1000 us
  waiting for transfers between devices  543 us (54%)
  matrix products  178 us (18%)
  other arithmetic  146 us (14%)
  blocking collectives  73.2 us (7%)
  local copies, waits for them, and re-layouts  32.8 us (3%)
  between operations  16.8 us (2%)
  starting transfers between devices  11.9 us (1%)
    reduce_scatter x3, waiting for transfers between devices, layer_forward(): lax.psum_scatter(project(mixed_heads, w_out).astype(jnp.bfloat16), 'tenso...  84.5 us
    reduce_scatter x3, waiting for transfers between devices, layer_backward(): lax.psum_scatter(times_transposed(grad_pre, w_up).astype(jnp.bfloat16), '...  76.5 us
    psum x1, blocking collectives, body(): lax.psum((grad_totals[0], grad_totals[1], grad_totals[6], grad_totals[7],...  61.3 us
    all_gather x3, waiting for transfers between devices, feed_rows(): lax.all_gather(normed_out.astype(jnp.bfloat16), 'tensor', axis=0, tiled=T...  57.1 us
    reduce_scatter x3, waiting for transfers between devices, layer_forward(): lax.psum_scatter(project(activated, w_down).astype(jnp.bfloat16), 'tensor...  56.5 us
    all_gather x3, waiting for transfers between devices, attention_rows(): lax.all_gather(normed_out.astype(jnp.bfloat16), 'tensor', axis=0, tiled=T...  56.3 us
    psum x1, waiting for transfers between devices, body(): lax.psum(grad_totals[2].astype(jnp.bfloat16), 'batch').astype(jnp.float32)  54.4 us
    reduce_scatter x3, waiting for transfers between devices, layer_backward(): lax.psum_scatter(partial_in.astype(jnp.bfloat16), 'tensor', scatter_dimen...  51.4 us
  transfers between devices with their start and end apart: 29, of which 26 were waited for; matrix products, arithmetic and copies ran while one was open for 14% of the time, Pallas kernels for 0%

commit v1 on v0

v1 whole, which is shorter than its diff:
```python
import jax
import jax.numpy as jnp
from jax import lax
from jax.sharding import PartitionSpec as P

HEAD_DIM = 64
EPSILON = 1e-05
LOW = jnp.bfloat16
FULL = jnp.float32

SIBLING = [(0, 1), (1, 0), (2, 3), (3, 2)]
PARTNER = [(0, 3), (3, 0), (1, 2), (2, 1)]
SWAP = [(0, 1), (1, 0)]


def dot(left, right):
    return jnp.dot(left, right, preferred_element_type=FULL)


def dot_rows(left, right):
    return lax.dot_general(left, right, (((0,), (0,)), ((), ())), preferred_element_type=FULL)


def dot_back(left, right):
    return lax.dot_general(left, right, (((1,), (1,)), ((), ())), preferred_element_type=FULL)


def norm_rows(values):
    center = values - jnp.mean(values, axis=-1, keepdims=True)
    inverse = lax.rsqrt(jnp.mean(center * center, axis=-1, keepdims=True) + EPSILON)
    return center * inverse, inverse


def norm_back(grad_norm, normed, inverse, gain):
    scaled = grad_norm * gain
    mean_one = jnp.mean(scaled, axis=-1, keepdims=True)
    mean_two = jnp.mean(scaled * normed, axis=-1, keepdims=True)
    return inverse * (scaled - mean_one - normed * mean_two)


def gelu_tanh(values):
    return jax.nn.gelu(values, approximate=True)


def to_partner(value):
    return lax.ppermute(value, "tensor", PARTNER)


def to_sibling(value):
    return lax.ppermute(value, "tensor", SIBLING)


class Place:
    def __init__(self, block):
        self.section = lax.axis_index("section")
        self.tensor = lax.axis_index("tensor")
        self.block = block
        self.first_core = (self.tensor % 2) == 0
        self.early = self.tensor < 2
        self.outer = (self.tensor == 0) | (self.tensor == 3)

    def low_high(self, own, other):
        return jnp.concatenate([jnp.where(self.early, own, other), jnp.where(self.early, other, own)], axis=0)

    def own(self, rows):
        return jnp.where(self.early, rows[: self.block], rows[self.block :])

    def in_order(self, own, other):
        n = self.block
        lows = own[:n], other[:n]
        highs = own[n:], other[n:]
        pick = self.outer
        return jnp.concatenate(
            [
                jnp.where(pick, lows[0], lows[1]),
                jnp.where(pick, lows[1], lows[0]),
                jnp.where(pick, highs[1], highs[0]),
                jnp.where(pick, highs[0], highs[1]),
            ],
            axis=0,
        )

    def split_order(self, rows):
        n = self.block
        parts = [rows[i * n : (i + 1) * n] for i in range(4)]
        pick = self.outer
        own = jnp.concatenate([jnp.where(pick, parts[0], parts[1]), jnp.where(pick, parts[3], parts[2])], axis=0)
        other = jnp.concatenate([jnp.where(pick, parts[1], parts[0]), jnp.where(pick, parts[2], parts[3])], axis=0)
        return own, other


def windows(place):
    n = place.block
    low = jnp.where(place.outer, 0, 1)
    high = 3 - low
    return ((0, low * n, 0, 2 * n), (n, high * n, (high - 2) * n, 3 * n))


def window_mask(segment, first_query, first_key, n, width):
    query_at = first_query + jnp.arange(n)
    key_at = first_key + jnp.arange(width)
    query_seg = lax.dynamic_slice_in_dim(segment, first_query, n)
    key_seg = lax.dynamic_slice_in_dim(segment, first_key, width)
    return (key_at[None, :] <= query_at[:, None]) & (key_seg[None, :] == query_seg[:, None])


def heads(rows):
    return rows.reshape(rows.shape[0], -1, HEAD_DIM)


def attend(place, segment, queries, keys, values):
    n = place.block
    outs, sums = [], []
    for row, first_query, first_key, width in windows(place):
        mask = window_mask(segment, first_query, first_key, n, width)
        q = heads(queries[row : row + n])
        k = heads(lax.dynamic_slice_in_dim(keys, first_key, width))
        v = heads(lax.dynamic_slice_in_dim(values, first_key, width))
        scores = jnp.einsum("qhd,khd->hqk", q, k, preferred_element_type=FULL) * HEAD_DIM**-0.5
        scores = jnp.where(mask[None], scores, -1e30)
        highest = jnp.max(scores, axis=-1, keepdims=True)
        exp_scores = jnp.exp(scores - highest)
        totals = jnp.sum(exp_scores, axis=-1, keepdims=True)
        probabilities = (exp_scores / totals).astype(LOW)
        mixed = jnp.einsum("hqk,khd->qhd", probabilities, v, preferred_element_type=FULL).astype(LOW)
        outs.append(mixed.reshape(n, -1))
        sums.append((highest + jnp.log(totals))[..., 0])
    return jnp.concatenate(outs, axis=0), jnp.concatenate(sums, axis=1)


def attend_back(place, segment, queries, keys, values, log_sums, grad_mixed):
    n = place.block
    scaling = HEAD_DIM**-0.5
    grad_queries = []
    grad_keys = jnp.zeros((keys.shape[0], keys.shape[1] // HEAD_DIM, HEAD_DIM), FULL)
    grad_values = jnp.zeros_like(grad_keys)
    for row, first_query, first_key, width in windows(place):
        mask = window_mask(segment, first_query, first_key, n, width)
        q = heads(queries[row : row + n])
        do = heads(grad_mixed[row : row + n])
        k = heads(lax.dynamic_slice_in_dim(keys, first_key, width))
        v = heads(lax.dynamic_slice_in_dim(values, first_key, width))
        scores = jnp.einsum("qhd,khd->hqk", q, k, preferred_element_type=FULL) * scaling
        scores = jnp.where(mask[None], scores, -1e30)
        probabilities = jnp.exp(scores - log_sums[:, row : row + n, None])
        dv = jnp.einsum("hqk,qhd->khd", probabilities.astype(LOW), do, preferred_element_type=FULL)
        dp = jnp.einsum("qhd,khd->hqk", do, v, preferred_element_type=FULL)
        inner = jnp.sum(probabilities * dp, axis=-1, keepdims=True)
        ds = (probabilities * (dp - inner)).astype(LOW)
        dq = jnp.einsum("hqk,khd->qhd", ds, k, preferred_element_type=FULL) * scaling
        dk = jnp.einsum("hqk,qhd->khd", ds, q, preferred_element_type=FULL) * scaling
        grad_queries.append(dq.reshape(n, -1).astype(LOW))
        old = lax.dynamic_slice_in_dim(grad_keys, first_key, width)
        grad_keys = lax.dynamic_update_slice_in_dim(grad_keys, old + dk, first_key, 0)
        old = lax.dynamic_slice_in_dim(grad_values, first_key, width)
        grad_values = lax.dynamic_update_slice_in_dim(grad_values, old + dv, first_key, 0)
    flat = (keys.shape[0], keys.shape[1])
    return jnp.concatenate(grad_queries, axis=0), grad_keys.reshape(flat), grad_values.reshape(flat)


def layer_forward(place, layer_in, segment, small, weights):
    gain_one, bias_one, gain_two, bias_two, b_down, b_up = small
    w_qkv, w_out, w_up, w_down = weights
    third = w_qkv.shape[1] // 3
    normed, _ = norm_rows(layer_in)
    a_one = (normed * gain_one + bias_one).astype(LOW)
    qkv = dot(a_one, w_qkv).astype(LOW)
    other = to_sibling(qkv[:, third:])
    both = place.in_order(qkv[:, third:], other)
    keys, values = both[:, :third], both[:, third:]
    queries = qkv[:, :third]
    mixed, log_sums = attend(place, segment, queries, keys, values)
    part = dot(mixed, w_out).astype(LOW)
    mid = layer_in + (part.astype(FULL) + to_partner(part).astype(FULL))
    normed_two, _ = norm_rows(mid)
    a_two = (normed_two * gain_two + bias_two).astype(LOW)
    pre = dot(a_two, w_up) + b_up
    active = gelu_tanh(pre).astype(LOW)
    part = dot(active, w_down).astype(LOW)
    out = mid + (part.astype(FULL) + to_partner(part).astype(FULL)) + b_down
    return out.astype(LOW), (layer_in, a_one, queries, keys, values, mixed, log_sums, mid, a_two, pre, active)


def layer_backward(place, grad_low, stored, segment, small, weights):
    gain_one, bias_one, gain_two, bias_two, b_down, b_up = small
    w_qkv, w_out, w_up, w_down = weights
    layer_in, a_one, queries, keys, values, mixed, log_sums, mid, a_two, pre, active = stored
    grad_out = grad_low.astype(FULL)
    grad_w_down = dot_rows(active, grad_low)
    _, gelu_back = jax.vjp(gelu_tanh, pre)
    grad_pre = gelu_back(dot_back(grad_low, w_down))[0].astype(LOW)
    part = dot_back(grad_pre, w_up).astype(LOW)
    grad_norm = part.astype(FULL) + to_partner(part).astype(FULL)
    grad_w_up = dot_rows(a_two, grad_pre)
    grad_b_up = jnp.sum(grad_pre.astype(FULL), axis=0)
    normed, inverse = norm_rows(mid)
    grad_mid = grad_out + norm_back(grad_norm, normed, inverse, gain_two)
    grad_gain_two = jnp.sum(grad_norm * normed, axis=0)
    grad_bias_two = jnp.sum(grad_norm, axis=0)
    grad_attn = grad_mid.astype(LOW)
    grad_w_out = dot_rows(mixed, grad_attn)
    grad_mixed = dot_back(grad_attn, w_out).astype(LOW)
    grad_q, grad_k, grad_v = attend_back(place, segment, queries, keys, values, log_sums, grad_mixed)
    own, other = place.split_order(jnp.concatenate([grad_k, grad_v], axis=1))
    grad_kv = (own + to_sibling(other.astype(LOW)).astype(FULL)).astype(LOW)
    grad_qkv = jnp.concatenate([grad_q, grad_kv], axis=1)
    part = dot_back(grad_qkv, w_qkv).astype(LOW)
    grad_norm = part.astype(FULL) + to_partner(part).astype(FULL)
    grad_w_qkv = dot_rows(a_one, grad_qkv)
    normed, inverse = norm_rows(layer_in)
    grad_in = grad_mid + norm_back(grad_norm, normed, inverse, gain_one)
    grad_gain_one = jnp.sum(grad_norm * normed, axis=0)
    grad_bias_one = jnp.sum(grad_norm, axis=0)
    grad_b_down = jnp.sum(grad_out, axis=0)
    small_sums = jnp.stack([grad_gain_one, grad_bias_one, grad_gain_two, grad_bias_two, grad_b_down])
    return grad_in.astype(LOW), small_sums, grad_b_up, (grad_w_qkv, grad_w_out, grad_w_up, grad_w_down)


def body(
    inputs, cotangent, segments, ln1_gain, ln1_bias, w_query, w_key, w_value, w_out,
    ln2_gain, ln2_bias, w_up, b_up, w_down, b_down,
):
    place = Place(inputs.shape[1])
    section = place.section
    on_first = section == 0
    first_core = place.first_core
    segment = jnp.where(on_first, segments[0, 0], segments[1, 0])

    def whole_rows(both):
        own = jnp.where(on_first, both[0], both[1])
        return place.low_high(own, to_partner(own))

    layer_in = whole_rows(inputs)
    grad_last = whole_rows(cotangent)

    small_own = jnp.concatenate([ln1_gain, ln1_bias, ln2_gain, ln2_bias, b_down, b_up], axis=0)
    small_other = lax.ppermute(small_own, "section", SWAP)
    qkv_own = jnp.concatenate([w_query[0], w_key[0], w_value[0]], axis=1)
    quarters_own = (qkv_own, w_out[0], w_up[0], w_down[0])
    quarters_other = tuple(lax.ppermute(q, "section", SWAP) for q in quarters_own)

    def layer_weights(layer):
        here = section == layer
        quarters = [jnp.where(here, a, b) for a, b in zip(quarters_own, quarters_other)]
        siblings = [to_sibling(q) for q in quarters]
        small = jnp.where(here, small_own, small_other)
        b_up_sibling = to_sibling(small[5])
        one = [jnp.where(first_core, a, b) for a, b in zip(quarters[:2], siblings[:2])]
        two = [jnp.where(first_core, b, a) for a, b in zip(quarters[:2], siblings[:2])]
        width = one[0].shape[1] // 3
        pieces = []
        for i in range(3):
            pieces += [one[0][:, i * width : (i + 1) * width], two[0][:, i * width : (i + 1) * width]]
        qkv = jnp.concatenate(pieces, axis=1)
        out = jnp.concatenate([one[1], two[1]], axis=0)
        up = jnp.concatenate([quarters[2], siblings[2]], axis=1)
        down = jnp.concatenate([quarters[3], siblings[3]], axis=0)
        rows = tuple(small[i] for i in range(5)) + (jnp.concatenate([small[5], b_up_sibling]),)
        return rows, (qkv, out, up, down)

    small_0, weights_0 = layer_weights(0)
    small_1, weights_1 = layer_weights(1)
    out_0, stored_0 = layer_forward(place, layer_in.astype(FULL), segment, small_0, weights_0)
    out_1, stored_1 = layer_forward(place, out_0.astype(FULL), segment, small_1, weights_1)
    back_1, sums_1, bup_1, grads_1 = layer_backward(place, grad_last, stored_1, segment, small_1, weights_1)
    back_0, sums_0, bup_0, grads_0 = layer_backward(place, back_1, stored_0, segment, small_0, weights_0)

    def quarter_grads(grads, grad_b_up):
        qkv, out, up, down = grads
        width = qkv.shape[1] // 6
        ones = [jnp.concatenate([qkv[:, 2 * i * width : (2 * i + 1) * width] for i in range(3)], axis=1), out[:width]]
        twos = [jnp.concatenate([qkv[:, (2 * i + 1) * width : (2 * i + 2) * width] for i in range(3)], axis=1), out[width:]]
        keep = [jnp.where(first_core, a, b) for a, b in zip(ones, twos)]
        send = [jnp.where(first_core, b, a) for a, b in zip(ones, twos)]
        half = up.shape[1] // 2
        keep += [up[:, :half], down[:half], grad_b_up[:half][None]]
        send += [up[:, half:], down[half:], grad_b_up[half:][None]]
        return [a + to_sibling(b.astype(LOW)).astype(FULL) for a, b in zip(keep, send)]

    quarter_0 = quarter_grads(grads_0, bup_0)
    quarter_1 = quarter_grads(grads_1, bup_1)
    totals = []
    for a, b in zip(quarter_0, quarter_1):
        mine = jnp.where(on_first, a, b)
        theirs = jnp.where(on_first, b, a).astype(LOW)
        total = (mine + lax.ppermute(theirs, "section", SWAP).astype(FULL)).astype(LOW)
        totals.append(lax.psum(total, "batch").astype(FULL))
    sums = lax.psum(jnp.stack([sums_0, sums_1]), ("section", "batch", "tensor")) * 0.5
    sums = jnp.where(on_first, sums[0], sums[1])

    def both_micro(first, second):
        first, second = place.own(first), place.own(second)
        mine = jnp.where(on_first, first, second)
        theirs = lax.ppermute(jnp.where(on_first, second, first), "section", SWAP)
        return jnp.stack([jnp.where(on_first, mine, theirs), jnp.where(on_first, theirs, mine)])[None]

    forward_out = both_micro(out_0, out_1)
    backward_out = both_micro(back_0, back_1)
    width = totals[0].shape[1] // 3
    return (
        forward_out,
        backward_out,
        sums[0][None],
        sums[1][None],
        totals[0][:, :width][None],
        totals[0][:, width : 2 * width][None],
        totals[0][:, 2 * width :][None],
        totals[1][None],
        sums[2][None],
        sums[3][None],
        totals[2][None],
        totals[4],
        totals[3][None],
        sums[4][None],
    )


def solution(mesh):
    rows = P(None, ("batch", "tensor"), None)
    layer = P("section", None)
    by_column = P("section", None, "tensor")
    by_row = P("section", "tensor", None)
    kept = P("section", None, ("batch", "tensor"), None)
    return jax.shard_map(
        body,
        mesh=mesh,
        in_specs=(
            rows, rows, P(None, "batch", None), layer, layer, by_column, by_column, by_column, by_row,
            layer, layer, by_column, P("section", "tensor"), by_row, layer,
        ),
        out_specs=(
            kept, kept, layer, layer, by_column, by_column, by_column, by_row,
            layer, layer, by_column, P("section", "tensor"), by_row, layer,
        ),
        check_vma=False,
    )
```

time: 1010 us -> 657 us (0.65)
  waiting for transfers between devices: 543 us -> 278 us
  matrix products: 178 us -> 86 us
  other arithmetic: 146 us -> 106 us
  local copies, waits for them, and re-layouts: 32.8 us -> 70 us
  starting transfers between devices: 11.9 us -> 32.5 us
  blocking collectives: 73.2 us -> 60.3 us
    reduce_scatter x12 -> x0, waiting for transfers between devices: 269 us -> none  [the longest x3 84.5 us: layer_forward(): lax.psum_scatter(project(mixed_heads, w_out).astype(jnp.bfloat16), 'tenso...]
    ppermute x4 -> x46, waiting for transfers between devices: 40.2 us -> 219 us  [the longest x10 97.3 us: to_partner(): return lax.ppermute(value, 'tensor', PARTNER)]
    all_gather x12 -> x0, waiting for transfers between devices: 179 us -> none  [the longest x3 57.1 us: feed_rows(): lax.all_gather(normed_out.astype(jnp.bfloat16), 'tensor', axis=0, tiled=T...]
    dot_general x96 -> x48, matrix products: 178 us -> 86 us  [the longest x8 20.4 us: dot_back(): lax.dot_general(left, right, (((1,), (1,)), ((), ())), preferred_element_...]
    another operation x19 -> x5, other arithmetic: 33.8 us -> 5.7 us  [body(): stored_all = jax.tree.map(lambda *items: jnp.stack(items), *stored_list)]
    ppermute x4 -> x46, starting transfers between devices: 9.48 us -> 32.5 us  [the longest x10 11.3 us: to_partner(): return lax.ppermute(value, 'tensor', PARTNER)]
    dynamic_slice x1 -> x14, local copies, waits for them, and re-layouts: 0.85 us -> 15.4 us  [the longest x6 8.19 us: attend(): k = heads(lax.dynamic_slice_in_dim(keys, first_key, width))]
    psum x2, blocking collectives: 73.2 us -> 60.3 us  [the longest x1 47.8 us: body(): lax.psum(jnp.stack([sums_0, sums_1]), ('section', 'batch', 'tensor')) * 0.5]
  transfers between devices with their start and end apart: 29 -> 47, of which waited for: 26 -> 19; matrix products, arithmetic and copies ran while one was open for 14% -> 36% of each run, Pallas kernels for 0% -> 0%
where the time goes in v1:
time: 657 us; the launch traced here: 649 us
  waiting for transfers between devices  278 us (42%)
  other arithmetic  106 us (16%)
  matrix products  86 us (13%)
  local copies, waits for them, and re-layouts  70 us (11%)
  blocking collectives  60.3 us (9%)
  starting transfers between devices  32.5 us (5%)
  between operations  16.8 us (3%)
    ppermute x10, waiting for transfers between devices, to_partner(): return lax.ppermute(value, 'tensor', PARTNER)  97.3 us
    ppermute x5, waiting for transfers between devices, body(): lax.ppermute(theirs, 'section', SWAP).astype(FULL)  72.1 us
    psum x1, waiting for transfers between devices, body(): totals.append(lax.psum(total, 'batch').astype(FULL))  58.6 us
    ppermute x4, waiting for transfers between devices, body(): lax.ppermute(q, 'section', SWAP)  49 us
    psum x1, blocking collectives, body(): lax.psum(jnp.stack([sums_0, sums_1]), ('section', 'batch', 'tensor')) * 0.5  47.8 us
    dot_general x8, matrix products, dot_back(): lax.dot_general(left, right, (((1,), (1,)), ((), ())), preferred_element_...  20.4 us
    dot_general x8, matrix products, dot(): return jnp.dot(left, right, preferred_element_type=FULL)  15.9 us
    unnamed x348, local copies, waits for them, and re-layouts  13.4 us
  transfers between devices with their start and end apart: 47, of which 19 were waited for; matrix products, arithmetic and copies ran while one was open for 36% of the time, Pallas kernels for 0%

profile of v1, /device:TPU:0, one launch (start us, length us, event | category | flops | bytes accessed | tf_op | source)
XLA Modules:
  0.0 649.0 jit_solution(10404394202805738032)
XLA Ops:
  29.9 10.5 %collective-permute-done.2 = bf16[768,576]{0,1:T(8,128)(2,1)} collective-permute-done((bf16[768,576]{0,1:T(8,128)(2,1)}, bf16[768,576]{0,1:T(8,128)(2,1)}, u32[]{:S(2)}, u32[]{:S(2)}) %collective-permute-start.2) | collective-permute-done | bytes 884768 | tf_op jit(solution)/shard_map/ppermute | solution.py:240
  48.2 17.5 %collective-permute-done.11 = bf16[768,768]{1,0:T(8,128)(2,1)} collective-permute-done((bf16[768,768]{1,0:T(8,128)(2,1)S(1)}, bf16[768,768]{1,0:T(8,128)(2,1)}, u32[]{:S(2)}, u32[]{:S(2)}) %collective-permute-start.11) | collective-permute-done | bytes 1179680 | tf_op jit(solution)/shard_map/ppermute | solution.py:240
  68.5 20.9 %collective-permute-done.8 = bf16[768,768]{1,0:T(8,128)(2,1)S(1)} collective-permute-done((bf16[768,768]{1,0:T(8,128)(2,1)}, bf16[768,768]{1,0:T(8,128)(2,1)S(1)}, u32[]{:S(2)}, u32[]{:S(2)}) %collective-permute-start.8) | collective-permute-done | bytes 1179680 | tf_op jit(solution)/shard_map/ppermute | solution.py:240
  109.3 3.8 fusion.133
  116.6 16.9 %collective-permute-done.7 = bf16[512,768]{1,0:T(8,128)(2,1)S(1)} collective-permute-done((bf16[512,768]{1,0:T(8,128)(2,1)S(1)}, bf16[512,768]{1,0:T(8,128)(2,1)S(1)}, u32[]{:S(2)}, u32[]{:S(2)}) %collective-permute-start.7) | collective-permute-done | bytes 786464 | tf_op jit(solution)/shard_map/ppermute | solution.py:46
  141.6 17.6 %collective-permute-done.13 = bf16[512,768]{1,0:T(8,128)(2,1)S(1)} collective-permute-done((bf16[512,768]{1,0:T(8,128)(2,1)S(1)}, bf16[512,768]{1,0:T(8,128)(2,1)S(1)}, u32[]{:S(2)}, u32[]{:S(2)}) %collective-permute-start.13) | collective-permute-done | bytes 786464 | tf_op jit(solution)/shard_map/ppermute | solution.py:46
  193.3 18.1 %collective-permute-done.17 = bf16[512,768]{1,0:T(8,128)(2,1)S(1)} collective-permute-done((bf16[512,768]{1,0:T(8,128)(2,1)S(1)}, bf16[512,768]{1,0:T(8,128)(2,1)S(1)}, u32[]{:S(2)}, u32[]{:S(2)}) %collective-permute-start.17) | collective-permute-done | bytes 786464 | tf_op jit(solution)/shard_map/ppermute | solution.py:46
  215.4 4.6 convert_reduce_fusion
  224.5 3.6 fusion.85
  236.6 6.1 collective-permute-done.24
  244.5 15.1 %collective-permute-done.21 = bf16[512,768]{1,0:T(8,128)(2,1)S(1)} collective-permute-done((bf16[512,768]{1,0:T(8,128)(2,1)S(1)}, bf16[512,768]{1,0:T(8,128)(2,1)S(1)}, u32[]{:S(2)}, u32[]{:S(2)}) %collective-permute-start.21) | collective-permute-done | bytes 786464 | tf_op jit(solution)/shard_map/ppermute | solution.py:46
  269.9 3.4 multiply_reduce_fusion.1
  280.1 4.4 multiply_convert_fusion.1
  312.2 13.5 %collective-permute-done.26 = bf16[512,768]{1,0:T(8,128)(2,1)S(1)} collective-permute-done((bf16[512,768]{1,0:T(8,128)(2,1)S(1)}, bf16[512,768]{1,0:T(8,128)(2,1)S(1)}, u32[]{:S(2)}, u32[]{:S(2)}) %collective-permute-start.26) | collective-permute-done | bytes 786464 | tf_op jit(solution)/shard_map/ppermute | solution.py:46
  328.9 4.6 convert_reduce_fusion.1
  348.1 8.5 %collective-permute-done.27 = bf16[512,768]{1,0:T(8,128)(2,1)S(1)} collective-permute-done((bf16[512,768]{1,0:T(8,128)(2,1)S(1)}, bf16[512,768]{1,0:T(8,128)(2,1)S(1)}, u32[]{:S(2)}, u32[]{:S(2)}) %collective-permute-start.27) | collective-permute-done | bytes 786464 | tf_op jit(solution)/shard_map/ppermute | solution.py:46
  365.6 3.6 multiply_reduce_fusion
  413.7 4.8 collective-permute-done.36
  423.4 20.5 %collective-permute-done.39 = bf16[768,768]{1,0:T(8,128)(2,1)S(1)} collective-permute-done((bf16[768,768]{1,0:T(8,128)(2,1)S(1)}, bf16[768,768]{1,0:T(8,128)(2,1)S(1)}, u32[]{:S(2)}, u32[]{:S(2)}) %collective-permute-start.39) | collective-permute-done | bytes 1179680 | tf_op jit(solution)/shard_map/ppermute | solution.py:286
  447.9 21.2 %collective-permute-done.45 = bf16[768,768]{1,0:T(8,128)(2,1)S(1)} collective-permute-done((bf16[768,768]{1,0:T(8,128)(2,1)}, bf16[768,768]{1,0:T(8,128)(2,1)S(1)}, u32[]{:S(2)}, u32[]{:S(2)}) %collective-permute-start.45) | collective-permute-done | bytes 1179680 | tf_op jit(solution)/shard_map/ppermute | solution.py:286
  472.1 23.9 %collective-permute-done.33 = bf16[768,576]{0,1:T(8,128)(2,1)S(1)} collective-permute-done((bf16[768,576]{0,1:T(8,128)(2,1)S(1)}, bf16[768,576]{0,1:T(8,128)(2,1)S(1)}, u32[]{:S(2)}, u32[]{:S(2)}) %collective-permute-start.33) | collective-permute-done | bytes 884768 | tf_op jit(solution)/shard_map/ppermute | solution.py:286
  508.6 12.5 %psum.46 = bf16[1,768]{1,0:T(2,128)(2,1)S(1)} all-reduce(bf16[1,768]{1,0:T(2,128)(2,1)S(1)} %fusion.154), channel_id=1, replica_groups=mesh['section'=2,'batch'=4,'tensor'=4] {'batch'}, use_global_device_ids=true, to_apply=%region_44.45 | all-reduce | flops 768 | bytes 3072 | tf_op jit(solution)/shard_map/psum | solution.py:287
  527.1 47.8 %psum.42 = f32[2,5,768]{2,1,0:T(8,128)S(1)} all-reduce(f32[2,5,768]{2,1,0:T(8,128)S(1)} %pad_maximum_fusion.57), channel_id=1, replica_groups=mesh['section'=2,'batch'=4,'tensor'=4] {'section','batch','tensor'}, use_global_device_ids=true, to_apply=%region_38.39 | all-reduce | flops 7680 | bytes 61440 | tf_op jit(solution)/shard_map/psum | solution.py:288
  576.6 58.6 %all-reduce.7.cloned.1.call-done = (bf16[768,576]{0,1:T(8,128)(2,1)}, bf16[1,192,768]{2,1,0:T(8,128)(2,1)}, bf16[1,768,768]{2,1,0:T(8,128)(2,1)}, bf16[1,768,768]{2,1,0:T(8,128)(2,1)}) async-done(((bf16[768,576]{0,1:T(8,128)(2,1)}, bf16[1,192,768]{2,1,0:T(8,128)(2,1)}, bf16[1,768,768]{2,1,0:T(8,128)(2,1)}, bf16[1,768,768]{2,1,0:T(8,128)(2,1)}), (bf16[768,576]{0,1:T(8,128)(2,1)}, ...) | async-done | bytes 3538960 | tf_op jit(solution)/shard_map/psum | solution.py:287
  (652 shorter events, 270.0 us)
Async XLA Ops:
  7.2 628.0 %all-reduce.7.cloned.1.call-start = ((), (), s32[]{:S(2)}) async-start(), calls=%async_computation | async-start | bytes 7077888 | tf_op jit(solution)/shard_map/psum | solution.py:287
  13.4 27.0 %collective-permute-start.2 = (bf16[768,576]{0,1:T(8,128)(2,1)}, bf16[768,576]{0,1:T(8,128)(2,1)}, u32[]{:S(2)}, u32[]{:S(2)}) collective-permute-start(bf16[768,576]{0,1:T(8,128)(2,1)} %pad_maximum_fusion.32), channel_id=1, source_target_pairs={{0,16},{16,0},{1,17},{17,1},{2,18},{18,2},{3,19},{19,3},{4,20},{20... | collective-permute-start | bytes 2654216 | tf_op jit(solution)/shard_map/ppermute | solution.py:240
  16.3 49.4 %collective-permute-start.11 = (bf16[768,768]{1,0:T(8,128)(2,1)S(1)}, bf16[768,768]{1,0:T(8,128)(2,1)}, u32[]{:S(2)}, u32[]{:S(2)}) collective-permute-start(bf16[768,768]{1,0:T(8,128)(2,1)S(1)} %bitcast.233), channel_id=1, source_target_pairs={{0,16},{16,0},{1,17},{17,1},{2,18},{18,2},{3,19},{19,3},{4,20},{20... | collective-permute-start | bytes 3538952 | tf_op jit(solution)/shard_map/ppermute | solution.py:240
  22.1 67.3 %collective-permute-start.8 = (bf16[768,768]{1,0:T(8,128)(2,1)}, bf16[768,768]{1,0:T(8,128)(2,1)S(1)}, u32[]{:S(2)}, u32[]{:S(2)}) collective-permute-start(bf16[768,768]{1,0:T(8,128)(2,1)} %bitcast.234), channel_id=1, source_target_pairs={{0,16},{16,0},{1,17},{17,1},{2,18},{18,2},{3,19},{19,3},{4,20},{20... | collective-permute-start | bytes 3538952 | tf_op jit(solution)/shard_map/ppermute | solution.py:240
  24.2 139.9 %collective-permute-start.23 = (bf16[256,768]{1,0:T(8,128)(2,1)}, bf16[256,768]{1,0:T(8,128)(2,1)}, u32[]{:S(2)}, u32[]{:S(2)}) collective-permute-start(bf16[256,768]{1,0:T(8,128)(2,1)} %select_bitcast_fusion.2), channel_id=1, source_target_pairs={{0,3},{3,0},{1,2},{2,1},{4,7},{7,4},{5,6},{6,5},{8,11},{11,8},{9,1... | collective-permute-start | bytes 1179656 | tf_op jit(solution)/shard_map/ppermute | solution.py:46
  43.4 119.4 %collective-permute-start.19 = (f32[768]{0:T(1024)}, f32[768]{0:T(1024)}, u32[]{:S(2)}, u32[]{:S(2)}) collective-permute-start(f32[768]{0:T(1024)} %get-tuple-element.73), channel_id=1, source_target_pairs={{0,1},{1,0},{2,3},{3,2},{4,5},{5,4},{6,7},{7,6},{8,9},{9,8},{10,11... | collective-permute-start | bytes 9224 | tf_op jit(solution)/shard_map/ppermute | solution.py:50
  45.3 120.8 %collective-permute-start.16 = (bf16[192,768]{1,0:T(8,128)(2,1)}, bf16[192,768]{1,0:T(8,128)(2,1)}, u32[]{:S(2)}, u32[]{:S(2)}) collective-permute-start(bf16[192,768]{1,0:T(8,128)(2,1)} %get-tuple-element.170), channel_id=1, source_target_pairs={{0,1},{1,0},{2,3},{3,2},{4,5},{5,4},{6,7},{7,6},{8,9},{9,8},{10,11... | collective-permute-start | bytes 884744 | tf_op jit(solution)/shard_map/ppermute | solution.py:50
  65.7 26.9 %collective-permute-start.4 = (bf16[512,768]{1,0:T(8,128)(2,1)}, bf16[512,768]{1,0:T(8,128)(2,1)}, u32[]{:S(2)}, u32[]{:S(2)}) collective-permute-start(bf16[512,768]{1,0:T(8,128)(2,1)} %slice.486), channel_id=1, source_target_pairs={{0,1},{1,0},{2,3},{3,2},{4,5},{5,4},{6,7},{7,6},{8,9},{9,8},{10,11... | collective-permute-start | bytes 2359304 | tf_op jit(solution)/shard_map/ppermute | solution.py:50
  89.4 24.4 %collective-permute-start.14 = (bf16[768,576]{0,1:T(8,128)(2,1)}, bf16[768,576]{0,1:T(8,128)(2,1)}, u32[]{:S(2)}, u32[]{:S(2)}) collective-permute-start(bf16[768,576]{0,1:T(8,128)(2,1)} %get-tuple-element.141), channel_id=1, source_target_pairs={{0,1},{1,0},{2,3},{3,2},{4,5},{5,4},{6,7},{7,6},{8,9},{9,8},{10,11... | collective-permute-start | bytes 2654216 | tf_op jit(solution)/shard_map/ppermute | solution.py:50
  92.6 41.8 %collective-permute-start.9 = (bf16[768,768]{1,0:T(8,128)(2,1)}, bf16[768,768]{1,0:T(8,128)(2,1)}, u32[]{:S(2)}, u32[]{:S(2)}) collective-permute-start(bf16[768,768]{1,0:T(8,128)(2,1)} %get-tuple-element.125), channel_id=1, source_target_pairs={{0,1},{1,0},{2,3},{3,2},{4,5},{5,4},{6,7},{7,6},{8,9},{9,8},{10,11... | collective-permute-start | bytes 3538952 | tf_op jit(solution)/shard_map/ppermute | solution.py:50
  168.0 44.1 %collective-permute-start.18 = (bf16[768,768]{1,0:T(8,128)(2,1)}, bf16[768,768]{1,0:T(8,128)(2,1)}, u32[]{:S(2)}, u32[]{:S(2)}) collective-permute-start(bf16[768,768]{1,0:T(8,128)(2,1)} %get-tuple-element.124), channel_id=1, source_target_pairs={{0,1},{1,0},{2,3},{3,2},{4,5},{5,4},{6,7},{7,6},{8,9},{9,8},{10,11... | collective-permute-start | bytes 3538952 | tf_op jit(solution)/shard_map/ppermute | solution.py:50
  168.1 47.3 %collective-permute-start.20 = (bf16[768,768]{1,0:T(8,128)(2,1)}, bf16[768,768]{1,0:T(8,128)(2,1)}, u32[]{:S(2)}, u32[]{:S(2)}) collective-permute-start(bf16[768,768]{1,0:T(8,128)(2,1)} %get-tuple-element.126), channel_id=1, source_target_pairs={{0,1},{1,0},{2,3},{3,2},{4,5},{5,4},{6,7},{7,6},{8,9},{9,8},{10,11... | collective-permute-start | bytes 3538952 | tf_op jit(solution)/shard_map/ppermute | solution.py:50
  228.1 31.5 %collective-permute-start.21 = (bf16[512,768]{1,0:T(8,128)(2,1)S(1)}, bf16[512,768]{1,0:T(8,128)(2,1)S(1)}, u32[]{:S(2)}, u32[]{:S(2)}) collective-permute-start(bf16[512,768]{1,0:T(8,128)(2,1)S(1)} %fusion.85), channel_id=1, source_target_pairs={{0,3},{3,0},{1,2},{2,1},{4,7},{7,4},{5,6},{6,5},{8,11},{11,8},{9,1... | collective-permute-start | bytes 2359304 | tf_op jit(solution)/shard_map/ppermute | solution.py:46
  234.3 170.9 %collective-permute-start.38 = (bf16[768,768]{1,0:T(8,128)(2,1)}, bf16[768,768]{1,0:T(8,128)(2,1)}, u32[]{:S(2)}, u32[]{:S(2)}) collective-permute-start(bf16[768,768]{1,0:T(8,128)(2,1)} %slice.789), channel_id=1, source_target_pairs={{0,1},{1,0},{2,3},{3,2},{4,5},{5,4},{6,7},{7,6},{8,9},{9,8},{10,11... | collective-permute-start | bytes 3538952 | tf_op jit(solution)/shard_map/ppermute | solution.py:50
  235.7 172.9 %collective-permute-start.44 = (bf16[768,768]{1,0:T(8,128)(2,1)}, bf16[768,768]{1,0:T(8,128)(2,1)}, u32[]{:S(2)}, u32[]{:S(2)}) collective-permute-start(bf16[768,768]{1,0:T(8,128)(2,1)} %slice.787), channel_id=1, source_target_pairs={{0,1},{1,0},{2,3},{3,2},{4,5},{5,4},{6,7},{7,6},{8,9},{9,8},{10,11... | collective-permute-start | bytes 3538952 | tf_op jit(solution)/shard_map/ppermute | solution.py:50
  301.1 97.4 %collective-permute-start.35 = (bf16[192,768]{1,0:T(8,128)(2,1)}, bf16[192,768]{1,0:T(8,128)(2,1)}, u32[]{:S(2)}, u32[]{:S(2)}) collective-permute-start(bf16[192,768]{1,0:T(8,128)(2,1)} %select_convert_fusion.10), channel_id=1, source_target_pairs={{0,1},{1,0},{2,3},{3,2},{4,5},{5,4},{6,7},{7,6},{8,9},{9,8},{10,11... | collective-permute-start | bytes 884744 | tf_op jit(solution)/shard_map/ppermute | solution.py:50
  398.6 105.6 %collective-permute-start.41 = (bf16[1,768]{1,0:T(2,128)(2,1)}, bf16[1,768]{1,0:T(2,128)(2,1)S(1)}, u32[]{:S(2)}, u32[]{:S(2)}) collective-permute-start(bf16[1,768]{1,0:T(2,128)(2,1)} %convert_element_type.468), channel_id=1, source_target_pairs={{0,1},{1,0},{2,3},{3,2},{4,5},{5,4},{6,7},{7,6},{8,9},{9,8},{10,11... | collective-permute-start | bytes 4616 | tf_op jit(solution)/shard_map/ppermute | solution.py:50
  409.5 34.3 %collective-permute-start.39 = (bf16[768,768]{1,0:T(8,128)(2,1)S(1)}, bf16[768,768]{1,0:T(8,128)(2,1)S(1)}, u32[]{:S(2)}, u32[]{:S(2)}) collective-permute-start(bf16[768,768]{1,0:T(8,128)(2,1)S(1)} %select_convert_fusion.1), channel_id=1, source_target_pairs={{0,16},{16,0},{1,17},{17,1},{2,18},{18,2},{3,19},{19,3},{4,20},{20... | collective-permute-start | bytes 3538952 | tf_op jit(solution)/shard_map/ppermute | solution.py:286
  418.6 50.6 %collective-permute-start.45 = (bf16[768,768]{1,0:T(8,128)(2,1)}, bf16[768,768]{1,0:T(8,128)(2,1)S(1)}, u32[]{:S(2)}, u32[]{:S(2)}) collective-permute-start(bf16[768,768]{1,0:T(8,128)(2,1)} %select_convert_fusion), channel_id=1, source_target_pairs={{0,16},{16,0},{1,17},{17,1},{2,18},{18,2},{3,19},{19,3},{4,20},{20... | collective-permute-start | bytes 3538952 | tf_op jit(solution)/shard_map/ppermute | solution.py:286
  421.3 81.6 %collective-permute-start.22 = (bf16[256,768]{1,0:T(8,128)(2,1)}, bf16[256,768]{1,0:T(8,128)(2,1)}, u32[]{:S(2)}, u32[]{:S(2)}) collective-permute-start(bf16[256,768]{1,0:T(8,128)(2,1)} %get-tuple-element.97), channel_id=1, source_target_pairs={{0,16},{16,0},{1,17},{17,1},{2,18},{18,2},{3,19},{19,3},{4,20},{20... | collective-permute-start | bytes 1179656 | tf_op jit(solution)/shard_map/ppermute | solution.py:294
  422.6 81.6 %collective-permute-start.40 = (bf16[1,768]{1,0:T(2,128)(2,1)S(1)}, bf16[1,768]{1,0:T(2,128)(2,1)S(1)}, u32[]{:S(2)}, u32[]{:S(2)}) collective-permute-start(bf16[1,768]{1,0:T(2,128)(2,1)S(1)} %copy-done.152), channel_id=1, source_target_pairs={{0,1},{1,0},{2,3},{3,2},{4,5},{5,4},{6,7},{7,6},{8,9},{9,8},{10,11... | collective-permute-start | bytes 4616 | tf_op jit(solution)/shard_map/ppermute | solution.py:50
  443.8 52.1 %collective-permute-start.33 = (bf16[768,576]{0,1:T(8,128)(2,1)S(1)}, bf16[768,576]{0,1:T(8,128)(2,1)S(1)}, u32[]{:S(2)}, u32[]{:S(2)}) collective-permute-start(bf16[768,576]{0,1:T(8,128)(2,1)S(1)} %select_convert_fusion.2), channel_id=1, source_target_pairs={{0,16},{16,0},{1,17},{17,1},{2,18},{18,2},{3,19},{19,3},{4,20},{20... | collective-permute-start | bytes 2654216 | tf_op jit(solution)/shard_map/ppermute | solution.py:286
  501.5 20.1 %collective-permute-start.29 = (bf16[512,768]{1,0:T(8,128)(2,1)S(1)}, bf16[512,768]{1,0:T(8,128)(2,1)}, u32[]{:S(2)}, u32[]{:S(2)}) collective-permute-start(bf16[512,768]{1,0:T(8,128)(2,1)S(1)} %convolution_convert_fusion.2), channel_id=1, source_target_pairs={{0,3},{3,0},{1,2},{2,1},{4,7},{7,4},{5,6},{6,5},{8,11},{11,8},{9,1... | collective-permute-start | bytes 2359304 | tf_op jit(solution)/shard_map/ppermute | solution.py:46
  525.8 49.8 %collective-permute-start.30 = (bf16[256,768]{1,0:T(8,128)(2,1)S(1)}, bf16[256,768]{1,0:T(8,128)(2,1)S(1)}, u32[]{:S(2)}, u32[]{:S(2)}) collective-permute-start(bf16[256,768]{1,0:T(8,128)(2,1)S(1)} %get-tuple-element.90), channel_id=1, source_target_pairs={{0,16},{16,0},{1,17},{17,1},{2,18},{18,2},{3,19},{19,3},{4,20},{20... | collective-permute-start | bytes 1179656 | tf_op jit(solution)/shard_map/ppermute | solution.py:294
  (192 other events, 1496.8 us)
Sparse Core Ops, SparseCore 0:
  497.7 137.4 all-reduce.6

commit v2 on v1

v2 whole, which is shorter than its diff:
```python
import functools

import jax
import jax.numpy as jnp
from jax import lax
from jax.experimental import pallas as pl
from jax.experimental.pallas import tpu as pltpu
from jax.sharding import PartitionSpec as P

HEAD_DIM = 64
EPSILON = 1e-05
LOW = jnp.bfloat16
FULL = jnp.float32
SCALING = HEAD_DIM**-0.5
MASKED = -1e30
VMEM_BYTES = 48 * 1024 * 1024

SIBLING = [(0, 1), (1, 0), (2, 3), (3, 2)]
PARTNER = [(0, 3), (3, 0), (1, 2), (2, 1)]
SWAP = [(0, 1), (1, 0)]


def dot(left, right):
    return jnp.dot(left, right, preferred_element_type=FULL)


def dot_rows(left, right):
    return lax.dot_general(left, right, (((0,), (0,)), ((), ())), preferred_element_type=FULL)


def dot_back(left, right):
    return lax.dot_general(left, right, (((1,), (1,)), ((), ())), preferred_element_type=FULL)


def norm_rows(values):
    center = values - jnp.mean(values, axis=-1, keepdims=True)
    inverse = lax.rsqrt(jnp.mean(center * center, axis=-1, keepdims=True) + EPSILON)
    return center * inverse, inverse


def norm_back(grad_norm, normed, inverse, gain):
    scaled = grad_norm * gain
    mean_one = jnp.mean(scaled, axis=-1, keepdims=True)
    mean_two = jnp.mean(scaled * normed, axis=-1, keepdims=True)
    return inverse * (scaled - mean_one - normed * mean_two)


def to_partner(value):
    return lax.ppermute(value, "tensor", PARTNER)


def to_sibling(value):
    return lax.ppermute(value, "tensor", SIBLING)


def call(kernel, operands, outs, flops, scalars=0, scratch=()):
    moved = sum(a.size * a.dtype.itemsize for a in operands) + sum(o.size * o.dtype.itemsize for o in outs)
    specs = [pl.BlockSpec(memory_space=pltpu.SMEM)] * scalars
    specs += [pl.BlockSpec(memory_space=pltpu.VMEM)] * (len(operands) - scalars)
    return pl.pallas_call(
        kernel,
        out_shape=tuple(outs),
        in_specs=specs,
        out_specs=tuple(pl.BlockSpec(memory_space=pltpu.VMEM) for _ in outs),
        scratch_shapes=list(scratch),
        compiler_params=pltpu.CompilerParams(vmem_limit_bytes=VMEM_BYTES),
        cost_estimate=pl.CostEstimate(flops=int(flops), bytes_accessed=int(moved), transcendentals=0),
    )(*operands)


def shape(*dims, dtype=LOW):
    return jax.ShapeDtypeStruct(dims, dtype)


def project_kernel(first, *refs):
    if first:
        rows_ref, gain, bias, w_own, w_sib, a_ref, q_ref, kv_ref, send_ref = refs
        layer_in = rows_ref[...].astype(FULL)
    else:
        mid, part, got, b_down, gain, bias, w_own, w_sib, in_ref, a_ref, q_ref, kv_ref, send_ref = refs
        low = (mid[...] + (part[...].astype(FULL) + got[...].astype(FULL)) + b_down[...]).astype(LOW)
        in_ref[...] = low
        layer_in = low.astype(FULL)
    normed, _ = norm_rows(layer_in)
    a_one = (normed * gain[...] + bias[...]).astype(LOW)
    a_ref[...] = a_one
    own = dot_back(a_one, w_own[...]).astype(LOW)
    sib = dot_back(a_one, w_sib[...]).astype(LOW)
    w = own.shape[1] // 3
    q_own, k_own, v_own = own[:, :w], own[:, w : 2 * w], own[:, 2 * w :]
    q_sib, k_sib, v_sib = sib[:, :w], sib[:, w : 2 * w], sib[:, 2 * w :]
    q_ref[...] = jnp.concatenate([q_own, q_sib], axis=1) * jnp.asarray(SCALING, LOW)
    kv_ref[...] = jnp.concatenate([k_own, k_sib, v_own, v_sib], axis=1)
    send_ref[...] = jnp.concatenate([k_sib, k_own, v_sib, v_own], axis=1)


def project(source, gain, bias, w_own, w_sib, first):
    n, d = source[0].shape
    h = 2 * (w_own.shape[0] // 3)
    outs = [shape(n, d), shape(n, h), shape(n, 2 * h), shape(n, 2 * h)]
    if not first:
        outs = [shape(n, d)] + outs
    got = call(
        functools.partial(project_kernel, first),
        (*source, gain, bias, w_own, w_sib),
        outs,
        2 * n * d * 3 * h,
    )
    return got if not first else (source[0], *got)


def pair_masks(q_pair):
    lane = lax.broadcasted_iota(jnp.int32, q_pair.shape, 1)
    zero = jnp.zeros_like(q_pair)
    return jnp.where(lane < HEAD_DIM, q_pair, zero), jnp.where(lane < HEAD_DIM, zero, q_pair)


def attend_kernel(late, *refs):
    if late:
        outer, q_ref, sib_low, own_high, sib_high, own_low, bias_ref, wo_own, wo_sib, o_ref, lse_ref, part_ref, extra = refs

        @pl.when(outer[0] == 1)
        def _():
            extra[...] = sib_high[...]

        @pl.when(outer[0] == 0)
        def _():
            extra[...] = own_low[...]

        kv = jnp.concatenate([sib_low[...], own_high[...], extra[...]], axis=0)
    else:
        q_ref, own_low, sib_low, bias_ref, wo_own, wo_sib, o_ref, lse_ref, part_ref = refs
        kv = jnp.concatenate([own_low[...], sib_low[...]], axis=0)
    h = kv.shape[1] // 2
    keys, values = kv[:, :h], kv[:, h:]
    values_t = values.T
    outs, sums = [], []
    for pair in range(h // 128):
        lanes = slice(pair * 128, pair * 128 + 128)
        for j, q in enumerate(pair_masks(q_ref[:, lanes])):
            head = 2 * pair + j
            scores = dot_back(keys[:, lanes], q) + bias_ref[...]
            highest = jnp.max(scores, axis=0, keepdims=True)
            e = jnp.exp(scores - highest)
            total = jnp.sum(e, axis=0, keepdims=True)
            mixed = dot(values_t[head * HEAD_DIM : (head + 1) * HEAD_DIM], e.astype(LOW))
            outs.append(mixed * (1.0 / total))
            sums.append(highest + jnp.log(total))
    o = jnp.concatenate(outs, axis=0).T.astype(LOW)
    o_ref[...] = o
    lse_ref[...] = jnp.concatenate(sums + sums[: 8 - len(sums)], axis=0)
    half = wo_own.shape[0]
    part_ref[...] = (dot(o[:, :half], wo_own[...]) + dot(o[:, half:], wo_sib[...])).astype(LOW)


def attend(late, q, blocks, bias, wo_own, wo_sib, outer):
    n, h = q.shape
    d = wo_own.shape[1]
    operands = ((outer,) if late else ()) + (q, *blocks, bias, wo_own, wo_sib)
    return call(
        functools.partial(attend_kernel, late),
        operands,
        [shape(n, h), shape(8, n, dtype=FULL), shape(n, d)],
        2 * n * h * (4 * bias.shape[0] + d),
        scalars=1 if late else 0,
        scratch=[pltpu.VMEM((n, 2 * h), LOW)] if late else (),
    )


def gelu_parts(z):
    c = 0.7978845608028654
    square = z * z
    t = jnp.tanh(c * (z + 0.044715 * (square * z)))
    half = 0.5 * (1.0 + t)
    return z * half, half + 0.5 * z * (1.0 - t * t) * (c + (3.0 * 0.044715 * c) * square)


def feed_kernel(last, *refs):
    if last:
        (u, part, got, gain, bias, up_own, up_sib, b_own, b_sib, dn_own, dn_sib, grad_ref,
         mid_ref, a_ref, g_ref, dz_ref, back_ref, hidden_sum, row_sum) = refs
    else:
        (u, part, got, gain, bias, up_own, up_sib, b_own, b_sib, dn_own, dn_sib,
         mid_ref, a_ref, g_ref, slope_ref, out_ref) = refs
    mid = u[...].astype(FULL) + (part[...].astype(FULL) + got[...].astype(FULL))
    mid_ref[...] = mid
    normed, _ = norm_rows(mid)
    a_two = (normed * gain[...] + bias[...]).astype(LOW)
    a_ref[...] = a_two
    f = up_own.shape[1]
    step = 256
    total = jnp.zeros(mid.shape, FULL)
    for side, (up, b, dn) in enumerate(((up_own, b_own, dn_own), (up_sib, b_sib, dn_sib))):
        for at in range(0, f, step):
            cols = slice(at, at + step)
            here = slice(side * f + at, side * f + at + step)
            z = dot(a_two, up[:, cols]) + b[:, cols]
            g, slope = gelu_parts(z)
            g = g.astype(LOW)
            g_ref[:, here] = g
            if last:
                dz = (dot_back(grad_ref[...], dn[cols, :]) * slope).astype(LOW)
                dz_ref[:, here] = dz
                hidden_sum[:, here] = jnp.sum(dz.astype(FULL), axis=0, keepdims=True)
                total = total + dot_back(dz, up[:, cols])
            else:
                slope_ref[:, here] = slope.astype(LOW)
                total = total + dot(g, dn[cols, :])
    if last:
        back_ref[...] = total.astype(LOW)
        row_sum[...] = jnp.sum(grad_ref[...].astype(FULL), axis=0, keepdims=True)
    else:
        out_ref[...] = total.astype(LOW)


def feed(u, part, got, gain, bias, up, b_up, dn, grad=None):
    n, d = u.shape
    f = up[0].shape[1]
    last = grad is not None
    outs = [shape(n, d, dtype=FULL), shape(n, d), shape(n, 2 * f), shape(n, 2 * f), shape(n, d)]
    operands = (u, part, got, gain, bias, *up, *b_up, *dn) + ((grad,) if last else ())
    if last:
        outs += [shape(1, 2 * f, dtype=FULL), shape(1, d, dtype=FULL)]
    return call(functools.partial(feed_kernel, last), operands, outs, 2 * n * d * 2 * f * (3 if last else 2))


def feed_back_kernel(mid_grad, part, got, in_ref, gain, slope, up_own, up_sib, dn_own, dn_sib,
                     grad_ref, sums_ref, dz_ref, back_ref, hidden_sum):
    grad_norm = part[...].astype(FULL) + got[...].astype(FULL)
    normed, inverse = norm_rows(in_ref[...].astype(FULL))
    grad = (mid_grad[...] + norm_back(grad_norm, normed, inverse, gain[...])).astype(LOW)
    grad_ref[...] = grad
    sums_ref[...] = jnp.concatenate(
        [
            jnp.sum(grad_norm * normed, axis=0, keepdims=True),
            jnp.sum(grad_norm, axis=0, keepdims=True),
            jnp.sum(grad.astype(FULL), axis=0, keepdims=True),
        ],
        axis=0,
    )
    f = up_own.shape[1]
    step = 256
    total = jnp.zeros(grad.shape, FULL)
    for side, (up, dn) in enumerate(((up_own, dn_own), (up_sib, dn_sib))):
        for at in range(0, f, step):
            cols = slice(at, at + step)
            here = slice(side * f + at, side * f + at + step)
            dz = (dot_back(grad, dn[cols, :]) * slope[:, here].astype(FULL)).astype(LOW)
            dz_ref[:, here] = dz
            hidden_sum[:, here] = jnp.sum(dz.astype(FULL), axis=0, keepdims=True)
            total = total + dot_back(dz, up[:, cols])
    back_ref[...] = total.astype(LOW)


def feed_back(mid_grad, part, got, layer_in, gain, slope, up, dn):
    n, d = mid_grad.shape
    f = up[0].shape[1]
    outs = [shape(n, d), shape(3, d, dtype=FULL), shape(n, 2 * f), shape(n, d), shape(1, 2 * f, dtype=FULL)]
    return call(
        feed_back_kernel, (mid_grad, part, got, layer_in, gain, slope, *up, *dn), outs, 2 * n * d * 2 * f * 2
    )


def attend_back_kernel(outer, *refs):
    (mids, parts, gots, grads, gain, wo_own, wo_sib, qs, owns, sibs, biases, lses) = (
        refs[0:2], refs[2:4], refs[4:6], refs[6:8], refs[8], refs[9], refs[10], refs[11:13], refs[13:15],
        refs[15:17], refs[17:19], refs[19:21],
    )
    mid_grads, lows, sums_ref, dq_refs, keep_refs, send_refs = (
        refs[21:23], refs[23:25], refs[25], refs[26:28], refs[28:30], refs[30:32]
    )
    extra, acc_own, acc_sib = refs[32], refs[33:35], refs[35:37]
    n = mids[0].shape[0]
    outside = outer[0].astype(FULL)

    @pl.when(outer[0] == 1)
    def _():
        extra[...] = sibs[1][...]

    @pl.when(outer[0] == 0)
    def _():
        extra[...] = owns[0][...]

    sums = None
    for late in (0, 1):
        grad_norm = parts[late][...].astype(FULL) + gots[late][...].astype(FULL)
        normed, inverse = norm_rows(mids[late][...])
        mid_grad = grads[late][...].astype(FULL) + norm_back(grad_norm, normed, inverse, gain[...])
        mid_grads[late][...] = mid_grad
        low = mid_grad.astype(LOW)
        lows[late][...] = low
        now = jnp.concatenate(
            [jnp.sum(grad_norm * normed, axis=0, keepdims=True), jnp.sum(grad_norm, axis=0, keepdims=True)], axis=0
        )
        sums = now if sums is None else sums + now
        do = jnp.concatenate([dot_back(low, wo_own[...]), dot_back(low, wo_sib[...])], axis=1).astype(LOW)
        blocks = (sibs[0], owns[1], extra) if late else (owns[0], sibs[0])
        kv = jnp.concatenate([b[...] for b in blocks], axis=0)
        h = kv.shape[1] // 2
        keys, values = kv[:, :h], kv[:, h:]
        keys_t = keys.T
        dq = []
        for pair in range(h // 128):
            lanes = slice(pair * 128, pair * 128 + 128)
            dk = dv = None
            qs_two, do_two = pair_masks(qs[late][:, lanes]), pair_masks(do[:, lanes])
            for j in (0, 1):
                head = 2 * pair + j
                scores = dot_back(keys[:, lanes], qs_two[j]) + biases[late][...]
                p = jnp.exp(scores - lses[late][head : head + 1, :])
                dp = dot_back(values[:, lanes], do_two[j])
                inner = jnp.sum(p * dp, axis=0, keepdims=True)
                ds = (p * (dp - inner)).astype(LOW)
                dv_now = dot(p.astype(LOW), do_two[j])
                dk_now = dot(ds, qs_two[j])
                dk = dk_now if dk is None else dk + dk_now
                dv = dv_now if dv is None else dv + dv_now
                dq.append(dot(keys_t[head * HEAD_DIM : (head + 1) * HEAD_DIM], ds) * SCALING)
            high_lanes = slice(h + pair * 128, h + pair * 128 + 128)
            for value, where in ((dk, lanes), (dv, high_lanes)):
                if not late:
                    acc_own[0][:, where] = value[:n]
                    acc_sib[0][:, where] = value[n:]
                else:
                    acc_sib[0][:, where] += value[:n]
                    acc_own[1][:, where] = value[n : 2 * n]
                    acc_own[0][:, where] += value[2 * n :] * (1.0 - outside)
                    acc_sib[1][:, where] = value[2 * n :] * outside
        dq_refs[late][...] = jnp.concatenate(dq, axis=0).T.astype(LOW)
    sums_ref[...] = sums

    for i in (0, 1):
        keep_refs[i][...] = acc_own[i][...]
        send = acc_sib[i][...].astype(LOW)
        w = send.shape[1] // 4
        send_refs[i][...] = jnp.concatenate(
            [send[:, w : 2 * w], send[:, :w], send[:, 3 * w :], send[:, 2 * w : 3 * w]], axis=1
        )


def attend_back(outer, mids, parts, gots, grads, gain, wo, qs, owns, sibs, biases, lses):
    n, d = mids[0].shape
    h = qs[0].shape[1]
    two = lambda *dims, dtype=LOW: [shape(*dims, dtype=dtype)] * 2
    outs = (
        two(n, d, dtype=FULL) + two(n, d) + [shape(2, d, dtype=FULL)] + two(n, h) + two(n, 2 * h, dtype=FULL)
        + two(n, 2 * h)
    )
    got = call(
        attend_back_kernel,
        (outer, *mids, *parts, *gots, *grads, gain, *wo, *qs, *owns, *sibs, *biases, *lses),
        outs,
        2 * n * h * (10 * (biases[0].shape[0] + biases[1].shape[0]) + 2 * d),
        scalars=1,
        scratch=[pltpu.VMEM((n, 2 * h), LOW)] + [pltpu.VMEM((n, 2 * h), FULL)] * 4,
    )
    return got[0:2], got[2:4], got[4], got[5:7], got[7:9], got[9:11]


def project_back_kernel(dq, keep, got, w_own, w_sib, own_ref, sib_ref, part_ref):
    dkv = (keep[...] + got[...].astype(FULL)).astype(LOW)
    w = dkv.shape[1] // 4
    own = jnp.concatenate([dq[:, :w], dkv[:, :w], dkv[:, 2 * w : 3 * w]], axis=1)
    sib = jnp.concatenate([dq[:, w:], dkv[:, w : 2 * w], dkv[:, 3 * w :]], axis=1)
    own_ref[...] = own
    sib_ref[...] = sib
    part_ref[...] = (dot(own, w_own[...]) + dot(sib, w_sib[...])).astype(LOW)


def project_back(dq, keep, got, w_own, w_sib):
    n = dq.shape[0]
    w, d = w_own.shape
    outs = [shape(n, w), shape(n, w), shape(n, d)]
    return call(project_back_kernel, (dq, keep, got, w_own, w_sib), outs, 2 * n * d * 2 * w)


def body(
    inputs, cotangent, segments, ln1_gain, ln1_bias, w_query, w_key, w_value, w_out,
    ln2_gain, ln2_bias, w_up, b_up, w_down, b_down, *, n_batch,
):
    n = inputs.shape[1]
    section = lax.axis_index("section")
    tensor = lax.axis_index("tensor")
    on_first = section == 0
    early = tensor < 2
    outer = (tensor == 0) | (tensor == 3)
    outer_flag = outer.astype(jnp.int32).reshape(1)
    segment = jnp.where(on_first, segments[0, 0], segments[1, 0])

    def low_high(both):
        own = jnp.where(on_first, both[0], both[1])
        other = to_partner(own)
        return jnp.where(early, own, other), jnp.where(early, other, own)

    low_at = jnp.where(outer, 0, 1)
    block_at = {"own_low": low_at, "sib_low": 1 - low_at, "own_high": 3 - low_at, "sib_high": 2 + low_at}

    def block_bias(query, key_blocks):
        span = jnp.arange(n)
        query_at = block_at[query] * n + span
        query_seg = lax.dynamic_slice_in_dim(segment, block_at[query] * n, n)
        rows = []
        for key in key_blocks:
            key_at = key * n + span
            key_seg = lax.dynamic_slice_in_dim(segment, key * n, n)
            kept = (key_at[:, None] <= query_at[None, :]) & (key_seg[:, None] == query_seg[None, :])
            rows.append(jnp.where(kept, 0.0, MASKED).astype(FULL))
        return jnp.concatenate(rows, axis=0)

    bias_low = block_bias("own_low", [block_at["own_low"], block_at["sib_low"]])
    bias_high = block_bias(
        "own_high",
        [block_at["sib_low"], block_at["own_high"], jnp.where(outer, block_at["sib_high"], block_at["own_low"])],
    )
    biases = (bias_low, bias_high)

    rows_in = low_high(inputs)
    grad_last = low_high(cotangent)

    small_own = jnp.concatenate([ln1_gain, ln1_bias, ln2_gain, ln2_bias, b_down, b_up], axis=0)
    small_other = lax.ppermute(small_own, "section", SWAP)
    qkv_own = jnp.concatenate([w_query[0].T, w_key[0].T, w_value[0].T], axis=0)
    quarters_own = [qkv_own, w_out[0], w_up[0], w_down[0]]
    quarters_other = []
    after = None
    for quarter in quarters_own:
        if after is not None:
            quarter, _ = lax.optimization_barrier((quarter, after))
        after = lax.ppermute(quarter, "section", SWAP)
        quarters_other.append(after)

    def layer_weights(layer):
        here = section == layer
        quarters = [jnp.where(here, a, b) for a, b in zip(quarters_own, quarters_other)]
        pairs = [(q, to_sibling(q)) for q in quarters]
        small = jnp.where(here, small_own, small_other)
        rows = [small[i : i + 1] for i in range(6)]
        return rows[:5] + [(rows[5], to_sibling(rows[5]))], pairs

    small_0, weights_0 = layer_weights(0)
    small_1, weights_1 = layer_weights(1)

    def attention(projected, wo):
        lo, hi = projected
        sib = [to_sibling(p[4]) for p in projected]
        own = [p[3] for p in projected]
        o_lo = attend(False, lo[2], (own[0], sib[0]), biases[0], *wo, None)
        got_lo = to_partner(o_lo[2])
        o_hi = attend(True, hi[2], (sib[0], own[1], sib[1], own[0]), biases[1], *wo, outer_flag)
        got_hi = to_partner(o_hi[2])
        return (o_lo, o_hi), (got_lo, got_hi), own, sib

    qkv, wo, up, dn = weights_0
    proj_0 = [project((rows_in[i],), small_0[0], small_0[1], *qkv, True) for i in (0, 1)]
    att_0, got, own_0, sib_0 = attention(proj_0, wo)
    feed_0, feed_got = [], []
    for i in (0, 1):
        feed_0.append(feed(proj_0[i][0], att_0[i][2], got[i], small_0[2], small_0[3], up, small_0[5], dn))
        feed_got.append(to_partner(feed_0[i][4]))

    qkv, wo, up, dn = weights_1
    proj_1 = [
        project((feed_0[i][0], feed_0[i][4], feed_got[i], small_0[4]), small_1[0], small_1[1], *qkv, False)
        for i in (0, 1)
    ]
    att_1, got, own_1, sib_1 = attention(proj_1, wo)
    feed_1, back_got = [], []
    for i in (0, 1):
        feed_1.append(
            feed(proj_1[i][0], att_1[i][2], got[i], small_1[2], small_1[3], up, small_1[5], dn, grad_last[i])
        )
        back_got.append(to_partner(feed_1[i][4]))

    half = up[0].shape[1]

    def join(two):
        return jnp.concatenate(two, axis=0)

    def grads_feed(g, grads, a_two, dz):
        g, grads, a_two, dz = map(join, (g, grads, a_two, dz))
        return [
            (dot_rows(a_two, dz[:, i : i + half]).astype(LOW), dot_rows(g[:, i : i + half], grads).astype(LOW))
            for i in (0, half)
        ]

    def grads_attend(o, lows, a_one, d_own, d_sib):
        o, lows, a_one = map(join, (o, lows, a_one))
        w = o.shape[1] // 2
        return [
            (dot_rows(join(d), a_one).astype(LOW), dot_rows(o[:, i : i + w], lows).astype(LOW))
            for i, d in ((0, d_own), (w, d_sib))
        ]

    def attention_back(mids, parts, gots, grads, gain, wo, projected, own, sib, att, qkv):
        mid_grads, lows, sums, dq, keep, send = attend_back(
            outer_flag, mids, parts, gots, grads, gain, wo, [p[2] for p in projected], own, sib, biases,
            [a[1] for a in att],
        )
        back = [project_back(dq[i], keep[i], to_sibling(send[i]), *qkv) for i in (0, 1)]
        return mid_grads, lows, sums, back

    mids = [f[0] for f in feed_1]
    mid_grads_1, lows_1, sums_two_1, back_1 = attention_back(
        mids, [f[4] for f in feed_1], back_got, grad_last, small_1[2], wo, proj_1, own_1, sib_1, att_1, qkv
    )
    part_got = [to_partner(b[2]) for b in back_1]
    by_feed_1 = grads_feed([f[2] for f in feed_1], grad_last, [f[1] for f in feed_1], [f[3] for f in feed_1])
    by_att_1 = grads_attend(
        [a[0] for a in att_1], lows_1, [p[1] for p in proj_1], [b[0] for b in back_1], [b[1] for b in back_1]
    )

    gain_one_1 = small_1[0]
    qkv, wo, up, dn = weights_0
    fb_0, back_got = [], []
    for i in (0, 1):
        fb_0.append(
            feed_back(mid_grads_1[i], back_1[i][2], part_got[i], proj_1[i][0], gain_one_1, feed_0[i][3], up, dn)
        )
        back_got.append(to_partner(fb_0[i][3]))
    grad_mid = [f[0] for f in fb_0]
    mid_grads_0, lows_0, sums_two_0, back_0 = attention_back(
        [f[0] for f in feed_0], [f[3] for f in fb_0], back_got, grad_mid, small_0[2], wo, proj_0, own_0, sib_0,
        att_0, qkv,
    )
    by_feed_0 = grads_feed([f[2] for f in feed_0], grad_mid, [f[1] for f in feed_0], [f[2] for f in fb_0])
    by_att_0 = grads_attend(
        [a[0] for a in att_0], lows_0, [p[1] for p in proj_0], [b[0] for b in back_0], [b[1] for b in back_0]
    )
    part_got = [to_partner(b[2]) for b in back_0]
    last, sums_one_0 = [], 0.0
    for i in (0, 1):
        grad_norm = back_0[i][2].astype(FULL) + part_got[i].astype(FULL)
        normed, inverse = norm_rows(rows_in[i].astype(FULL))
        last.append((mid_grads_0[i] + norm_back(grad_norm, normed, inverse, small_0[0])).astype(LOW))
        sums_one_0 += jnp.stack([jnp.sum(grad_norm * normed, axis=0), jnp.sum(grad_norm, axis=0)])
    sums_one_1 = fb_0[0][1] + fb_0[1][1]

    outs_1 = []
    for i in (0, 1):
        part = (dot(feed_1[i][2][:, :half], weights_1[3][0]) + dot(feed_1[i][2][:, half:], weights_1[3][1])).astype(LOW)
        total = part.astype(FULL) + to_partner(part).astype(FULL)
        outs_1.append((feed_1[i][0] + total + small_1[4]).astype(LOW))

    def ready(first, second):
        first, second = [own.astype(FULL) + to_sibling(sib).astype(FULL) for own, sib in (first, second)]
        return jnp.where(on_first, first, second).astype(LOW), jnp.where(on_first, second, first).astype(LOW)

    def side(both, kind):
        return tuple(part[kind] for part in both)

    w_rows = by_att_0[0][1].shape[0]
    f_rows = half // 2
    feed_parts = [ready(side(by_feed_0, kind), side(by_feed_1, kind)) for kind in (1, 0)]
    att_parts = [ready(side(by_att_0, kind), side(by_att_1, kind)) for kind in (1, 0)]
    cuts = [(part, k * f_rows, f_rows) for part in feed_parts for k in (0, 1)]
    cuts += [(att_parts[0], 0, w_rows)] + [(att_parts[1], k * w_rows, w_rows) for k in range(3)]
    pieces = [tuple(x[at : at + size] for x in part) for part, at, size in cuts]
    crossed = [lax.ppermute(theirs, "section", SWAP) for _, theirs in pieces]

    sums_two = [sums_two_0, sums_two_1]
    last_rows = [fb_0[0][1][2:] + fb_0[1][1][2:], feed_1[0][6] + feed_1[1][6]]
    sums_one = [sums_one_0, fb_0[0][1][:2] + fb_0[1][1][:2]]
    hidden = [fb_0[0][4] + fb_0[1][4], feed_1[0][5] + feed_1[1][5]]
    rows = join([join([a, b, c]) for a, b, c in zip(sums_one, sums_two, last_rows)])
    count = rows.shape[0]
    hidden_own = join([x[:, :half] for x in hidden])
    hidden_sib = join([x[:, half:] for x in hidden])
    five = count // 2

    def to_both(values):
        got = to_sibling(join([values, hidden_sib]))
        return values + got[:count], hidden_own + got[count:]

    def to_all(both):
        values = (both[0] + to_partner(both[0])) * 0.5
        a = join([values[:five], both[1][:1]])
        b = join([values[five:], both[1][1:]])
        return jnp.where(on_first, a, b) + lax.ppermute(jnp.where(on_first, b, a), "section", SWAP)

    def doubled(distance):
        return lambda x: x + lax.ppermute(x, "batch", [(i, i ^ distance) for i in range(n_batch)])

    small_steps = [to_both, to_all]
    if n_batch & (n_batch - 1):
        small_steps.append(lambda x: lax.psum(x, "batch"))
    else:
        distance = 1
        while distance < n_batch:
            small_steps.append(doubled(distance))
            distance *= 2

    if n_batch == 4:
        batch = lax.axis_index("batch")
        middle = (batch == 1) | (batch == 2)
        stage = [None] * len(pieces)
        latest = rows

        def added(left, right):
            left, right, _ = lax.optimization_barrier((left, right, latest))
            return left + right

        small = rows
        for turn in range(len(pieces) + 3):
            if turn < len(pieces):
                k = turn
                latest = added(pieces[k][0], crossed[k])
                stage[k] = (latest, lax.ppermute(latest, "batch", [(0, 1), (3, 2)]))
            if 0 <= turn - 1 < len(pieces):
                k = turn - 1
                latest = added(*stage[k])
                stage[k] = (latest, lax.ppermute(latest, "batch", [(1, 2), (2, 1)]))
            if 0 <= turn - 2 < len(pieces):
                k = turn - 2
                latest = added(*stage[k])
                stage[k] = (latest, lax.ppermute(latest, "batch", [(1, 0), (2, 3)]))
            if 0 <= turn - 3 < len(pieces):
                k = turn - 3
                low, got, _ = lax.optimization_barrier((*stage[k], latest))
                stage[k] = jnp.where(middle, low, got).astype(FULL)
            if turn >= 6 and small_steps:
                small = small_steps.pop(0)(small)
    else:
        small = rows
        stage = [lax.psum(mine + got, "batch").astype(FULL) for (mine, _), got in zip(pieces, crossed)]
    for step in small_steps:
        small = step(small)
    sums = small
    total_feed = [join(stage[2:4]), join(stage[0:2])]
    total_out = stage[4]
    total_qkv = [x.T[None] for x in stage[5:8]]

    def both_micro(first, second):
        first, second = jnp.where(early, *first), jnp.where(early, *second)
        mine = jnp.where(on_first, first, second)
        theirs = lax.ppermute(jnp.where(on_first, second, first), "section", SWAP)
        return jnp.stack([jnp.where(on_first, mine, theirs), jnp.where(on_first, theirs, mine)])[None]

    forward_out = both_micro([p[0] for p in proj_1], outs_1)
    backward_out = both_micro(last, [f[0] for f in fb_0])
    return (
        forward_out,
        backward_out,
        sums[0:1],
        sums[1:2],
        *total_qkv,
        total_out[None],
        sums[2:3],
        sums[3:4],
        total_feed[0][None],
        sums[5:6],
        total_feed[1][None],
        sums[4:5],
    )


def solution(mesh):
    rows = P(None, ("batch", "tensor"), None)
    layer = P("section", None)
    by_column = P("section", None, "tensor")
    by_row = P("section", "tensor", None)
    kept = P("section", None, ("batch", "tensor"), None)
    return jax.shard_map(
        functools.partial(body, n_batch=mesh.shape["batch"]),
        mesh=mesh,
        in_specs=(
            rows, rows, P(None, "batch", None), layer, layer, by_column, by_column, by_column, by_row,
            layer, layer, by_column, P("section", "tensor"), by_row, layer,
        ),
        out_specs=(
            kept, kept, layer, layer, by_column, by_column, by_column, by_row,
            layer, layer, by_column, P("section", "tensor"), by_row, layer,
        ),
        check_vma=False,
    )
```

time: 657 us -> 486 us (0.74)
  Pallas kernels: 0 us -> 78.3 us
  waiting for transfers between devices: 278 us -> 208 us
  other arithmetic: 106 us -> 41.8 us
  starting transfers between devices: 32.5 us -> 92.9 us
  blocking collectives: 60.3 us -> 0 us
  matrix products: 86 us -> 31.9 us
  local copies, waits for them, and re-layouts: 70 us -> 22.2 us
  between operations: 16.8 us -> 2.92 us
    pallas_call x0 -> x20, Pallas kernels: none -> 78.3 us  [call(): pl.pallas_call(kernel, out_shape=tuple(outs), in_specs=specs, out_specs=t...]
    psum x2 -> x0, blocking collectives: 60.3 us -> none  [the longest x1 47.8 us: body(): lax.psum(jnp.stack([sums_0, sums_1]), ('section', 'batch', 'tensor')) * 0.5]
    psum x1 -> x0, waiting for transfers between devices: 58.6 us -> none  [body(): totals.append(lax.psum(total, 'batch').astype(FULL))]
    dot_general x32 -> x0, matrix products: 57.7 us -> none  [the longest x8 20.4 us: dot_back(): lax.dot_general(left, right, (((1,), (1,)), ((), ())), preferred_element_...]
    ppermute x9 -> x39, starting transfers between devices: 8.63 us -> 63.7 us  [the longest x8 27.1 us: body(): stage[k] = (latest, lax.ppermute(latest, 'batch', [(0, 1), (3, 2)]))]
    convert_element_type x20 -> x3, other arithmetic: 33 us -> 6.67 us  [ready(): jnp.where(on_first, second, first).astype(LOW)]
    ppermute x10 -> x19, waiting for transfers between devices: 97.3 us -> 71.1 us  [to_partner(): return lax.ppermute(value, 'tensor', PARTNER)]
    ppermute x9 -> x39, waiting for transfers between devices: 121 us -> 137 us  [the longest x4 62.5 us: body(): after = lax.ppermute(quarter, 'section', SWAP)]
  transfers between devices with their start and end apart: 47 -> 88, of which waited for: 19 -> 32; matrix products, arithmetic and copies ran while one was open for 36% -> 15% of each run, Pallas kernels for 0% -> 15%
where the time goes in v2:
time: 486 us; the launch traced here: 478 us
  waiting for transfers between devices  208 us (43%)
  starting transfers between devices  92.9 us (19%)
  Pallas kernels  78.3 us (16%)
  other arithmetic  41.8 us (9%)
  matrix products  31.9 us (7%)
  local copies, waits for them, and re-layouts  22.2 us (5%)
    pallas_call x20, Pallas kernels, call(): pl.pallas_call(kernel, out_shape=tuple(outs), in_specs=specs, out_specs=t...  78.3 us
    ppermute x19, waiting for transfers between devices, to_partner(): return lax.ppermute(value, 'tensor', PARTNER)  71.1 us
    ppermute x4, waiting for transfers between devices, body(): after = lax.ppermute(quarter, 'section', SWAP)  62.5 us
    ppermute x8, waiting for transfers between devices, body(): stage[k] = (latest, lax.ppermute(latest, 'batch', [(1, 0), (2, 3)]))  34 us
    ppermute x8, starting transfers between devices, body(): stage[k] = (latest, lax.ppermute(latest, 'batch', [(0, 1), (3, 2)]))  27.1 us
    dot_general x16, matrix products, dot_rows(): lax.dot_general(left, right, (((0,), (0,)), ((), ())), preferred_element_...  25 us
    ppermute x8, waiting for transfers between devices, body(): crossed = [lax.ppermute(theirs, 'section', SWAP) for _, theirs in pieces]  18.5 us
    ppermute x19, starting transfers between devices, to_partner(): return lax.ppermute(value, 'tensor', PARTNER)  16.3 us
  transfers between devices with their start and end apart: 88, of which 32 were waited for; matrix products, arithmetic and copies ran while one was open for 15% of the time, Pallas kernels for 15%

profile of v2, /device:TPU:0, one launch (start us, length us, event | category | flops | bytes accessed | tf_op | source)
XLA Modules:
  0.0 478.4 jit_solution(14474945325126151219)
XLA Ops:
  8.6 16.5 %collective-permute-done.2 = bf16[576,768]{1,0:T(8,128)(2,1)} collective-permute-done((bf16[576,768]{1,0:T(8,128)(2,1)S(1)}, bf16[576,768]{1,0:T(8,128)(2,1)}, u32[]{:S(2)}, u32[]{:S(2)}) %collective-permute-start.2) | collective-permute-done | bytes 884768 | tf_op jit(solution)/shard_map/ppermute | solution.py:429
  27.2 6.0 %collective-permute-done.5 = bf16[192,768]{1,0:T(8,128)(2,1)S(1)} collective-permute-done((bf16[192,768]{1,0:T(8,128)(2,1)}, bf16[192,768]{1,0:T(8,128)(2,1)S(1)}, u32[]{:S(2)}, u32[]{:S(2)}) %collective-permute-start.5) | collective-permute-done | bytes 294944 | tf_op jit(solution)/shard_map/ppermute | solution.py:429
  36.3 23.2 %collective-permute-done.8 = bf16[768,768]{1,0:T(8,128)(2,1)} collective-permute-done((bf16[768,768]{1,0:T(8,128)(2,1)}, bf16[768,768]{1,0:T(8,128)(2,1)}, u32[]{:S(2)}, u32[]{:S(2)}) %collective-permute-start.8) | collective-permute-done | bytes 1179680 | tf_op jit(solution)/shard_map/ppermute | solution.py:429
  67.9 16.9 %collective-permute-done.11 = bf16[768,768]{1,0:T(8,128)(2,1)S(1)} collective-permute-done((bf16[768,768]{1,0:T(8,128)(2,1)}, bf16[768,768]{1,0:T(8,128)(2,1)S(1)}, u32[]{:S(2)}, u32[]{:S(2)}) %collective-permute-start.11) | collective-permute-done | bytes 1179680 | tf_op jit(solution)/shard_map/ppermute | solution.py:429
  106.0 4.9 %shard_map.256 = (f32[256,768]{1,0:T(8,128)S(1)}, bf16[256,768]{1,0:T(8,128)(2,1)S(1)}, bf16[256,1536]{1,0:T(8,128)(2,1)S(1)}, bf16[256,1536]{1,0:T(8,128)(2,1)S(1)}, bf16[256,768]{1,0:T(8,128)(2,1)S(1)}) custom-call(bf16[256,768]{1,0:T(8,128)(2,1)S(1)} %get-tuple-element.395.refs_0_, bf16[256,768]{1,0:T(8,128)(2,1)S(1)} %get-tuple-element.183.refs_1_, ...), custom_call_target="tpu_custom_call" | custom-call | flops 1207959552 | bytes 9056256 | tf_op jit(solution)/shard_map/pallas_call | solution.py:60
  114.6 4.9 %shard_map.260 = (f32[256,768]{1,0:T(8,128)S(1)}, bf16[256,768]{1,0:T(8,128)(2,1)S(1)}, bf16[256,1536]{1,0:T(8,128)(2,1)S(1)}, bf16[256,1536]{1,0:T(8,128)(2,1)S(1)}, bf16[256,768]{1,0:T(8,128)(2,1)S(1)}) custom-call(bf16[256,768]{1,0:T(8,128)(2,1)S(1)} %get-tuple-element.358.refs_0_, bf16[256,768]{1,0:T(8,128)(2,1)S(1)} %get-tuple-element.192.refs_1_, ...), custom_call_target="tpu_custom_call" | custom-call | flops 1207959552 | bytes 9056256 | tf_op jit(solution)/shard_map/pallas_call | solution.py:60
  127.7 5.0 %collective-permute-done.17.refs_2_ = bf16[256,768]{1,0:T(8,128)(2,1)S(1)} collective-permute-done((bf16[256,768]{1,0:T(8,128)(2,1)S(1)}, bf16[256,768]{1,0:T(8,128)(2,1)S(1)}, u32[]{:S(2)}, u32[]{:S(2)}) %collective-permute-start.17) | collective-permute-done | bytes 393248 | tf_op jit(solution)/shard_map/ppermute | solution.py:49
  150.0 5.7 %shard_map.263 = (f32[256,768]{1,0:T(8,128)S(1)}, bf16[256,768]{1,0:T(8,128)(2,1)S(1)}, bf16[256,1536]{1,0:T(8,128)(2,1)S(1)}, bf16[256,1536]{1,0:T(8,128)(2,1)S...) custom-call(bf16[256,768]{1,0:T(8,128)(2,1)S(1)} %get-tuple-element.188.refs_0_.in_ref, ...), custom_call_target="tpu_custom_call" | custom-call | flops 1811939328 | bytes 9458688 | tf_op jit(solution)/shard_map/pallas_call | solution.py:60
  158.4 5.7 %shard_map.265 = (f32[256,768]{1,0:T(8,128)S(1)}, bf16[256,768]{1,0:T(8,128)(2,1)S(1)}, bf16[256,1536]{1,0:T(8,128)(2,1)S(1)}, bf16[256,1536]{1,0:T(8,128)(2,1)S...) custom-call(bf16[256,768]{1,0:T(8,128)(2,1)S(1)} %get-tuple-element.195.refs_0_.in_ref, ...), custom_call_target="tpu_custom_call" | custom-call | flops 1811939328 | bytes 9458688 | tf_op jit(solution)/shard_map/pallas_call | solution.py:60
  187.0 7.4 %collective-permute-done.25 = bf16[256,768]{1,0:T(8,128)(2,1)S(1)} collective-permute-done((bf16[256,768]{1,0:T(8,128)(2,1)S(1)}, bf16[256,768]{1,0:T(8,128)(2,1)S(1)}, u32[]{:S(2)}, u32[]{:S(2)}) %collective-permute-start.25) | collective-permute-done | bytes 393248 | tf_op jit(solution)/shard_map/ppermute | solution.py:49
  196.8 6.0 %collective-permute-done.30.refs_4_ = bf16[256,768]{1,0:T(8,128)(2,1)S(1)} collective-permute-done((bf16[256,768]{1,0:T(8,128)(2,1)S(1)}, bf16[256,768]{1,0:T(8,128)(2,1)S(1)}, u32[]{:S(2)}, u32[]{:S(2)}) %collective-permute-start.30) | collective-permute-done | bytes 393248 | tf_op jit(solution)/shard_map/ppermute | solution.py:49
  202.8 8.4 %collective-permute-done.31.refs_5_ = bf16[256,768]{1,0:T(8,128)(2,1)S(1)} collective-permute-done((bf16[256,768]{1,0:T(8,128)(2,1)S(1)}, bf16[256,768]{1,0:T(8,128)(2,1)S(1)}, u32[]{:S(2)}, u32[]{:S(2)}) %collective-permute-start.31) | collective-permute-done | bytes 393248 | tf_op jit(solution)/shard_map/ppermute | solution.py:49
  211.3 12.1 %shard_map.266 = (f32[256,768]{1,0:T(8,128)}, f32[256,768]{1,0:T(8,128)}, bf16[256,768]{1,0:T(8,128)(2,1)S(1)}, bf16[256,768]{1,0:T(8,128)(2,1)S(1)}, f32[2,768]...) custom-call(s32[1]{0:T(128)} %bitcast.12.refs_0_.outer, ...), custom_call_target="tpu_custom_call" | custom-call | flops 2818572288 | bytes 12936196 | tf_op jit(solution)/shard_map/pallas_call | solution.py:60
  237.9 5.1 %shard_map.268 = (bf16[256,768]{1,0:T(8,128)(2,1)S(1)}, f32[3,768]{1,0:T(4,128)S(1)}, bf16[256,1536]{1,0:T(8,128)(2,1)S(1)}, bf16[256,768]{1,0:T(8,128)(2,1)S(1)}, f32[1,1536]{1,0:T(1,128)S(1)}) custom-call(f32[256,768]{1,0:T(8,128)S(1)} %copy-done.15, bf16[256,768]{1,0:T(8,128)(2,1)S(1)} %get-tuple-element.216.part, ...), custom_call_target="tpu_custom_call" | custom-call | flops 1207959552 | bytes 9062400 | tf_op jit(solution)/shard_map/pallas_call | solution.py:60
  246.3 4.7 shard_map.270
  259.4 6.6 %collective-permute-done.36.refs_4_ = bf16[256,768]{1,0:T(8,128)(2,1)S(1)} collective-permute-done((bf16[256,768]{1,0:T(8,128)(2,1)S(1)}, bf16[256,768]{1,0:T(8,128)(2,1)S(1)}, u32[]{:S(2)}, u32[]{:S(2)}) %collective-permute-start.36) | collective-permute-done | bytes 393248 | tf_op jit(solution)/shard_map/ppermute | solution.py:49
  266.0 8.4 %collective-permute-done.37.refs_5_ = bf16[256,768]{1,0:T(8,128)(2,1)S(1)} collective-permute-done((bf16[256,768]{1,0:T(8,128)(2,1)S(1)}, bf16[256,768]{1,0:T(8,128)(2,1)S(1)}, u32[]{:S(2)}, u32[]{:S(2)}) %collective-permute-start.37) | collective-permute-done | bytes 393248 | tf_op jit(solution)/shard_map/ppermute | solution.py:49
  274.4 12.2 %shard_map.271 = (f32[256,768]{1,0:T(8,128)}, f32[256,768]{1,0:T(8,128)}, bf16[256,768]{1,0:T(8,128)(2,1)S(1)}, bf16[256,768]{1,0:T(8,128)(2,1)S(1)}, f32[2,768]...) custom-call(s32[1]{0:T(128)} %bitcast.12.refs_0_.outer, ...), custom_call_target="tpu_custom_call" | custom-call | flops 2818572288 | bytes 12936196 | tf_op jit(solution)/shard_map/pallas_call | solution.py:60
  310.1 8.4 %collective-permute-done.41 = bf16[256,768]{1,0:T(8,128)(2,1)S(1)} collective-permute-done((bf16[256,768]{1,0:T(8,128)(2,1)S(1)}, bf16[256,768]{1,0:T(8,128)(2,1)S(1)}, u32[]{:S(2)}, u32[]{:S(2)}) %collective-permute-start.41) | collective-permute-done | bytes 393248 | tf_op jit(solution)/shard_map/ppermute | solution.py:49
  330.0 10.5 %collective-permute-done.56 = bf16[384,768]{1,0:T(8,128)(2,1)} collective-permute-done((bf16[384,768]{1,0:T(8,128)(2,1)}, bf16[384,768]{1,0:T(8,128)(2,1)}, u32[]{:S(2)}, u32[]{:S(2)}) %collective-permute-start.56) | collective-permute-done | bytes 589856 | tf_op jit(solution)/shard_map/ppermute | solution.py:558
  346.6 6.1 %collective-permute-done.45 = f32[6,768]{1,0:T(8,128)S(1)} collective-permute-done((f32[6,768]{1,0:T(8,128)S(1)}, f32[6,768]{1,0:T(8,128)S(1)}, u32[]{:S(2)}, u32[]{:S(2)}) %collective-permute-start.45) | collective-permute-done | bytes 18464 | tf_op jit(solution)/shard_map/ppermute | solution.py:578
  363.8 6.5 %collective-permute-done.62 = bf16[384,768]{1,0:T(8,128)(2,1)S(1)} collective-permute-done((bf16[384,768]{1,0:T(8,128)(2,1)S(1)}, bf16[384,768]{1,0:T(8,128)(2,1)S(1)}, u32[]{:S(2)}, u32[]{:S(2)}) %collective-permute-start.62) | collective-permute-done | bytes 589856 | tf_op jit(solution)/shard_map/ppermute | solution.py:607
  414.3 7.8 %collective-permute-done.87 = bf16[384,768]{1,0:T(8,128)(2,1)S(1)} collective-permute-done((bf16[384,768]{1,0:T(8,128)(2,1)S(1)}, bf16[384,768]{1,0:T(8,128)(2,1)S(1)}, u32[]{:S(2)}, u32[]{:S(2)}) %collective-permute-start.87) | collective-permute-done | bytes 589856 | tf_op jit(solution)/shard_map/ppermute | solution.py:615
  451.1 16.7 %collective-permute-done.77 = bf16[192,768]{1,0:T(8,128)(2,1)S(1)} collective-permute-done((bf16[192,768]{1,0:T(8,128)(2,1)S(1)}, bf16[192,768]{1,0:T(8,128)(2,1)S(1)}, u32[]{:S(2)}, u32[]{:S(2)}) %collective-permute-start.77) | collective-permute-done | bytes 294944 | tf_op jit(solution)/shard_map/ppermute | solution.py:615
  (539 shorter events, 259.7 us)
Async XLA Ops:
  2.0 23.0 %collective-permute-start.2 = (bf16[576,768]{1,0:T(8,128)(2,1)S(1)}, bf16[576,768]{1,0:T(8,128)(2,1)}, u32[]{:S(2)}, u32[]{:S(2)}) collective-permute-start(bf16[576,768]{1,0:T(8,128)(2,1)S(1)} %pad_maximum_fusion), channel_id=1, source_target_pairs={{0,16},{16,0},{1,17},{17,1},{2,18},{18,2},{3,19},{19,3},{4,20},{20... | collective-permute-start | bytes 2654216 | tf_op jit(solution)/shard_map/ppermute | solution.py:429
  5.8 29.0 %collective-permute-start = (bf16[256,768]{1,0:T(8,128)(2,1)}, bf16[256,768]{1,0:T(8,128)(2,1)}, u32[]{:S(2)}, u32[]{:S(2)}) collective-permute-start(bf16[256,768]{1,0:T(8,128)(2,1)} %select_bitcast_fusion.5), channel_id=1, source_target_pairs={{0,3},{3,0},{1,2},{2,1},{4,7},{7,4},{5,6},{6,5},{8,11},{11,8},{9,1... | collective-permute-start | bytes 1179656 | tf_op jit(solution)/shard_map/ppermute | solution.py:49
  6.6 28.1 %collective-permute-start.1 = (f32[6,768]{1,0:T(8,128)S(1)}, f32[6,768]{1,0:T(8,128)S(1)}, u32[]{:S(2)}, u32[]{:S(2)}) collective-permute-start(f32[6,768]{1,0:T(8,128)S(1)} %concatenate.90), channel_id=1, source_target_pairs={{0,16},{16,0},{1,17},{17,1},{2,18},{18,2},{3,19},{19,3},{4,20},{20... | collective-permute-start | bytes 55304 | tf_op jit(solution)/shard_map/ppermute | solution.py:421
  8.0 53.2 %collective-permute-start.24 = (bf16[256,768]{1,0:T(8,128)(2,1)}, bf16[256,768]{1,0:T(8,128)(2,1)S(1)}, u32[]{:S(2)}, u32[]{:S(2)}) collective-permute-start(bf16[256,768]{1,0:T(8,128)(2,1)} %select_bitcast_fusion.4), channel_id=1, source_target_pairs={{0,3},{3,0},{1,2},{2,1},{4,7},{7,4},{5,6},{6,5},{8,11},{11,8},{9,1... | collective-permute-start | bytes 1179656 | tf_op jit(solution)/shard_map/ppermute | solution.py:49
  33.2 26.3 %collective-permute-start.8 = (bf16[768,768]{1,0:T(8,128)(2,1)}, bf16[768,768]{1,0:T(8,128)(2,1)}, u32[]{:S(2)}, u32[]{:S(2)}) collective-permute-start(bf16[768,768]{1,0:T(8,128)(2,1)} %bitcast.86), channel_id=1, source_target_pairs={{0,16},{16,0},{1,17},{17,1},{2,18},{18,2},{3,19},{19,3},{4,20},{20... | collective-permute-start | bytes 3538952 | tf_op jit(solution)/shard_map/ppermute | solution.py:429
  59.5 25.3 %collective-permute-start.11 = (bf16[768,768]{1,0:T(8,128)(2,1)}, bf16[768,768]{1,0:T(8,128)(2,1)S(1)}, u32[]{:S(2)}, u32[]{:S(2)}) collective-permute-start(bf16[768,768]{1,0:T(8,128)(2,1)} %bitcast.87), channel_id=1, source_target_pairs={{0,16},{16,0},{1,17},{17,1},{2,18},{18,2},{3,19},{19,3},{4,20},{20... | collective-permute-start | bytes 3538952 | tf_op jit(solution)/shard_map/ppermute | solution.py:429
  67.5 38.5 %collective-permute-start.9 = (bf16[768,768]{1,0:T(8,128)(2,1)S(1)}, bf16[768,768]{1,0:T(8,128)(2,1)}, u32[]{:S(2)}, u32[]{:S(2)}) collective-permute-start(bf16[768,768]{1,0:T(8,128)(2,1)S(1)} %get-tuple-element.371.refs_5_.up_own), channel_id=1, source_target_pairs={{0,1},{1,0},{2,3},{3,2},{4,5},{5,4},{6,7},{7,6},{8,9},{9,8},{10,11... | collective-permute-start | bytes 3538952 | tf_op jit(solution)/shard_map/ppermute | solution.py:53
  104.7 41.4 %collective-permute-start.21 = (bf16[768,768]{1,0:T(8,128)(2,1)}, bf16[768,768]{1,0:T(8,128)(2,1)}, u32[]{:S(2)}, u32[]{:S(2)}) collective-permute-start(bf16[768,768]{1,0:T(8,128)(2,1)} %get-tuple-element.370.refs_5_), channel_id=1, source_target_pairs={{0,1},{1,0},{2,3},{3,2},{4,5},{5,4},{6,7},{7,6},{8,9},{9,8},{10,11... | collective-permute-start | bytes 3538952 | tf_op jit(solution)/shard_map/ppermute | solution.py:53
  106.0 40.1 %collective-permute-start.23 = (bf16[768,768]{1,0:T(8,128)(2,1)}, bf16[768,768]{1,0:T(8,128)(2,1)}, u32[]{:S(2)}, u32[]{:S(2)}) collective-permute-start(bf16[768,768]{1,0:T(8,128)(2,1)} %get-tuple-element.368.refs_9_), channel_id=1, source_target_pairs={{0,1},{1,0},{2,3},{3,2},{4,5},{5,4},{6,7},{7,6},{8,9},{9,8},{10,11... | collective-permute-start | bytes 3538952 | tf_op jit(solution)/shard_map/ppermute | solution.py:53
  180.4 22.4 %collective-permute-start.30 = (bf16[256,768]{1,0:T(8,128)(2,1)S(1)}, bf16[256,768]{1,0:T(8,128)(2,1)S(1)}, u32[]{:S(2)}, u32[]{:S(2)}) collective-permute-start(bf16[256,768]{1,0:T(8,128)(2,1)S(1)} %get-tuple-element.208.refs_2_), channel_id=1, source_target_pairs={{0,3},{3,0},{1,2},{2,1},{4,7},{7,4},{5,6},{6,5},{8,11},{11,8},{9,1... | collective-permute-start | bytes 1179656 | tf_op jit(solution)/shard_map/ppermute | solution.py:49
  181.4 29.8 %collective-permute-start.31 = (bf16[256,768]{1,0:T(8,128)(2,1)S(1)}, bf16[256,768]{1,0:T(8,128)(2,1)S(1)}, u32[]{:S(2)}, u32[]{:S(2)}) collective-permute-start(bf16[256,768]{1,0:T(8,128)(2,1)S(1)} %get-tuple-element.209.refs_3_), channel_id=1, source_target_pairs={{0,3},{3,0},{1,2},{2,1},{4,7},{7,4},{5,6},{6,5},{8,11},{11,8},{9,1... | collective-permute-start | bytes 1179656 | tf_op jit(solution)/shard_map/ppermute | solution.py:49
  186.6 112.5 %collective-permute-start.52 = (bf16[768,768]{1,0:T(8,128)(2,1)}, bf16[768,768]{1,0:T(8,128)(2,1)}, u32[]{:S(2)}, u32[]{:S(2)}) collective-permute-start(bf16[768,768]{1,0:T(8,128)(2,1)} %convolution_convert_fusion.4), channel_id=1, source_target_pairs={{0,1},{1,0},{2,3},{3,2},{4,5},{5,4},{6,7},{7,6},{8,9},{9,8},{10,11... | collective-permute-start | bytes 3538952 | tf_op jit(solution)/shard_map/ppermute | solution.py:53
  195.8 35.3 %collective-permute-start.29 = (bf16[256,768]{1,0:T(8,128)(2,1)}, bf16[256,768]{1,0:T(8,128)(2,1)S(1)}, u32[]{:S(2)}, u32[]{:S(2)}) collective-permute-start(bf16[256,768]{1,0:T(8,128)(2,1)} %get-tuple-element.359), channel_id=1, source_target_pairs={{0,16},{16,0},{1,17},{17,1},{2,18},{18,2},{3,19},{19,3},{4,20},{20... | collective-permute-start | bytes 1179656 | tf_op jit(solution)/shard_map/ppermute | solution.py:635
  225.6 65.1 %collective-permute-start.66 = (bf16[192,768]{1,0:T(8,128)(2,1)}, bf16[192,768]{1,0:T(8,128)(2,1)}, u32[]{:S(2)}, u32[]{:S(2)}) collective-permute-start(bf16[192,768]{1,0:T(8,128)(2,1)} %convolution_convert_fusion.12), channel_id=1, source_target_pairs={{0,1},{1,0},{2,3},{3,2},{4,5},{5,4},{6,7},{7,6},{8,9},{9,8},{10,11... | collective-permute-start | bytes 884744 | tf_op jit(solution)/shard_map/ppermute | solution.py:53
  293.1 95.9 %collective-permute-start.49 = (bf16[576,768]{1,0:T(8,128)(2,1)}, bf16[576,768]{1,0:T(8,128)(2,1)}, u32[]{:S(2)}, u32[]{:S(2)}) collective-permute-start(bf16[576,768]{1,0:T(8,128)(2,1)} %convolution_convert_fusion.8), channel_id=1, source_target_pairs={{0,1},{1,0},{2,3},{3,2},{4,5},{5,4},{6,7},{7,6},{8,9},{9,8},{10,11... | collective-permute-start | bytes 2654216 | tf_op jit(solution)/shard_map/ppermute | solution.py:53
  304.8 54.6 %collective-permute-start.53 = (bf16[384,768]{1,0:T(8,128)(2,1)}, bf16[384,768]{1,0:T(8,128)(2,1)}, u32[]{:S(2)}, u32[]{:S(2)}) collective-permute-start(bf16[384,768]{1,0:T(8,128)(2,1)} %get-tuple-element.375), channel_id=1, source_target_pairs={{0,16},{16,0},{1,17},{17,1},{2,18},{18,2},{3,19},{19,3},{4,20},{20... | collective-permute-start | bytes 1769480 | tf_op jit(solution)/shard_map/ppermute | solution.py:558
  325.1 28.8 %collective-permute-start.58 = (bf16[384,768]{1,0:T(8,128)(2,1)}, bf16[384,768]{1,0:T(8,128)(2,1)}, u32[]{:S(2)}, u32[]{:S(2)}) collective-permute-start(bf16[384,768]{1,0:T(8,128)(2,1)} %get-tuple-element.378), channel_id=1, source_target_pairs={{0,16},{16,0},{1,17},{17,1},{2,18},{18,2},{3,19},{19,3},{4,20},{20... | collective-permute-start | bytes 1769480 | tf_op jit(solution)/shard_map/ppermute | solution.py:558
  359.3 34.1 %collective-permute-start.48 = (bf16[576,768]{1,0:T(8,128)(2,1)S(1)}, bf16[576,768]{1,0:T(8,128)(2,1)S(1)}, u32[]{:S(2)}, u32[]{:S(2)}) collective-permute-start(bf16[576,768]{1,0:T(8,128)(2,1)S(1)} %copy-done.107), channel_id=1, source_target_pairs={{0,1},{1,0},{2,3},{3,2},{4,5},{5,4},{6,7},{7,6},{8,9},{9,8},{10,11... | collective-permute-start | bytes 2654216 | tf_op jit(solution)/shard_map/ppermute | solution.py:53
  395.9 27.7 %collective-permute-start.86 = (bf16[384,768]{1,0:T(8,128)(2,1)S(1)}, bf16[384,768]{1,0:T(8,128)(2,1)S(1)}, u32[]{:S(2)}, u32[]{:S(2)}) collective-permute-start(bf16[384,768]{1,0:T(8,128)(2,1)S(1)} %add.318), channel_id=1, source_target_pairs={{4,0},{8,12},{5,1},{9,13},{6,2},{10,14},{7,3},{11,15},{20,16},{24,... | collective-permute-start | bytes 1769480 | tf_op jit(solution)/shard_map/ppermute | solution.py:615
  397.5 24.6 %collective-permute-start.87 = (bf16[384,768]{1,0:T(8,128)(2,1)S(1)}, bf16[384,768]{1,0:T(8,128)(2,1)S(1)}, u32[]{:S(2)}, u32[]{:S(2)}) collective-permute-start(bf16[384,768]{1,0:T(8,128)(2,1)S(1)} %add.323), channel_id=1, source_target_pairs={{4,0},{8,12},{5,1},{9,13},{6,2},{10,14},{7,3},{11,15},{20,16},{24,... | collective-permute-start | bytes 1769480 | tf_op jit(solution)/shard_map/ppermute | solution.py:615
  439.9 30.1 %collective-permute-start.85 = (bf16[384,768]{1,0:T(8,128)(2,1)S(1)}, bf16[384,768]{1,0:T(8,128)(2,1)S(1)}, u32[]{:S(2)}, u32[]{:S(2)}) collective-permute-start(bf16[384,768]{1,0:T(8,128)(2,1)S(1)} %add.329), channel_id=1, source_target_pairs={{4,0},{8,12},{5,1},{9,13},{6,2},{10,14},{7,3},{11,15},{20,16},{24,... | collective-permute-start | bytes 1769480 | tf_op jit(solution)/shard_map/ppermute | solution.py:615
  442.1 25.7 %collective-permute-start.77 = (bf16[192,768]{1,0:T(8,128)(2,1)S(1)}, bf16[192,768]{1,0:T(8,128)(2,1)S(1)}, u32[]{:S(2)}, u32[]{:S(2)}) collective-permute-start(bf16[192,768]{1,0:T(8,128)(2,1)S(1)} %add.335), channel_id=1, source_target_pairs={{4,0},{8,12},{5,1},{9,13},{6,2},{10,14},{7,3},{11,15},{20,16},{24,... | collective-permute-start | bytes 884744 | tf_op jit(solution)/shard_map/ppermute | solution.py:615
  443.4 24.4 %collective-permute-start.81 = (bf16[192,768]{1,0:T(8,128)(2,1)S(1)}, bf16[192,768]{1,0:T(8,128)(2,1)S(1)}, u32[]{:S(2)}, u32[]{:S(2)}) collective-permute-start(bf16[192,768]{1,0:T(8,128)(2,1)S(1)} %add.336), channel_id=1, source_target_pairs={{4,8},{8,4},{5,9},{9,5},{6,10},{10,6},{7,11},{11,7},{20,24},{24,20... | collective-permute-start | bytes 884744 | tf_op jit(solution)/shard_map/ppermute | solution.py:611
  449.8 22.6 %collective-permute-start.80 = (bf16[192,768]{1,0:T(8,128)(2,1)S(1)}, bf16[192,768]{1,0:T(8,128)(2,1)S(1)}, u32[]{:S(2)}, u32[]{:S(2)}) collective-permute-start(bf16[192,768]{1,0:T(8,128)(2,1)S(1)} %add.337), channel_id=1, source_target_pairs={{4,0},{8,12},{5,1},{9,13},{6,2},{10,14},{7,3},{11,15},{20,16},{24,... | collective-permute-start | bytes 884744 | tf_op jit(solution)/shard_map/ppermute | solution.py:615
  (173 other events, 2847.1 us)

commit v3 on v2

v3 whole, which is shorter than its diff:
```python
import functools

import jax
import jax.numpy as jnp
from jax import lax
from jax.experimental import pallas as pl
from jax.experimental.pallas import tpu as pltpu
from jax.sharding import PartitionSpec as P

HEAD_DIM = 64
EPSILON = 1e-05
LOW = jnp.bfloat16
FULL = jnp.float32
SCALING = HEAD_DIM**-0.5
MASKED = -1e30
VMEM_BYTES = 16 * 1024 * 1024

SIBLING = [(0, 1), (1, 0), (2, 3), (3, 2)]
PARTNER = [(0, 3), (3, 0), (1, 2), (2, 1)]
SWAP = [(0, 1), (1, 0)]


def dot(left, right):
    return jnp.dot(left, right, preferred_element_type=FULL)


def dot_rows(left, right):
    return lax.dot_general(left, right, (((0,), (0,)), ((), ())), preferred_element_type=FULL)


def dot_back(left, right):
    return lax.dot_general(left, right, (((1,), (1,)), ((), ())), preferred_element_type=FULL)


def norm_rows(values):
    center = values - jnp.mean(values, axis=-1, keepdims=True)
    inverse = lax.rsqrt(jnp.mean(center * center, axis=-1, keepdims=True) + EPSILON)
    return center * inverse, inverse


def norm_back(grad_norm, normed, inverse, gain):
    scaled = grad_norm * gain
    mean_one = jnp.mean(scaled, axis=-1, keepdims=True)
    mean_two = jnp.mean(scaled * normed, axis=-1, keepdims=True)
    return inverse * (scaled - mean_one - normed * mean_two)


def to_partner(value):
    return lax.ppermute(value, "tensor", PARTNER)


def to_sibling(value):
    return lax.ppermute(value, "tensor", SIBLING)


LATEST = []
CHAINED = [False]
PACE = 6e7


def call(kernel, operands, outs, scalars=0, scratch=(), after=(), micros=0.6):
    after = (*LATEST, *after) if CHAINED[0] else tuple(after)
    count, waited = len(operands), len(after)
    specs = [pl.BlockSpec(memory_space=pltpu.SMEM)] * scalars
    specs += [pl.BlockSpec(memory_space=pltpu.VMEM)] * (count - scalars)
    specs += [pl.BlockSpec(memory_space=pl.ANY)] * waited
    got = pl.pallas_call(
        lambda *refs: kernel(*refs[:count], *refs[count + waited :]),
        out_shape=tuple(outs),
        in_specs=specs,
        out_specs=tuple(pl.BlockSpec(memory_space=pltpu.VMEM) for _ in outs),
        scratch_shapes=list(scratch),
        compiler_params=pltpu.CompilerParams(vmem_limit_bytes=VMEM_BYTES),
        cost_estimate=pl.CostEstimate(flops=int(micros * PACE), bytes_accessed=1024, transcendentals=0),
    )(*operands, *after)
    LATEST[:] = [min(got, key=lambda array: array.size)]
    return got


def shape(*dims, dtype=LOW):
    return jax.ShapeDtypeStruct(dims, dtype)


def halves(pieces):
    middle = len(pieces) // 2
    return pieces[:middle], pieces[middle:]


def stacked(pieces, axis=0):
    return jnp.concatenate([p[...] for p in pieces], axis=axis) if len(pieces) > 1 else pieces[0][...]


def project_kernel(first, *refs):
    if first:
        rows_ref, gain, bias, *ws, a_ref, q_ref, kv_ref, send_ref = refs
        layer_in = rows_ref[...].astype(FULL)
    else:
        mid, part, got, b_down, gain, bias, *ws, in_ref, a_ref, q_ref, kv_ref, send_ref = refs
        low = (mid[...] + (part[...].astype(FULL) + got[...].astype(FULL)) + b_down[...]).astype(LOW)
        in_ref[...] = low
        layer_in = low.astype(FULL)
    normed, _ = norm_rows(layer_in)
    a_one = (normed * gain[...] + bias[...]).astype(LOW)
    a_ref[...] = a_one
    own, sib = [dot_back(a_one, stacked(w)).astype(LOW) for w in halves(ws)]
    w = own.shape[1] // 3
    q_own, k_own, v_own = own[:, :w], own[:, w : 2 * w], own[:, 2 * w :]
    q_sib, k_sib, v_sib = sib[:, :w], sib[:, w : 2 * w], sib[:, 2 * w :]
    q_ref[...] = jnp.concatenate([q_own, q_sib], axis=1) * jnp.asarray(SCALING, LOW)
    kv_ref[...] = jnp.concatenate([k_own, k_sib, v_own, v_sib], axis=1)
    send_ref[...] = jnp.concatenate([k_sib, k_own, v_sib, v_own], axis=1)


def project(source, gain, bias, weights, first, after=()):
    n, d = source[0].shape
    h = sum(w.shape[0] for w in weights) // 3
    outs = [shape(n, d), shape(n, h), shape(n, 2 * h), shape(n, 2 * h)]
    if not first:
        outs = [shape(n, d)] + outs
    got = call(
        functools.partial(project_kernel, first),
        (*source, gain, bias, *weights),
        outs,
        after=after,
        micros=1.1,
    )
    return got if not first else (source[0], *got)


def pair_masks(q_pair):
    lane = lax.broadcasted_iota(jnp.int32, q_pair.shape, 1)
    zero = jnp.zeros_like(q_pair)
    return jnp.where(lane < HEAD_DIM, q_pair, zero), jnp.where(lane < HEAD_DIM, zero, q_pair)


def attend_kernel(late, *refs):
    if late:
        outer, q_ref, sib_low, own_high, sib_high, own_low, bias_ref, wo_own, wo_sib, o_ref, lse_ref, part_ref, extra = refs

        @pl.when(outer[0] == 1)
        def _():
            extra[...] = sib_high[...]

        @pl.when(outer[0] == 0)
        def _():
            extra[...] = own_low[...]

        kv = jnp.concatenate([sib_low[...], own_high[...], extra[...]], axis=0)
    else:
        q_ref, own_low, sib_low, bias_ref, wo_own, wo_sib, o_ref, lse_ref, part_ref = refs
        kv = jnp.concatenate([own_low[...], sib_low[...]], axis=0)
    h = kv.shape[1] // 2
    keys, values = kv[:, :h], kv[:, h:]
    values_t = values.T
    outs, sums = [], []
    for pair in range(h // 128):
        lanes = slice(pair * 128, pair * 128 + 128)
        for j, q in enumerate(pair_masks(q_ref[:, lanes])):
            head = 2 * pair + j
            scores = dot_back(keys[:, lanes], q) + bias_ref[...]
            highest = jnp.max(scores, axis=0, keepdims=True)
            e = jnp.exp(scores - highest)
            total = jnp.sum(e, axis=0, keepdims=True)
            mixed = dot(values_t[head * HEAD_DIM : (head + 1) * HEAD_DIM], e.astype(LOW))
            outs.append(mixed * (1.0 / total))
            sums.append(highest + jnp.log(total))
    o = jnp.concatenate(outs, axis=0).T.astype(LOW)
    o_ref[...] = o
    lse_ref[...] = jnp.concatenate(sums + sums[: 8 - len(sums)], axis=0)
    half = wo_own.shape[0]
    part_ref[...] = (dot(o[:, :half], wo_own[...]) + dot(o[:, half:], wo_sib[...])).astype(LOW)


def attend(late, q, blocks, bias, wo_own, wo_sib, outer, after=()):
    n, h = q.shape
    d = wo_own.shape[1]
    operands = ((outer,) if late else ()) + (q, *blocks, bias, wo_own, wo_sib)
    return call(
        functools.partial(attend_kernel, late),
        operands,
        [shape(n, h), shape(8, n, dtype=FULL), shape(n, d)],
        scalars=1 if late else 0,
        scratch=[pltpu.VMEM((n, 2 * h), LOW)] if late else (),
        after=after,
        micros=4.5 if late else 3.2,
    )


def gelu_parts(z):
    c = 0.7978845608028654
    square = z * z
    t = jnp.tanh(c * (z + 0.044715 * (square * z)))
    half = 0.5 * (1.0 + t)
    return z * half, half + 0.5 * z * (1.0 - t * t) * (c + (3.0 * 0.044715 * c) * square)


def feed_kernel(last, ups, dns, *refs):
    refs = (*refs[:7], refs[7 : 7 + ups], refs[7 + ups : 7 + ups + dns], *refs[7 + ups + dns :])
    if last:
        (u, part, got, gain, bias, b_own, b_sib, ups, dns, grad_ref,
         mid_ref, a_ref, g_ref, dz_ref, back_ref, hidden_sum, row_sum) = refs
    else:
        (u, part, got, gain, bias, b_own, b_sib, ups, dns,
         mid_ref, a_ref, g_ref, slope_ref, out_ref) = refs
    mid = u[...].astype(FULL) + (part[...].astype(FULL) + got[...].astype(FULL))
    mid_ref[...] = mid
    normed, _ = norm_rows(mid)
    a_two = (normed * gain[...] + bias[...]).astype(LOW)
    a_ref[...] = a_two
    f = b_own.shape[1]
    step = 256
    total = jnp.zeros(mid.shape, FULL)
    for side, (up, b, dn) in enumerate(zip(halves(ups), (b_own, b_sib), halves(dns))):
        up, dn = stacked(up, axis=1), stacked(dn)
        for at in range(0, f, step):
            cols = slice(at, at + step)
            here = slice(side * f + at, side * f + at + step)
            z = dot(a_two, up[:, cols]) + b[:, cols]
            g, slope = gelu_parts(z)
            g = g.astype(LOW)
            g_ref[:, here] = g
            if last:
                dz = (dot_back(grad_ref[...], dn[cols, :]) * slope).astype(LOW)
                dz_ref[:, here] = dz
                hidden_sum[:, here] = jnp.sum(dz.astype(FULL), axis=0, keepdims=True)
                total = total + dot_back(dz, up[:, cols])
            else:
                slope_ref[:, here] = slope.astype(LOW)
                total = total + dot(g, dn[cols, :])
    if last:
        back_ref[...] = total.astype(LOW)
        row_sum[...] = jnp.sum(grad_ref[...].astype(FULL), axis=0, keepdims=True)
    else:
        out_ref[...] = total.astype(LOW)


def feed(u, part, got, gain, bias, up, b_up, dn, grad=None, after=()):
    n, d = u.shape
    f = b_up[0].shape[1]
    last = grad is not None
    outs = [shape(n, d, dtype=FULL), shape(n, d), shape(n, 2 * f), shape(n, 2 * f), shape(n, d)]
    operands = (u, part, got, gain, bias, *b_up, *up, *dn) + ((grad,) if last else ())
    if last:
        outs += [shape(1, 2 * f, dtype=FULL), shape(1, d, dtype=FULL)]
    return call(functools.partial(feed_kernel, last, len(up), len(dn)), operands, outs, after=after, micros=3.2)


def feed_back_kernel(ups, dns, mid_grad, part, got, in_ref, gain, slope, *refs):
    grad_ref, sums_ref, dz_ref, back_ref, hidden_sum = refs[ups + dns :]
    ups, dns = refs[:ups], refs[ups : ups + dns]
    grad_norm = part[...].astype(FULL) + got[...].astype(FULL)
    normed, inverse = norm_rows(in_ref[...].astype(FULL))
    grad = (mid_grad[...] + norm_back(grad_norm, normed, inverse, gain[...])).astype(LOW)
    grad_ref[...] = grad
    sums_ref[...] = jnp.concatenate(
        [
            jnp.sum(grad_norm * normed, axis=0, keepdims=True),
            jnp.sum(grad_norm, axis=0, keepdims=True),
            jnp.sum(grad.astype(FULL), axis=0, keepdims=True),
        ],
        axis=0,
    )
    f = slope.shape[1] // 2
    step = 256
    total = jnp.zeros(grad.shape, FULL)
    for side, (up, dn) in enumerate(zip(halves(ups), halves(dns))):
        up, dn = stacked(up, axis=1), stacked(dn)
        for at in range(0, f, step):
            cols = slice(at, at + step)
            here = slice(side * f + at, side * f + at + step)
            dz = (dot_back(grad, dn[cols, :]) * slope[:, here].astype(FULL)).astype(LOW)
            dz_ref[:, here] = dz
            hidden_sum[:, here] = jnp.sum(dz.astype(FULL), axis=0, keepdims=True)
            total = total + dot_back(dz, up[:, cols])
    back_ref[...] = total.astype(LOW)


def feed_back(mid_grad, part, got, layer_in, gain, slope, up, dn, after=()):
    n, d = mid_grad.shape
    f = slope.shape[1] // 2
    outs = [shape(n, d), shape(3, d, dtype=FULL), shape(n, 2 * f), shape(n, d), shape(1, 2 * f, dtype=FULL)]
    return call(
        functools.partial(feed_back_kernel, len(up), len(dn)), (mid_grad, part, got, layer_in, gain, slope, *up, *dn), outs, after=after, micros=2.9
    )


def attend_back_kernel(outer, *refs):
    (mids, parts, gots, grads, gain, wo_own, wo_sib, qs, owns, sibs, biases, lses) = (
        refs[0:2], refs[2:4], refs[4:6], refs[6:8], refs[8], refs[9], refs[10], refs[11:13], refs[13:15],
        refs[15:17], refs[17:19], refs[19:21],
    )
    mid_grads, lows, sums_ref, dq_refs, keep_refs, send_refs = (
        refs[21:23], refs[23:25], refs[25], refs[26:28], refs[28:30], refs[30:32]
    )
    extra, acc_own, acc_sib = refs[32], refs[33:35], refs[35:37]
    n = mids[0].shape[0]
    outside = outer[0].astype(FULL)

    @pl.when(outer[0] == 1)
    def _():
        extra[...] = sibs[1][...]

    @pl.when(outer[0] == 0)
    def _():
        extra[...] = owns[0][...]

    sums = None
    for late in (0, 1):
        grad_norm = parts[late][...].astype(FULL) + gots[late][...].astype(FULL)
        normed, inverse = norm_rows(mids[late][...])
        mid_grad = grads[late][...].astype(FULL) + norm_back(grad_norm, normed, inverse, gain[...])
        mid_grads[late][...] = mid_grad
        low = mid_grad.astype(LOW)
        lows[late][...] = low
        now = jnp.concatenate(
            [jnp.sum(grad_norm * normed, axis=0, keepdims=True), jnp.sum(grad_norm, axis=0, keepdims=True)], axis=0
        )
        sums = now if sums is None else sums + now
        do = jnp.concatenate([dot_back(low, wo_own[...]), dot_back(low, wo_sib[...])], axis=1).astype(LOW)
        blocks = (sibs[0], owns[1], extra) if late else (owns[0], sibs[0])
        kv = jnp.concatenate([b[...] for b in blocks], axis=0)
        h = kv.shape[1] // 2
        keys, values = kv[:, :h], kv[:, h:]
        keys_t = keys.T
        dq = []
        for pair in range(h // 128):
            lanes = slice(pair * 128, pair * 128 + 128)
            dk = dv = None
            qs_two, do_two = pair_masks(qs[late][:, lanes]), pair_masks(do[:, lanes])
            for j in (0, 1):
                head = 2 * pair + j
                scores = dot_back(keys[:, lanes], qs_two[j]) + biases[late][...]
                p = jnp.exp(scores - lses[late][head : head + 1, :])
                dp = dot_back(values[:, lanes], do_two[j])
                inner = jnp.sum(p * dp, axis=0, keepdims=True)
                ds = (p * (dp - inner)).astype(LOW)
                dv_now = dot(p.astype(LOW), do_two[j])
                dk_now = dot(ds, qs_two[j])
                dk = dk_now if dk is None else dk + dk_now
                dv = dv_now if dv is None else dv + dv_now
                dq.append(dot(keys_t[head * HEAD_DIM : (head + 1) * HEAD_DIM], ds) * SCALING)
            high_lanes = slice(h + pair * 128, h + pair * 128 + 128)
            for value, where in ((dk, lanes), (dv, high_lanes)):
                if not late:
                    acc_own[0][:, where] = value[:n]
                    acc_sib[0][:, where] = value[n:]
                else:
                    acc_sib[0][:, where] += value[:n]
                    acc_own[1][:, where] = value[n : 2 * n]
                    acc_own[0][:, where] += value[2 * n :] * (1.0 - outside)
                    acc_sib[1][:, where] = value[2 * n :] * outside
        dq_refs[late][...] = jnp.concatenate(dq, axis=0).T.astype(LOW)
    sums_ref[...] = sums

    for i in (0, 1):
        keep_refs[i][...] = acc_own[i][...]
        send = acc_sib[i][...].astype(LOW)
        w = send.shape[1] // 4
        send_refs[i][...] = jnp.concatenate(
            [send[:, w : 2 * w], send[:, :w], send[:, 3 * w :], send[:, 2 * w : 3 * w]], axis=1
        )


def attend_back(outer, mids, parts, gots, grads, gain, wo, qs, owns, sibs, biases, lses, after=()):
    n, d = mids[0].shape
    h = qs[0].shape[1]
    two = lambda *dims, dtype=LOW: [shape(*dims, dtype=dtype)] * 2
    outs = (
        two(n, d, dtype=FULL) + two(n, d) + [shape(2, d, dtype=FULL)] + two(n, h) + two(n, 2 * h, dtype=FULL)
        + two(n, 2 * h)
    )
    got = call(
        attend_back_kernel,
        (outer, *mids, *parts, *gots, *grads, gain, *wo, *qs, *owns, *sibs, *biases, *lses),
        outs,
        scalars=1,
        scratch=[pltpu.VMEM((n, 2 * h), LOW)] + [pltpu.VMEM((n, 2 * h), FULL)] * 4,
        after=after,
        micros=9.5,
    )
    return got[0:2], got[2:4], got[4], got[5:7], got[7:9], got[9:11]


def project_back_kernel(dq, keep, got, *refs):
    *ws, own_ref, sib_ref, part_ref = refs
    dkv = (keep[...] + got[...].astype(FULL)).astype(LOW)
    w = dkv.shape[1] // 4
    own = jnp.concatenate([dq[:, :w], dkv[:, :w], dkv[:, 2 * w : 3 * w]], axis=1)
    sib = jnp.concatenate([dq[:, w:], dkv[:, w : 2 * w], dkv[:, 3 * w :]], axis=1)
    own_ref[...] = own
    sib_ref[...] = sib
    w_own, w_sib = [stacked(x) for x in halves(ws)]
    part_ref[...] = (dot(own, w_own) + dot(sib, w_sib)).astype(LOW)


def project_back(dq, keep, got, weights):
    n = dq.shape[0]
    w, d = sum(x.shape[0] for x in weights) // 2, weights[0].shape[1]
    outs = [shape(n, w), shape(n, w), shape(n, d)]
    return call(project_back_kernel, (dq, keep, got, *weights), outs, micros=0.9)


def outer_kernel(plan, *refs):
    outs = refs[-2:]
    for lefts, first, count, rights, at, width, which, base in plan:
        right = jnp.concatenate([refs[i][:, at : at + width] for i in rights], axis=0)
        for row in range(0, count, 256):
            size = min(256, count - row)
            cols = slice(first + row, first + row + size)
            left = jnp.concatenate([refs[i][:, cols] for i in lefts], axis=0)
            outs[which][base + row : base + row + size, :] = dot_rows(left, right).astype(LOW)


def outer_products(operands, plan, rows, width, after=()):
    return call(functools.partial(outer_kernel, plan), operands, [shape(rows, width)] * 2, after=after, micros=2.5)


def down_kernel(count, *refs):
    gs, dns, outs = refs[:2], refs[2 : 2 + count], refs[2 + count :]
    dn = stacked(dns)
    for g, out in zip(gs, outs):
        out[...] = dot(g[...], dn).astype(LOW)


def down(gs, dns, after=()):
    n, d = gs[0].shape[0], dns[0].shape[1]
    return call(functools.partial(down_kernel, len(dns)), (*gs, *dns), [shape(n, d)] * 2, after=after, micros=1.4)


def ready_kernel(cuts, flags, first_own, first_got, second_own, second_got, *outs):
    on_first = flags[1] == 1
    for i, (at, size) in enumerate(cuts):
        rows = slice(at, at + size)
        first = (first_own[rows, :].astype(FULL) + first_got[rows, :].astype(FULL)).astype(LOW)
        second = (second_own[rows, :].astype(FULL) + second_got[rows, :].astype(FULL)).astype(LOW)
        mine, theirs = outs[2 * i], outs[2 * i + 1]

        @pl.when(on_first)
        def _():
            mine[...] = first
            theirs[...] = second

        @pl.when(flags[1] == 0)
        def _():
            mine[...] = second
            theirs[...] = first


def ready_pieces(flags, first, second, sizes):
    cuts, at = [], 0
    for size in sizes:
        cuts.append((at, size))
        at += size
    width = first[0].shape[1]
    outs = [shape(size, width) for size in sizes for _ in (0, 1)]
    got = call(functools.partial(ready_kernel, tuple(cuts)), (flags, *first, *second), outs, scalars=1)
    return [(got[2 * i], got[2 * i + 1]) for i in range(len(sizes))]


def added_kernel(left, right, out):
    out[...] = (left[...].astype(FULL) + right[...].astype(FULL)).astype(out.dtype)


def sums_kernel(*refs):
    count = len(refs) // 3
    for i in range(count):
        refs[2 * count + i][...] = (refs[2 * i][...].astype(FULL) + refs[2 * i + 1][...].astype(FULL)).astype(LOW)


def added(left, right, after=()):
    return call(added_kernel, (left, right), [shape(*left.shape, dtype=left.dtype)], after=after)[0]


def chosen_kernel(count, which, flags, *refs):
    sums, gots, outs = refs[:count], refs[count : 2 * count], refs[2 * count :]
    for flag, pieces in ((1, sums), (0, gots)):

        @pl.when(flags[which] == flag)
        def _():
            first = 0
            for out in outs:
                at, last = 0, first + out.shape[0]
                for piece in pieces:
                    low, high = max(first, at), min(last, at + piece.shape[0])
                    if low < high:
                        out[low - first : high - first, :] = piece[low - at : high - at, :].astype(FULL)
                    at += piece.shape[0]
                first = last


def chosen(flags, stages, sizes, which):
    if which is None:
        flags, which = jnp.ones_like(flags), 0
    operands = (flags, *[low for low, _ in stages], *[got for _, got in stages])
    outs = [shape(size, stages[0][0].shape[1], dtype=FULL) for size in sizes]
    return call(functools.partial(chosen_kernel, len(stages), which), operands, outs, scalars=1)


def last_kernel(flags, part_low, part_high, got, mid_low, mid_high, in_low, in_high, gain, out, sums):
    for flag, part, mid, rows in ((1, part_low, mid_low, in_low), (0, part_high, mid_high, in_high)):

        @pl.when(flags[4] == flag)
        def _():
            grad_norm = part[...].astype(FULL) + got[...].astype(FULL)
            normed, inverse = norm_rows(rows[...].astype(FULL))
            out[...] = (mid[...] + norm_back(grad_norm, normed, inverse, gain[...])).astype(LOW)
            sums[0:1, :] = 2.0 * jnp.sum(grad_norm * normed, axis=0, keepdims=True)
            sums[1:2, :] = 2.0 * jnp.sum(grad_norm, axis=0, keepdims=True)


def last_rows(flags, parts, got, mids, rows, gain):
    n, d = got.shape
    return call(
        last_kernel, (flags, *parts, got, *mids, *rows, gain), [shape(n, d), shape(2, d, dtype=FULL)], scalars=1,
        micros=1.0,
    )


def gather_kernel(one_0, one_lo, one_hi, two_0, two_1, down_lo, down_hi, up_lo_0, up_hi_0, up_lo_1, up_hi_1, rows, own):
    half = own.shape[1]
    both = one_lo[...] + one_hi[...]
    rows[0:2, :] = one_0[...]
    rows[2:4, :] = two_0[...]
    rows[4:5, :] = both[2:3]
    rows[5:7, :] = both[0:2]
    rows[7:9, :] = two_1[...]
    rows[9:10, :] = down_lo[...] + down_hi[...]
    for i, hidden in enumerate((up_lo_0[...] + up_hi_0[...], up_lo_1[...] + up_hi_1[...])):
        rows[10 + i : 11 + i, :] = hidden[:, half:]
        own[i : i + 1, :] = hidden[:, :half]


def chip_kernel(rows, own, got, out):
    out[0:10, :] = rows[0:10, :] + got[0:10, :]
    out[10:12, :] = own[...] + got[10:12, :]


def layers_kernel(flags, rows, got, mine, theirs):
    both = (rows[0:10, :] + got[0:10, :]) * 0.5
    for flag, first, second in ((1, mine, theirs), (0, theirs, mine)):

        @pl.when(flags[1] == flag)
        def _():
            first[0:5, :] = both[0:5]
            first[5:6, :] = rows[10:11, :]
            second[0:5, :] = both[5:10]
            second[5:6, :] = rows[11:12, :]


def fill(out, wholes, axis, first):
    if axis:
        out[...] = wholes[0][:, first : first + out.shape[1]]
        return
    at, last = 0, first + out.shape[0]
    for whole in wholes:
        low, high = max(first, at), min(last, at + whole.shape[0])
        if low < high:
            out[low - first : high - first, :] = whole[low - at : high - at, :]
        at += whole.shape[0]


def half_kernel(axis, flags, *refs):
    *wholes, out = refs
    for flag in (1, 0):

        @pl.when(flags[3] == flag)
        def _():
            fill(out, wholes, axis, 0 if flag else out.shape[axis])


def half_of(flags, wholes, axis, after=()):
    dims = [sum(w.shape[0] for w in wholes), wholes[0].shape[1]]
    dims[axis] //= 2
    return call(functools.partial(half_kernel, axis), (flags, *wholes), [shape(*dims)], scalars=1, after=after)[0]


def pick_kernel(layer, count, got_count, flags, *refs):
    wholes, gots, outs = refs[:count], refs[count : count + got_count], refs[count + got_count :]
    ways = [(flags[1] == 1 - layer, wholes), (flags[1] == layer, gots)]
    if got_count == 2:
        ways = [ways[0]] + [((flags[1] == layer) & (flags[3] == flag), gots[::step]) for flag, step in ((1, 1), (0, -1))]
    for wanted, sources in ways:

        @pl.when(wanted)
        def _():
            at = 0
            for out in outs:
                fill(out, sources, 0, at)
                at += out.shape[0]


def picked(flags, layer, wholes, gots, sizes, after=()):
    outs = [shape(size, wholes[0].shape[1]) for size in sizes]
    kernel = functools.partial(pick_kernel, layer, len(wholes), len(gots))
    return call(kernel, (flags, *wholes, *gots), outs, scalars=1, after=after)


def stack_kernel(*refs):
    *wholes, out = refs
    fill(out, wholes, 0, 0)


def stacked_rows(wholes, after):
    rows = sum(w.shape[0] for w in wholes)
    return call(stack_kernel, wholes, [shape(rows, wholes[0].shape[1])], after=after)[0]


def copy_kernel(source, out):
    out[...] = source[...]


def copied(source, after):
    return call(copy_kernel, (source,), [shape(*source.shape)], after=after)[0]


def micro_kernel(flags, both, out):
    for flag in (1, 0):

        @pl.when(flags[1] == flag)
        def _():
            out[...] = both[1 - flag]


def output_kernel(flags, mid_low, mid_high, part_low, part_high, got, bias, out):
    for flag, mid, part in ((1, mid_low, part_low), (0, mid_high, part_high)):

        @pl.when(flags[4] == flag)
        def _():
            out[...] = (mid[...] + (part[...].astype(FULL) + got[...].astype(FULL)) + bias[...]).astype(LOW)


def own_kernel(flags, if_low, if_high, out):
    for flag, rows in ((1, if_low), (0, if_high)):

        @pl.when(flags[4] == flag)
        def _():
            out[...] = rows[...]


def own_or(flags, if_low, if_high, after=()):
    return call(own_kernel, (flags, if_low, if_high), [shape(*if_low.shape)], scalars=1, after=after)[0]


def output_rows(flags, mids, parts, got, bias):
    return call(output_kernel, (flags, *mids, *parts, got, bias), [shape(*got.shape)], scalars=1)[0]


def body(
    inputs, cotangent, segments, ln1_gain, ln1_bias, w_query, w_key, w_value, w_out,
    ln2_gain, ln2_bias, w_up, b_up, w_down, b_down, *, n_batch,
):
    LATEST.clear()
    CHAINED[0] = False
    n, d = inputs.shape[1:]
    half = w_up.shape[2]
    section = lax.axis_index("section")
    tensor = lax.axis_index("tensor")
    batch = lax.axis_index("batch")
    on_first = section == 0
    early = tensor < 2
    outer = (tensor == 0) | (tensor == 3)
    middle = (batch == 1) | (batch == 2)
    even = batch % 2 == 0
    flags = jnp.stack([outer, on_first, middle, even, early]).astype(jnp.int32)
    paired = n_batch % 2 == 0
    beside = [(i, i ^ 1) for i in range(n_batch)]

    def across(value):
        return lax.ppermute(value, "section", SWAP)

    qkv_parts = (w_query[0].T, w_key[0].T, w_value[0].T)
    if paired:
        got_qkv = across(half_of(flags, qkv_parts, 0))
    else:
        got_qkv = across(jnp.concatenate(qkv_parts, axis=0))
    own_in = call(micro_kernel, (flags, inputs), [shape(n, d)], scalars=1)[0]
    other_in = to_partner(own_in)
    own_cot = call(micro_kernel, (flags, cotangent), [shape(n, d)], scalars=1)[0]
    other_cot = to_partner(own_cot)
    small_own = jnp.concatenate([ln1_gain, ln1_bias, ln2_gain, ln2_bias, b_down, b_up], axis=0)
    small_other = across(small_own)
    got_wo = across(copied(w_out[0], (got_qkv,)))
    got_feed = across(stacked_rows((w_up[0], w_down[0]), (got_wo,)))
    gots_qkv = (got_qkv, lax.ppermute(got_qkv, "batch", beside)) if paired else jnp.split(got_qkv, 2)

    def low_high(own, other):
        return jnp.where(early, own, other), jnp.where(early, other, own)

    rows_in = low_high(own_in, other_in)
    grad_last = low_high(own_cot, other_cot)

    segment = jnp.where(on_first, segments[0, 0], segments[1, 0])
    low_at = jnp.where(outer, 0, 1)
    block_at = {"own_low": low_at, "sib_low": 1 - low_at, "own_high": 3 - low_at, "sib_high": 2 + low_at}

    def block_bias(query, key_blocks):
        span = jnp.arange(n)
        query_at = block_at[query] * n + span
        query_seg = lax.dynamic_slice_in_dim(segment, block_at[query] * n, n)
        rows = []
        for key in key_blocks:
            key_at = key * n + span
            key_seg = lax.dynamic_slice_in_dim(segment, key * n, n)
            kept = (key_at[:, None] <= query_at[None, :]) & (key_seg[:, None] == query_seg[None, :])
            rows.append(jnp.where(kept, 0.0, MASKED).astype(FULL))
        return jnp.concatenate(rows, axis=0)

    biases = (
        block_bias("own_low", [block_at["own_low"], block_at["sib_low"]]),
        block_bias(
            "own_high",
            [block_at["sib_low"], block_at["own_high"], jnp.where(outer, block_at["sib_high"], block_at["own_low"])],
        ),
    )

    def layer_rows(layer):
        small = jnp.where(section == layer, small_own, small_other)
        rows = [small[i : i + 1] for i in range(6)]
        return rows[:5] + [(rows[5], to_sibling(rows[5]))]

    small_0, small_1 = layer_rows(0), layer_rows(1)

    def weights(layer, wholes, gots, sizes, after):
        return [(own, to_sibling(own)) for own in picked(flags, layer, wholes, gots, sizes, after)]

    def qkv_weight(layer, after=()):
        return weights(layer, qkv_parts, gots_qkv, [3 * w_query.shape[2]], after)[0]

    def out_weight(layer, after=()):
        return weights(layer, (w_out[0],), (got_wo,), [w_out.shape[1]], after)[0]

    def feed_weights(layer, after=()):
        return weights(layer, (w_up[0], w_down[0]), (got_feed,), [d, half], after)

    def attend_low(projected, sib, wo):
        return attend(False, projected[2], (projected[3], sib[0]), biases[0], *wo, None)

    def attend_high(both, sib, wo):
        return attend(True, both[1][2], (sib[0], both[1][3], sib[1], both[0][3]), biases[1], *wo, flags)

    qkv_0 = qkv_weight(0, (got_wo,))
    wo_0 = out_weight(0)
    tied = (other_cot, small_0[5][1], small_1[5][1])
    proj_0, sib_0 = [], []
    for i in (0, 1):
        proj_0.append(project((rows_in[i],), small_0[0], small_0[1], qkv_0, True, tied))
        sib_0.append(to_sibling(proj_0[i][4]))
    att_0 = [attend_low(proj_0[0], sib_0, wo_0)]
    got = [to_partner(att_0[0][2])]
    att_0.append(attend_high(proj_0, sib_0, wo_0))
    got.append(to_partner(att_0[1][2]))
    up_0, down_0 = feed_weights(0, got)
    feed_0, feed_got, after = [], [], ()
    for i in (0, 1):
        feed_0.append(
            feed(proj_0[i][0], att_0[i][2], got[i], small_0[2], small_0[3], up_0, small_0[5], down_0, after=after)
        )
        feed_got.append(to_partner(feed_0[i][4]))
        if i == 0:
            qkv_1 = qkv_weight(1, (feed_0[0][4],))
            wo_1 = out_weight(1, (feed_0[0][4],))
            after = (qkv_1[0], wo_1[0])

    proj_1, sib_1, att_1, got, after = [], [], [], [], ()
    for i in (0, 1):
        source = (feed_0[i][0], feed_0[i][4], feed_got[i], small_0[4])
        proj_1.append(project(source, small_1[0], small_1[1], qkv_1, False, after))
        sib_1.append(to_sibling(proj_1[i][4]))
        if i == 0:
            up_1, down_1 = feed_weights(1, (proj_1[0][2],))
            after = (up_1[0], down_1[0])
            att_1.append(attend_low(proj_1[0], sib_1, wo_1))
        else:
            att_1.append(attend_high(proj_1, sib_1, wo_1))
        got.append(to_partner(att_1[i][2]))
    feed_1, back_got = [], []
    for i in (0, 1):
        feed_1.append(
            feed(proj_1[i][0], att_1[i][2], got[i], small_1[2], small_1[3], up_1, small_1[5], down_1, grad_last[i])
        )
        back_got.append(to_partner(feed_1[i][4]))

    def grads_feed(g, grads, a_two, dz):
        plan = (
            ((4, 5), 0, d, (6, 7), 0, half, 0, 0),
            ((4, 5), 0, d, (6, 7), half, half, 1, 0),
            ((0, 1), 0, half, (2, 3), 0, d, 0, d),
            ((0, 1), half, half, (2, 3), 0, d, 1, d),
        )
        return outer_products((*g, *grads, *a_two, *dz), plan, d + half, d)

    def grads_attend(o, lows, a_one, d_own, d_sib):
        w, w3 = o[0].shape[1] // 2, d_own[0].shape[1]
        plan = (
            ((6, 7), 0, w3, (4, 5), 0, d, 0, 0),
            ((8, 9), 0, w3, (4, 5), 0, d, 1, 0),
            ((0, 1), 0, w, (2, 3), 0, d, 0, w3),
            ((0, 1), w, w, (2, 3), 0, d, 1, w3),
        )
        return outer_products((*o, *lows, *a_one, *d_own, *d_sib), plan, w3 + w, d)

    mids = [f[0] for f in feed_1]
    by_feed_1 = grads_feed([f[2] for f in feed_1], grad_last, [f[1] for f in feed_1], [f[3] for f in feed_1])
    feed_1_got = to_sibling(by_feed_1[1])
    out_parts = down([f[2] for f in feed_1], down_1)
    mid_grads_1, lows_1, two_1, dq, keep, send = attend_back(
        flags, mids, [f[4] for f in feed_1], back_got, grad_last, small_1[2], wo_1, [p[2] for p in proj_1],
        [p[3] for p in proj_1], sib_1, biases, [a[1] for a in att_1], (*out_parts, *by_feed_1),
    )
    kv_got = [to_sibling(x) for x in send]
    back_1, part_got = [], []
    for i in (0, 1):
        back_1.append(project_back(dq[i], keep[i], kv_got[i], qkv_1))
        part_got.append(to_partner(back_1[i][2]))
    by_att_1 = grads_attend(
        [a[0] for a in att_1], lows_1, [p[1] for p in proj_1], [b[0] for b in back_1], [b[1] for b in back_1]
    )
    att_1_got = to_sibling(by_att_1[1])

    fb_0, back_got, after = [], [], by_att_1
    for i in (0, 1):
        fb_0.append(
            feed_back(
                mid_grads_1[i], back_1[i][2], part_got[i], proj_1[i][0], small_1[0], feed_0[i][3], up_0, down_0, after
            )
        )
        after = ()
        back_got.append(to_partner(fb_0[i][3]))
    grad_mid = [f[0] for f in fb_0]
    by_feed_0 = grads_feed([f[2] for f in feed_0], grad_mid, [f[1] for f in feed_0], [f[2] for f in fb_0])
    feed_0_got = to_sibling(by_feed_0[1])

    CHAINED[0] = True
    along = [[(0, 1), (3, 2)], [(1, 2), (2, 1)], [(1, 0), (2, 3)]]
    feed_pieces = ready_pieces(
        flags, (by_feed_0[0], feed_0_got), (by_feed_1[0], feed_1_got), [(d + half) // 4] * 4
    )
    stage, hops = {}, {}

    def begin(k, piece):
        stage[k], hops[k] = (piece[0], across(piece[1])), 0

    def advance(*ks, after=()):
        if n_batch != 4:
            ks = [k for k in ks if hops[k] == 0]
        if not ks:
            return
        values = call(
            sums_kernel, [x for k in ks for x in stage[k]], [shape(*stage[k][0].shape) for k in ks],
            after=[stage[k][1] for k in after], micros=0.5 * len(ks),
        )
        for k, value in zip(ks, values):
            stage[k] = (value, lax.ppermute(value, "batch", along[hops[k]]) if n_batch == 4 else value)
            hops[k] += 1

    def settled(ks, sizes):
        if n_batch == 4:
            return chosen(flags, [stage[k] for k in ks], sizes, 2)
        return chosen(flags, [(lax.psum(stage[k][0], "batch"), stage[k][0]) for k in ks], sizes, None)

    begin(0, feed_pieces[0])
    begin(1, feed_pieces[1])
    advance(0)
    begin(2, feed_pieces[2])
    mid_grads_0, lows_0, two_0, dq, keep, send = attend_back(
        flags, [f[0] for f in feed_0], [f[3] for f in fb_0], back_got, grad_mid, small_0[2], wo_0,
        [p[2] for p in proj_0], [p[3] for p in proj_0], sib_0, biases, [a[1] for a in att_0],
    )
    advance(1)
    begin(3, feed_pieces[3])
    kv_got = [to_sibling(x) for x in send]
    back_0 = [project_back(dq[i], keep[i], kv_got[i], qkv_0) for i in (0, 1)]
    part_got = to_partner(own_or(flags, back_0[1][2], back_0[0][2]))
    by_att_0 = grads_attend(
        [a[0] for a in att_0], lows_0, [p[1] for p in proj_0], [b[0] for b in back_0], [b[1] for b in back_0]
    )
    att_0_got = to_sibling(by_att_0[1])
    advance(0, 2)
    att_rows = by_att_0[0].shape[0]
    att_pieces = ready_pieces(flags, (by_att_0[0], att_0_got), (by_att_1[0], att_1_got), [att_rows // 2] * 2)
    begin(4, att_pieces[0])
    begin(5, att_pieces[1])
    last, one_0 = last_rows(flags, [b[2] for b in back_0], part_got, mid_grads_0, rows_in, small_0[0])

    def both_micro(first, second):
        mine = jnp.where(on_first, first, second)
        theirs = across(jnp.where(on_first, second, first))
        return jnp.stack([jnp.where(on_first, mine, theirs), jnp.where(on_first, theirs, mine)])[None]

    backward_out = both_micro(last, jnp.where(early, *grad_mid))

    def output_sent():
        return to_partner(own_or(flags, out_parts[1], out_parts[0]))

    def output_done(got):
        out_1 = output_rows(flags, mids, out_parts, got, small_1[4])
        return both_micro(jnp.where(early, *[p[0] for p in proj_1]), out_1)

    def sums_gathered():
        operands = (
            one_0, fb_0[0][1], fb_0[1][1], two_0, two_1, feed_1[0][6], feed_1[1][6], fb_0[0][4], fb_0[1][4],
            feed_1[0][5], feed_1[1][5],
        )
        rows, own = call(gather_kernel, operands, [shape(12, d, dtype=FULL), shape(2, half, dtype=FULL)])
        return rows, own, to_sibling(rows)

    def sums_chip(rows, own, got):
        rows = call(chip_kernel, (rows, own, got), [shape(12, d, dtype=FULL)])[0]
        return rows, to_partner(rows)

    def sums_layers(rows, got):
        mine, theirs = call(layers_kernel, (flags, rows, got), [shape(6, d, dtype=FULL)] * 2, scalars=1)
        return mine, across(theirs)

    def sums_on(distance):
        def step(left, right):
            value = added(left, right)
            return value, lax.ppermute(value, "batch", [(i, i ^ distance) for i in range(n_batch)])

        return step

    side = [lambda: (output_sent(),), lambda got: (output_done(got),)]
    sums_steps = [sums_gathered, sums_chip, sums_layers]
    whole_power = n_batch & (n_batch - 1) == 0
    distance = 1
    while whole_power and distance < n_batch:
        sums_steps.append(sums_on(distance))
        distance *= 2
    sums_steps.append(lambda left, right: (added(left, right),))
    advance(1, 3)
    sums_state = sums_gathered()
    advance(0, 2, 4)
    sums_state = sums_chip(*sums_state)
    out_state = side[0]()
    advance(1, 3, 5)
    sums_state = sums_layers(*sums_state)
    advance(2, 4, after=(0,))
    out_state = side[1](*out_state)
    advance(3, 5, after=(1,))
    up_total = settled((0, 1), [d])[0]
    for step in sums_steps[3:-1]:
        sums_state = step(*sums_state)
    advance(4, after=(2,))
    sums_state = sums_steps[-1](*sums_state)
    advance(5, after=(3,))
    down_total = settled((2, 3), [half])[0]
    att_totals = settled((4, 5), [att_rows // 4] * 4)
    forward_out = out_state[0]
    sums = sums_state[0] if whole_power else lax.psum(sums_state[0], "batch")
    return (
        forward_out,
        backward_out,
        sums[0:1],
        sums[1:2],
        *[x.T[None] for x in att_totals[:3]],
        att_totals[3][None],
        sums[2:3],
        sums[3:4],
        up_total[None],
        sums[5:6],
        down_total[None],
        sums[4:5],
    )


def solution(mesh):
    rows = P(None, ("batch", "tensor"), None)
    layer = P("section", None)
    by_column = P("section", None, "tensor")
    by_row = P("section", "tensor", None)
    kept = P("section", None, ("batch", "tensor"), None)
    return jax.shard_map(
        functools.partial(body, n_batch=mesh.shape["batch"]),
        mesh=mesh,
        in_specs=(
            rows, rows, P(None, "batch", None), layer, layer, by_column, by_column, by_column, by_row,
            layer, layer, by_column, P("section", "tensor"), by_row, layer,
        ),
        out_specs=(
            kept, kept, layer, layer, by_column, by_column, by_column, by_row,
            layer, layer, by_column, P("section", "tensor"), by_row, layer,
        ),
        check_vma=False,
    )
```

time: 486 us -> 408 us (0.84)
  other arithmetic: 41.8 us -> 6 us
  matrix products: 31.9 us -> 0 us
  waiting for transfers between devices: 208 us -> 181 us
  Pallas kernels: 78.3 us -> 101 us
  local copies, waits for them, and re-layouts: 22.2 us -> 14.1 us
    dot_general x20 -> x0, matrix products: 31.9 us -> none  [the longest x16 25 us: dot_rows(): lax.dot_general(left, right, (((0,), (0,)), ((), ())), preferred_element_...]
    ppermute x42 -> x34, waiting for transfers between devices: 137 us -> 112 us  [the longest x13 48.8 us: across(): return lax.ppermute(value, 'section', SWAP)]
    pallas_call x20 -> x61, Pallas kernels: 78.3 us -> 101 us  [call(): pl.pallas_call(lambda *refs: kernel(*refs[:count], *refs[count + waited:]...]
    ppermute x19 -> x17, waiting for transfers between devices: 71.1 us -> 56.5 us  [to_partner(): return lax.ppermute(value, 'tensor', PARTNER)]
    ppermute x27 -> x23, waiting for transfers between devices: 0.07 us -> 13 us  [to_sibling(): return lax.ppermute(value, 'tensor', SIBLING)]
    select_n x14 -> x3, other arithmetic: 10.5 us -> 0.15 us  [the longest x2 0.14 us: both_micro(): theirs = across(jnp.where(on_first, second, first))]
    add x35 -> x0, other arithmetic: 7.84 us -> none  [the longest x24 6.46 us: added(): return left + right]
    slice x12 -> x2, local copies, waits for them, and re-layouts: 6.73 us -> 0.03 us  [layer_rows(): rows = [small[i:i + 1] for i in range(6)]]
  transfers between devices with their start and end apart: 88 -> 74, of which waited for: 32 -> 33; matrix products, arithmetic and copies ran while one was open for 15% -> 2% of each run, Pallas kernels for 15% -> 20%
where the time goes in v3:
time: 408 us; the launch traced here: 400 us
  waiting for transfers between devices  181 us (44%)
  Pallas kernels  101 us (25%)
  starting transfers between devices  95.4 us (23%)
  local copies, waits for them, and re-layouts  14.1 us (3%)
  other arithmetic  6 us (1%)
    pallas_call x61, Pallas kernels, call(): pl.pallas_call(lambda *refs: kernel(*refs[:count], *refs[count + waited:]...  101 us
    ppermute x17, waiting for transfers between devices, to_partner(): return lax.ppermute(value, 'tensor', PARTNER)  56.5 us
    ppermute x18, starting transfers between devices, advance(): lax.ppermute(value, 'batch', along[hops[k]])  52.4 us
    ppermute x13, waiting for transfers between devices, across(): return lax.ppermute(value, 'section', SWAP)  48.8 us
    ppermute x18, waiting for transfers between devices, advance(): lax.ppermute(value, 'batch', along[hops[k]])  38.4 us
    ppermute x2, waiting for transfers between devices, step(): lax.ppermute(value, 'batch', [(i, i ^ distance) for i in range(n_batch)])  18.3 us
    ppermute x13, starting transfers between devices, across(): return lax.ppermute(value, 'section', SWAP)  16.2 us
    ppermute x17, starting transfers between devices, to_partner(): return lax.ppermute(value, 'tensor', PARTNER)  15 us
  transfers between devices with their start and end apart: 74, of which 33 were waited for; matrix products, arithmetic and copies ran while one was open for 2% of the time, Pallas kernels for 20%

profile of v3, /device:TPU:0, one launch (start us, length us, event | category | flops | bytes accessed | tf_op | source)
XLA Modules:
  0.0 400.0 jit_solution(13887939123649646317)
XLA Ops:
  7.3 10.2 %collective-permute-done.2.refs_1_.refs_4_ = bf16[288,768]{1,0:T(8,128)(2,1)S(1)} collective-permute-done((bf16[288,768]{1,0:T(8,128)(2,1)S(1)}, bf16[288,768]{1,0:T(8,128)(2,1)S(1)}, u32[]{:S(2)}, u32[]{:S(2)}) %collective-permute-start.2) | collective-permute-done | bytes 442400 | tf_op jit(solution)/shard_map/ppermute | solution.py:669
  33.7 6.3 %collective-permute-done.3.refs_5_ = bf16[288,768]{1,0:T(8,128)(2,1)} collective-permute-done((bf16[288,768]{1,0:T(8,128)(2,1)S(1)}, bf16[288,768]{1,0:T(8,128)(2,1)}, u32[]{:S(2)}, u32[]{:S(2)}) %collective-permute-start.3) | collective-permute-done | bytes 442400 | tf_op jit(solution)/shard_map/ppermute | solution.py:684
  51.4 4.5 %shard_map.264 = (bf16[256,384]{1,0:T(8,128)(2,1)S(1)}, f32[8,256]{1,0:T(8,128)S(1)}, bf16[256,768]{1,0:T(8,128)(2,1)S(1)}) custom-call(s32[5]{0:T(128)S(1)} %convert_element_type.3.refs_0_, bf16[256,384]{1,0:T(8,128)(2,1)S(1)} %get-tuple-element.166.refs_1_.refs_13_, bf16[256,768]{1,0:T(8,128)(2,1)S(1)} %collective-permute-done.9.refs_2_.refs_16_, ...), custom_call_target="tpu_custom_call" | custom-call | flops 270000000 | bytes 1024 | tf_op jit(solution)/shard_map/pallas_call | solution.py:67
  61.6 5.3 %collective-permute-done.14.refs_5_.refs_2_ = bf16[256,768]{1,0:T(8,128)(2,1)S(1)} collective-permute-done((bf16[256,768]{1,0:T(8,128)(2,1)S(1)}, bf16[256,768]{1,0:T(8,128)(2,1)S(1)}, u32[]{:S(2)}, u32[]{:S(2)}) %collective-permute-start.14) | collective-permute-done | bytes 393248 | tf_op jit(solution)/shard_map/ppermute | solution.py:49
  67.0 8.4 %collective-permute-done.11.refs_4_.refs_2_ = bf16[256,768]{1,0:T(8,128)(2,1)S(1)} collective-permute-done((bf16[256,768]{1,0:T(8,128)(2,1)S(1)}, bf16[256,768]{1,0:T(8,128)(2,1)S(1)}, u32[]{:S(2)}, u32[]{:S(2)}) %collective-permute-start.11) | collective-permute-done | bytes 393248 | tf_op jit(solution)/shard_map/ppermute | solution.py:49
  75.4 8.8 %collective-permute-done.12.refs_3_ = bf16[1536,768]{1,0:T(8,128)(2,1)} collective-permute-done((bf16[1536,768]{1,0:T(8,128)(2,1)}, bf16[1536,768]{1,0:T(8,128)(2,1)}, u32[]{:S(2)}, u32[]{:S(2)}) %collective-permute-start.12) | collective-permute-done | bytes 2359328 | tf_op jit(solution)/shard_map/ppermute | solution.py:669
  100.6 5.6 %collective-permute-done.17.refs_2_ = bf16[256,768]{1,0:T(8,128)(2,1)S(1)} collective-permute-done((bf16[256,768]{1,0:T(8,128)(2,1)S(1)}, bf16[256,768]{1,0:T(8,128)(2,1)S(1)}, u32[]{:S(2)}, u32[]{:S(2)}) %collective-permute-start.17) | collective-permute-done | bytes 393248 | tf_op jit(solution)/shard_map/ppermute | solution.py:49
  121.7 4.7 %shard_map.275 = (bf16[256,384]{1,0:T(8,128)(2,1)S(1)}, f32[8,256]{1,0:T(8,128)S(1)}, bf16[256,768]{1,0:T(8,128)(2,1)S(1)}) custom-call(s32[5]{0:T(128)S(1)} %convert_element_type.3.refs_0_, bf16[256,384]{1,0:T(8,128)(2,1)S(1)} %get-tuple-element.185.refs_1_.refs_13_, bf16[256,768]{1,0:T(8,128)(2,1)S(1)} %collective-permute-done.20.refs_2_.refs_16_, ...), custom_call_target="tpu_custom_call" | custom-call | flops 270000000 | bytes 1024 | tf_op jit(solution)/shard_map/pallas_call | solution.py:67
  149.3 8.3 %collective-permute-done.28.refs_6_ = bf16[256,768]{1,0:T(8,128)(2,1)S(1)} collective-permute-done((bf16[256,768]{1,0:T(8,128)(2,1)S(1)}, bf16[256,768]{1,0:T(8,128)(2,1)S(1)}, u32[]{:S(2)}, u32[]{:S(2)}) %collective-permute-start.28) | collective-permute-done | bytes 393248 | tf_op jit(solution)/shard_map/ppermute | solution.py:49
  157.6 9.7 %shard_map.279 = (f32[256,768]{1,0:T(8,128)S(1)}, f32[256,768]{1,0:T(8,128)S(1)}, bf16[256,768]{1,0:T(8,128)(2,1)S(1)}, bf16[256,768]{1,0:T(8,128)(2,1)S(1)}, f3...) custom-call(s32[5]{0:T(128)S(1)} %convert_element_type.3.refs_0_, ...), custom_call_target="tpu_custom_call" | custom-call | flops 570000000 | bytes 1024 | tf_op jit(solution)/shard_map/pallas_call | solution.py:67
  174.5 6.6 %collective-permute-done.32.refs_2_ = bf16[256,768]{1,0:T(8,128)(2,1)S(1)} collective-permute-done((bf16[256,768]{1,0:T(8,128)(2,1)S(1)}, bf16[256,768]{1,0:T(8,128)(2,1)S(1)}, u32[]{:S(2)}, u32[]{:S(2)}) %collective-permute-start.32) | collective-permute-done | bytes 393248 | tf_op jit(solution)/shard_map/ppermute | solution.py:49
  184.0 5.5 %collective-permute-done.30.refs_2_ = bf16[256,768]{1,0:T(8,128)(2,1)S(1)} collective-permute-done((bf16[256,768]{1,0:T(8,128)(2,1)S(1)}, bf16[256,768]{1,0:T(8,128)(2,1)S(1)}, u32[]{:S(2)}, u32[]{:S(2)}) %collective-permute-start.30) | collective-permute-done | bytes 393248 | tf_op jit(solution)/shard_map/ppermute | solution.py:49
  206.1 12.4 %collective-permute-done.37.refs_1_ = bf16[384,768]{1,0:T(8,128)(2,1)S(1)} collective-permute-done((bf16[384,768]{1,0:T(8,128)(2,1)S(1)}, bf16[384,768]{1,0:T(8,128)(2,1)S(1)}, u32[]{:S(2)}, u32[]{:S(2)}) %collective-permute-start.37) | collective-permute-done | bytes 589856 | tf_op jit(solution)/shard_map/ppermute | solution.py:669
  218.6 4.9 %collective-permute-done.34.refs_6_ = bf16[256,768]{1,0:T(8,128)(2,1)S(1)} collective-permute-done((bf16[256,768]{1,0:T(8,128)(2,1)S(1)}, bf16[256,768]{1,0:T(8,128)(2,1)S(1)}, u32[]{:S(2)}, u32[]{:S(2)}) %collective-permute-start.34) | collective-permute-done | bytes 393248 | tf_op jit(solution)/shard_map/ppermute | solution.py:49
  223.5 9.5 %shard_map.288 = (f32[256,768]{1,0:T(8,128)S(1)}, f32[256,768]{1,0:T(8,128)S(1)}, bf16[256,768]{1,0:T(8,128)(2,1)S(1)}, bf16[256,768]{1,0:T(8,128)(2,1)S(1)}, f3...) custom-call(s32[5]{0:T(128)S(1)} %convert_element_type.3.refs_0_, ...), custom_call_target="tpu_custom_call" | custom-call | flops 570000000 | bytes 1024 | tf_op jit(solution)/shard_map/pallas_call | solution.py:67
  244.0 11.6 %collective-permute-done.45.refs_3_ = bf16[384,768]{1,0:T(8,128)(2,1)S(1)} collective-permute-done((bf16[384,768]{1,0:T(8,128)(2,1)S(1)}, bf16[384,768]{1,0:T(8,128)(2,1)S(1)}, u32[]{:S(2)}, u32[]{:S(2)}) %collective-permute-start.45) | collective-permute-done | bytes 589856 | tf_op jit(solution)/shard_map/ppermute | solution.py:669
  273.6 4.4 %collective-permute-start.57 = (bf16[384,768]{1,0:T(8,128)(2,1)S(1)}, bf16[384,768]{1,0:T(8,128)(2,1)S(1)}, u32[]{:S(2)}, u32[]{:S(2)}) collective-permute-start(bf16[384,768]{1,0:T(8,128)(2,1)S(1)} %get-tuple-element.293.refs_2_), channel_id=1, source_target_pairs={{0,4},{12,8},{1,5},{13,9},{2,6},{14,10},{3,7},{15,11},{16,20},{28,... | collective-permute-start | bytes 1769480 | tf_op jit(solution)/shard_map/ppermute | solution.py:853
  278.1 7.9 %collective-permute-done.50.refs_3_ = bf16[384,768]{1,0:T(8,128)(2,1)S(1)} collective-permute-done((bf16[384,768]{1,0:T(8,128)(2,1)S(1)}, bf16[384,768]{1,0:T(8,128)(2,1)S(1)}, u32[]{:S(2)}, u32[]{:S(2)}) %collective-permute-start.50) | collective-permute-done | bytes 589856 | tf_op jit(solution)/shard_map/ppermute | solution.py:853
  287.8 9.7 %collective-permute-start.54 = (bf16[384,768]{1,0:T(8,128)(2,1)S(1)}, bf16[384,768]{1,0:T(8,128)(2,1)S(1)}, u32[]{:S(2)}, u32[]{:S(2)}) collective-permute-start(bf16[384,768]{1,0:T(8,128)(2,1)S(1)} %get-tuple-element.292.refs_2_), channel_id=1, source_target_pairs={{0,4},{12,8},{1,5},{13,9},{2,6},{14,10},{3,7},{15,11},{16,20},{28,... | collective-permute-start | bytes 1769480 | tf_op jit(solution)/shard_map/ppermute | solution.py:853
  303.6 18.4 %collective-permute-start.65 = (bf16[384,768]{1,0:T(8,128)(2,1)S(1)}, bf16[384,768]{1,0:T(8,128)(2,1)S(1)}, u32[]{:S(2)}, u32[]{:S(2)}) collective-permute-start(bf16[384,768]{1,0:T(8,128)(2,1)S(1)} %get-tuple-element.302.refs_2_), channel_id=1, source_target_pairs={{0,4},{12,8},{1,5},{13,9},{2,6},{14,10},{3,7},{15,11},{16,20},{28,... | collective-permute-start | bytes 1769480 | tf_op jit(solution)/shard_map/ppermute | solution.py:853
  327.8 6.6 %collective-permute-done.65.refs_3_ = bf16[384,768]{1,0:T(8,128)(2,1)S(1)} collective-permute-done((bf16[384,768]{1,0:T(8,128)(2,1)S(1)}, bf16[384,768]{1,0:T(8,128)(2,1)S(1)}, u32[]{:S(2)}, u32[]{:S(2)}) %collective-permute-start.65) | collective-permute-done | bytes 589856 | tf_op jit(solution)/shard_map/ppermute | solution.py:853
  348.0 16.4 %collective-permute-done.66.refs_1_ = f32[6,768]{1,0:T(8,128)S(1)} collective-permute-done((f32[6,768]{1,0:T(8,128)S(1)}, f32[6,768]{1,0:T(8,128)S(1)}, u32[]{:S(2)}, u32[]{:S(2)}) %collective-permute-start.66) | collective-permute-done | bytes 18464 | tf_op jit(solution)/shard_map/ppermute | solution.py:918
  377.9 7.7 %collective-permute-done.72.refs_3_ = bf16[384,768]{1,0:T(8,128)(2,1)S(1)} collective-permute-done((bf16[384,768]{1,0:T(8,128)(2,1)S(1)}, bf16[384,768]{1,0:T(8,128)(2,1)S(1)}, u32[]{:S(2)}, u32[]{:S(2)}) %collective-permute-start.72) | collective-permute-done | bytes 589856 | tf_op jit(solution)/shard_map/ppermute | solution.py:853
  385.6 10.2 %collective-permute-done.73.refs_4_ = bf16[384,768]{1,0:T(8,128)(2,1)S(1)} collective-permute-done((bf16[384,768]{1,0:T(8,128)(2,1)S(1)}, bf16[384,768]{1,0:T(8,128)(2,1)S(1)}, u32[]{:S(2)}, u32[]{:S(2)}) %collective-permute-start.73) | collective-permute-done | bytes 589856 | tf_op jit(solution)/shard_map/ppermute | solution.py:853
  (285 shorter events, 194.1 us)
Async XLA Ops:
  20.1 24.1 %collective-permute-start.1 = (f32[6,768]{1,0:T(8,128)S(1)}, f32[6,768]{1,0:T(8,128)S(1)}, u32[]{:S(2)}, u32[]{:S(2)}) collective-permute-start(f32[6,768]{1,0:T(8,128)S(1)} %concatenate.9), channel_id=1, source_target_pairs={{0,16},{16,0},{1,17},{17,1},{2,18},{18,2},{3,19},{19,3},{4,20},{20... | collective-permute-start | bytes 55304 | tf_op jit(solution)/shard_map/ppermute | solution.py:669
  23.1 24.1 %collective-permute-start.6 = (bf16[256,768]{1,0:T(8,128)(2,1)}, bf16[256,768]{1,0:T(8,128)(2,1)S(1)}, u32[]{:S(2)}, u32[]{:S(2)}) collective-permute-start(bf16[256,768]{1,0:T(8,128)(2,1)} %shard_map.258), channel_id=1, source_target_pairs={{0,3},{3,0},{1,2},{2,1},{4,7},{7,4},{5,6},{6,5},{8,11},{11,8},{9,1... | collective-permute-start | bytes 1179656 | tf_op jit(solution)/shard_map/ppermute | solution.py:49
  31.1 53.1 %collective-permute-start.12 = (bf16[1536,768]{1,0:T(8,128)(2,1)}, bf16[1536,768]{1,0:T(8,128)(2,1)}, u32[]{:S(2)}, u32[]{:S(2)}) collective-permute-start(bf16[1536,768]{1,0:T(8,128)(2,1)} %shard_map.262), channel_id=1, source_target_pairs={{0,16},{16,0},{1,17},{17,1},{2,18},{18,2},{3,19},{19,3},{4,20},{20... | collective-permute-start | bytes 7077896 | tf_op jit(solution)/shard_map/ppermute | solution.py:669
  109.4 22.9 %collective-permute-start.23 = (bf16[768,768]{1,0:T(8,128)(2,1)S(1)}, bf16[768,768]{1,0:T(8,128)(2,1)S(1)}, u32[]{:S(2)}, u32[]{:S(2)}) collective-permute-start(bf16[768,768]{1,0:T(8,128)(2,1)S(1)} %get-tuple-element.178.refs_8_.refs_7_), channel_id=1, source_target_pairs={{0,1},{1,0},{2,3},{3,2},{4,5},{5,4},{6,7},{7,6},{8,9},{9,8},{10,11... | collective-permute-start | bytes 3538952 | tf_op jit(solution)/shard_map/ppermute | solution.py:53
  172.6 22.5 %collective-permute-start.36 = (bf16[1536,768]{1,0:T(8,128)(2,1)S(1)}, bf16[1536,768]{1,0:T(8,128)(2,1)S(1)}, u32[]{:S(2)}, u32[]{:S(2)}) collective-permute-start(bf16[1536,768]{1,0:T(8,128)(2,1)S(1)} %get-tuple-element.203.refs_25_), channel_id=1, source_target_pairs={{0,1},{1,0},{2,3},{3,2},{4,5},{5,4},{6,7},{7,6},{8,9},{9,8},{10,11... | collective-permute-start | bytes 7077896 | tf_op jit(solution)/shard_map/ppermute | solution.py:53
  205.5 28.3 %collective-permute-start.39 = (bf16[384,768]{1,0:T(8,128)(2,1)S(1)}, bf16[384,768]{1,0:T(8,128)(2,1)S(1)}, u32[]{:S(2)}, u32[]{:S(2)}) collective-permute-start(bf16[384,768]{1,0:T(8,128)(2,1)S(1)} %get-tuple-element.248), channel_id=1, source_target_pairs={{0,16},{16,0},{1,17},{17,1},{2,18},{18,2},{3,19},{19,3},{4,20},{20... | collective-permute-start | bytes 1769480 | tf_op jit(solution)/shard_map/ppermute | solution.py:669
  233.6 26.3 %collective-permute-start.43 = (bf16[768,768]{1,0:T(8,128)(2,1)S(1)}, bf16[768,768]{1,0:T(8,128)(2,1)S(1)}, u32[]{:S(2)}, u32[]{:S(2)}) collective-permute-start(bf16[768,768]{1,0:T(8,128)(2,1)S(1)} %get-tuple-element.224.refs_11_), channel_id=1, source_target_pairs={{0,1},{1,0},{2,3},{3,2},{4,5},{5,4},{6,7},{7,6},{8,9},{9,8},{10,11... | collective-permute-start | bytes 3538952 | tf_op jit(solution)/shard_map/ppermute | solution.py:53
  239.2 22.3 %collective-permute-start.42 = (bf16[768,768]{1,0:T(8,128)(2,1)S(1)}, bf16[768,768]{1,0:T(8,128)(2,1)S(1)}, u32[]{:S(2)}, u32[]{:S(2)}) collective-permute-start(bf16[768,768]{1,0:T(8,128)(2,1)S(1)} %get-tuple-element.268), channel_id=1, source_target_pairs={{0,1},{1,0},{2,3},{3,2},{4,5},{5,4},{6,7},{7,6},{8,9},{9,8},{10,11... | collective-permute-start | bytes 3538952 | tf_op jit(solution)/shard_map/ppermute | solution.py:53
  242.5 25.2 %collective-permute-start.47 = (bf16[384,768]{1,0:T(8,128)(2,1)S(1)}, bf16[384,768]{1,0:T(8,128)(2,1)S(1)}, u32[]{:S(2)}, u32[]{:S(2)}) collective-permute-start(bf16[384,768]{1,0:T(8,128)(2,1)S(1)} %get-tuple-element.284), channel_id=1, source_target_pairs={{0,16},{16,0},{1,17},{17,1},{2,18},{18,2},{3,19},{19,3},{4,20},{20... | collective-permute-start | bytes 1769480 | tf_op jit(solution)/shard_map/ppermute | solution.py:669
  259.9 26.1 %collective-permute-start.50 = (bf16[384,768]{1,0:T(8,128)(2,1)S(1)}, bf16[384,768]{1,0:T(8,128)(2,1)S(1)}, u32[]{:S(2)}, u32[]{:S(2)}) collective-permute-start(bf16[384,768]{1,0:T(8,128)(2,1)S(1)} %get-tuple-element.288.refs_2_), channel_id=1, source_target_pairs={{0,4},{12,8},{1,5},{13,9},{2,6},{14,10},{3,7},{15,11},{16,20},{28,... | collective-permute-start | bytes 1769480 | tf_op jit(solution)/shard_map/ppermute | solution.py:853
  261.5 24.5 %collective-permute-start.49 = (bf16[384,768]{1,0:T(8,128)(2,1)S(1)}, bf16[384,768]{1,0:T(8,128)(2,1)S(1)}, u32[]{:S(2)}, u32[]{:S(2)}) collective-permute-start(bf16[384,768]{1,0:T(8,128)(2,1)S(1)} %get-tuple-element.271.refs_5_.refs_0_), channel_id=1, source_target_pairs={{4,8},{8,4},{5,9},{9,5},{6,10},{10,6},{7,11},{11,7},{20,24},{24,20... | collective-permute-start | bytes 1769480 | tf_op jit(solution)/shard_map/ppermute | solution.py:853
  268.3 29.3 %collective-permute-start.58 = (bf16[384,768]{1,0:T(8,128)(2,1)S(1)}, bf16[384,768]{1,0:T(8,128)(2,1)S(1)}, u32[]{:S(2)}, u32[]{:S(2)}) collective-permute-start(bf16[384,768]{1,0:T(8,128)(2,1)S(1)} %get-tuple-element.295), channel_id=1, source_target_pairs={{0,16},{16,0},{1,17},{17,1},{2,18},{18,2},{3,19},{19,3},{4,20},{20... | collective-permute-start | bytes 1769480 | tf_op jit(solution)/shard_map/ppermute | solution.py:669
  273.6 25.3 %collective-permute-start.57 = (bf16[384,768]{1,0:T(8,128)(2,1)S(1)}, bf16[384,768]{1,0:T(8,128)(2,1)S(1)}, u32[]{:S(2)}, u32[]{:S(2)}) collective-permute-start(bf16[384,768]{1,0:T(8,128)(2,1)S(1)} %get-tuple-element.293.refs_2_), channel_id=1, source_target_pairs={{0,4},{12,8},{1,5},{13,9},{2,6},{14,10},{3,7},{15,11},{16,20},{28,... | collective-permute-start | bytes 1769480 | tf_op jit(solution)/shard_map/ppermute | solution.py:853
  287.8 34.1 %collective-permute-start.54 = (bf16[384,768]{1,0:T(8,128)(2,1)S(1)}, bf16[384,768]{1,0:T(8,128)(2,1)S(1)}, u32[]{:S(2)}, u32[]{:S(2)}) collective-permute-start(bf16[384,768]{1,0:T(8,128)(2,1)S(1)} %get-tuple-element.292.refs_2_), channel_id=1, source_target_pairs={{0,4},{12,8},{1,5},{13,9},{2,6},{14,10},{3,7},{15,11},{16,20},{28,... | collective-permute-start | bytes 1769480 | tf_op jit(solution)/shard_map/ppermute | solution.py:853
  297.6 25.8 %collective-permute-start.59 = (bf16[384,768]{1,0:T(8,128)(2,1)S(1)}, bf16[384,768]{1,0:T(8,128)(2,1)S(1)}, u32[]{:S(2)}, u32[]{:S(2)}) collective-permute-start(bf16[384,768]{1,0:T(8,128)(2,1)S(1)} %get-tuple-element.290.refs_3_.refs_1_), channel_id=1, source_target_pairs={{4,0},{8,12},{5,1},{9,13},{6,2},{10,14},{7,3},{11,15},{20,16},{24,... | collective-permute-start | bytes 1769480 | tf_op jit(solution)/shard_map/ppermute | solution.py:853
  299.6 26.0 %collective-permute-start.52 = (bf16[256,768]{1,0:T(8,128)(2,1)S(1)}, bf16[256,768]{1,0:T(8,128)(2,1)S(1)}, u32[]{:S(2)}, u32[]{:S(2)}) collective-permute-start(bf16[256,768]{1,0:T(8,128)(2,1)S(1)} %shard_map.301.refs_6_), channel_id=1, source_target_pairs={{0,3},{3,0},{1,2},{2,1},{4,7},{7,4},{5,6},{6,5},{8,11},{11,8},{9,1... | collective-permute-start | bytes 1179656 | tf_op jit(solution)/shard_map/ppermute | solution.py:49
  302.9 23.4 %collective-permute-start.64 = (bf16[384,768]{1,0:T(8,128)(2,1)S(1)}, bf16[384,768]{1,0:T(8,128)(2,1)S(1)}, u32[]{:S(2)}, u32[]{:S(2)}) collective-permute-start(bf16[384,768]{1,0:T(8,128)(2,1)S(1)} %get-tuple-element.301.refs_0_), channel_id=1, source_target_pairs={{4,8},{8,4},{5,9},{9,5},{6,10},{10,6},{7,11},{11,7},{20,24},{24,20... | collective-permute-start | bytes 1769480 | tf_op jit(solution)/shard_map/ppermute | solution.py:853
  303.6 30.8 %collective-permute-start.65 = (bf16[384,768]{1,0:T(8,128)(2,1)S(1)}, bf16[384,768]{1,0:T(8,128)(2,1)S(1)}, u32[]{:S(2)}, u32[]{:S(2)}) collective-permute-start(bf16[384,768]{1,0:T(8,128)(2,1)S(1)} %get-tuple-element.302.refs_2_), channel_id=1, source_target_pairs={{0,4},{12,8},{1,5},{13,9},{2,6},{14,10},{3,7},{15,11},{16,20},{28,... | collective-permute-start | bytes 1769480 | tf_op jit(solution)/shard_map/ppermute | solution.py:853
  323.4 23.9 %collective-permute-start.61 = (bf16[256,768]{1,0:T(8,128)(2,1)S(1)}, bf16[256,768]{1,0:T(8,128)(2,1)S(1)}, u32[]{:S(2)}, u32[]{:S(2)}) collective-permute-start(bf16[256,768]{1,0:T(8,128)(2,1)S(1)} %get-tuple-element.310), channel_id=1, source_target_pairs={{0,16},{16,0},{1,17},{17,1},{2,18},{18,2},{3,19},{19,3},{4,20},{20... | collective-permute-start | bytes 1179656 | tf_op jit(solution)/shard_map/ppermute | solution.py:669
  325.6 40.2 %collective-permute-start.68 = (bf16[384,768]{1,0:T(8,128)(2,1)S(1)}, bf16[384,768]{1,0:T(8,128)(2,1)S(1)}, u32[]{:S(2)}, u32[]{:S(2)}) collective-permute-start(bf16[384,768]{1,0:T(8,128)(2,1)S(1)} %get-tuple-element.304.refs_0_), channel_id=1, source_target_pairs={{4,8},{8,4},{5,9},{9,5},{6,10},{10,6},{7,11},{11,7},{20,24},{24,20... | collective-permute-start | bytes 1769480 | tf_op jit(solution)/shard_map/ppermute | solution.py:853
  334.4 32.9 %collective-permute-start.69 = (bf16[384,768]{1,0:T(8,128)(2,1)S(1)}, bf16[384,768]{1,0:T(8,128)(2,1)S(1)}, u32[]{:S(2)}, u32[]{:S(2)}) collective-permute-start(bf16[384,768]{1,0:T(8,128)(2,1)S(1)} %get-tuple-element.298.refs_7_.refs_1_), channel_id=1, source_target_pairs={{4,0},{8,12},{5,1},{9,13},{6,2},{10,14},{7,3},{11,15},{20,16},{24,... | collective-permute-start | bytes 1769480 | tf_op jit(solution)/shard_map/ppermute | solution.py:853
  339.5 31.2 %collective-permute-start.71 = (bf16[384,768]{1,0:T(8,128)(2,1)S(1)}, bf16[384,768]{1,0:T(8,128)(2,1)S(1)}, u32[]{:S(2)}, u32[]{:S(2)}) collective-permute-start(bf16[384,768]{1,0:T(8,128)(2,1)S(1)} %get-tuple-element.303.refs_5_.refs_2_), channel_id=1, source_target_pairs={{4,0},{8,12},{5,1},{9,13},{6,2},{10,14},{7,3},{11,15},{20,16},{24,... | collective-permute-start | bytes 1769480 | tf_op jit(solution)/shard_map/ppermute | solution.py:853
  347.3 23.4 %collective-permute-start.70 = (bf16[384,768]{1,0:T(8,128)(2,1)S(1)}, bf16[384,768]{1,0:T(8,128)(2,1)S(1)}, u32[]{:S(2)}, u32[]{:S(2)}) collective-permute-start(bf16[384,768]{1,0:T(8,128)(2,1)S(1)} %get-tuple-element.305.refs_0_), channel_id=1, source_target_pairs={{4,8},{8,4},{5,9},{9,5},{6,10},{10,6},{7,11},{11,7},{20,24},{24,20... | collective-permute-start | bytes 1769480 | tf_op jit(solution)/shard_map/ppermute | solution.py:853
  370.8 25.0 %collective-permute-start.73 = (bf16[384,768]{1,0:T(8,128)(2,1)S(1)}, bf16[384,768]{1,0:T(8,128)(2,1)S(1)}, u32[]{:S(2)}, u32[]{:S(2)}) collective-permute-start(bf16[384,768]{1,0:T(8,128)(2,1)S(1)} %shard_map.312.refs_5_.refs_2_), channel_id=1, source_target_pairs={{4,0},{8,12},{5,1},{9,13},{6,2},{10,14},{7,3},{11,15},{20,16},{24,... | collective-permute-start | bytes 1769480 | tf_op jit(solution)/shard_map/ppermute | solution.py:853
  (89 other events, 719.5 us)
